TPU v7x, 32 devices: a whole 2x2x4 slice. The times are simulated.
32 devices in a mesh: col: 8 (over y, x, core), row: 4 (over z).
Axes of the slice: x: 2, y: 2, z: 4, core: 2. Of those that a mesh axis runs over, the one named last changes fastest.
Arguments:
- targets: float32 [4, 8, 1024, 128], P(None, 'col', 'row'), as said below
- src_panels: bfloat16 [512, 1024, 128], P('col', 'row')
- live_counts: int32 [8], P('col'), may hold values from 1 to 64, 256 in all
- dest_owner: int32 [512, 4], P('col'), may hold values from 0 to 7
- relative_map: int32 [512, 4, 8], P('col', None, 'row'), may hold values from 0 to 1, as said below
- diag_row: int32 [4, 8], replicated, may hold values from 0 to 3
- parent: int32 [3, 8], replicated, may hold values from 0 to 7
- chain_map: int32 [3, 8, 8], P(None, None, 'row'), may hold values from 0 to 1, as said below
Outputs:
- factors: float32 [4, 8, 1024, 128], P(None, 'col', 'row')
Inputs may be any that keep to these rules, and one draw needn't show every extreme that they name: For each i, s and row group r, the 2 entries relative_map[i, s, r * 2 : (r + 1) * 2] are a permutation of 0 to 1; on r = diag_row[s, dest_owner[i, s]] it maps 0 to 0. For each s, k and row group r, the 2 entries chain_map[s, k, r * 2 : (r + 1) * 2] are a permutation of 0 to 1; on r = diag_row[s + 1, parent[s, k]] it maps 1 to 0. `live_counts`: the counts sum to 256 and the largest is 64. `targets`: every diagonal block after all updates is symmetric positive definite.
All inputs are finite; a program needn't handle non-finite values. No bound on the sum of `live_counts` on one device may be relied on, other than what follows from the above.
Results may differ from a plain program's by a relative error of at most 0.0003.
Values may be sent and summed in bfloat16 or wider, within the bound.
No kernel may reach another device: no remote copies, remote signals or barrier semaphores. Data moves between devices by JAX's collectives and lax.ppermute only.
A program may use at most 128 MiB of HBM per device.

v0:
```python
import jax
import jax.numpy as jnp
from jax import lax
from jax.sharding import PartitionSpec as P


def spread(block, axis, owner):
    block = jnp.where(lax.axis_index(axis) == owner, block, jnp.zeros_like(block))
    return lax.psum(block, axis)


def local(targets, src_panels, live_counts, dest_owner, relative_map, diag_row, parent, chain_map):
    col_count = lax.axis_size("col")
    owner_index = lax.axis_index("col")
    row_index = lax.axis_index("row")
    src_count = src_panels.shape[0]
    block_width = src_panels.shape[2]
    local_blocks = src_panels.shape[1] // block_width
    sections = targets.shape[0]
    panels = src_panels.reshape(src_count, local_blocks, block_width, block_width)
    alive_mask = (jnp.arange(src_count) < live_counts[0]).astype(jnp.float32)
    column_heads = lax.all_gather(panels[:, 0][None], "row", axis=0, tiled=True)
    source_root = diag_row[jnp.arange(sections)[None, :], dest_owner]
    block_index = jnp.arange(local_blocks)
    sources = jnp.arange(src_count)
    results = []
    for s in range(sections):
        columns = column_heads[source_root[:, s], sources]
        source_products = jnp.einsum(
            "iqab,icb->iqac", panels, columns, preferred_element_type=jnp.float32
        )
        source_products = source_products * alive_mask[:, None, None, None]
        source_slot_ids = dest_owner[:, s, None] * local_blocks + relative_map[:, s, :]
        slot_sums = jax.ops.segment_sum(
            source_products.reshape(src_count * local_blocks, block_width, block_width),
            source_slot_ids.reshape(-1),
            num_segments=col_count * local_blocks,
        )
        if s > 0:
            child_rows = results[-1].astype(jnp.bfloat16)
            parent_root = diag_row[s, parent[s - 1, owner_index]]
            column = spread(child_rows[block_width : 2 * block_width], "row", parent_root)
            products = jnp.einsum(
                "qab,cb->qac",
                child_rows.reshape(local_blocks, block_width, block_width),
                column,
                preferred_element_type=jnp.float32,
            )
            kept_mask = jnp.logical_not(
                (diag_row[s - 1, owner_index] == row_index) & (block_index == 0)
            )
            products = products * kept_mask[:, None, None].astype(jnp.float32)
            slot_ids = parent[s - 1, owner_index] * local_blocks + chain_map[s - 1, owner_index]
            slot_sums = slot_sums.at[slot_ids].add(products)
        gathered = lax.psum_scatter(
            slot_sums.reshape(col_count * local_blocks * block_width, block_width),
            "col",
            scatter_dimension=0,
            tiled=True,
        )
        updated = targets[s, 0] - gathered
        root_row = diag_row[s, owner_index]
        is_root = row_index == root_row
        blocks = updated.reshape(local_blocks, block_width, block_width)
        identity = jnp.eye(block_width, dtype=jnp.float32)
        own_block = jnp.where(is_root, blocks[0], identity)
        own_lower = jnp.linalg.cholesky(own_block)
        own_inverse = lax.linalg.triangular_solve(
            own_lower, identity, left_side=False, lower=True, transpose_a=True
        )
        lower_block = spread(own_lower, "row", root_row)
        inverse_t = spread(own_inverse, "row", root_row)
        solved = jnp.einsum("qab,bc->qac", blocks, inverse_t, precision=lax.Precision.HIGHEST)
        first_block = jnp.where(is_root, lower_block, solved[0])
        results.append(
            jnp.concatenate([first_block[None], solved[1:]], axis=0).reshape(
                local_blocks * block_width, block_width
            )
        )
    return jnp.stack(results)[:, None]


def solution(mesh):
    return jax.shard_map(
        local,
        mesh=mesh,
        in_specs=(
            P(None, "col", "row", None),
            P("col", "row", None),
            P("col"),
            P("col", None),
            P("col", None, "row"),
            P(),
            P(),
            P(None, None, "row"),
        ),
        out_specs=P(None, "col", "row", None),
        check_vma=False,
    )
```

profile of v0, /device:TPU:0, one launch (start us, length us, event | category | flops | bytes accessed | tf_op | source)
XLA Modules:
  0.0 652.2 jit_solution(12158117070164362434)
XLA Ops:
  14.3 148.0 %all-gather.3.cloned.1.call-done = bf16[256,1,128,128]{3,2,1,0:T(8,128)(2,1)} async-done(((bf16[64,1,128,128]{3,2,1,0:T(8,128)(2,1)}), bf16[256,1,128,128]{3,2,1,0:T(8,128)(2,1)}) %all-gather.3.cloned.1.call-update) | async-done | bytes 8388624 | tf_op jit(solution)/shard_map/all_gather | solution.py:22
  182.4 17.0 %scatter_fusion = f32[16,128,128]{2,1,0:T(8,128)S(1)} fusion(f32[16,128,128]{2,1,0:T(8,128)S(1)} %broadcast.189.clone.3, s32[128]{0:T(128)S(1)} %add_bitcast_fusion.3, f32[128,128,128]{2,1,0:T(8,128)} %copy.74), kind=kCustom, calls=%fused_computation.5 | custom fusion | flops 2097152 | bytes 25166336 | tf_op jit(solution)/shard_map/scatter-add | solution.py:34
  216.9 18.1 %reduce-scatter.5.cloned.1.call-done = f32[256,128]{1,0:T(8,128)} async-done(((f32[2048,128]{1,0:T(8,128)}), f32[256,128]{1,0:T(8,128)}) %reduce-scatter.5.cloned.1.call-update) | async-done | bytes 131088 | tf_op jit(solution)/shard_map/reduce_scatter | solution.py:55
  236.2 11.7 %cholesky.74 = f32[128,128]{1,0:T(8,128)S(1)} custom-call(f32[128,128]{1,0:T(8,128)S(1)} %copy.76), custom_call_target="Cholesky" | custom-call | tf_op jit(solution)/shard_map/jit(cholesky)/cholesky | solution.py:67
  249.8 9.8 %custom-call.18 = f32[1,128,128]{1,2,0:T(8,128)S(1)} custom-call(f32[1,128,128]{2,1,0:T(8,128)S(1)} %get-tuple-element.29), custom_call_target="InvertDiagBlocksLowerTriangular" | custom-call | tf_op jit(solution)/shard_map/triangular_solve/custom-call.0 | solution.py:68
  267.3 9.0 %copy.80 = f32[128,128,128]{2,1,0:T(8,128)} copy(f32[128,128,128]{1,2,0:T(8,128)} %bitcast.235) | data formatting | bytes 16777216 | tf_op jit(solution)/shard_map/reshape | solution.py:35
  276.4 17.1 %scatter_fusion.1 = f32[16,128,128]{2,1,0:T(8,128)S(1)} fusion(f32[16,128,128]{2,1,0:T(8,128)S(1)} %broadcast.189.clone.2, s32[128]{0:T(128)S(1)} %add_bitcast_fusion.2, f32[128,128,128]{2,1,0:T(8,128)} %copy.80), kind=kCustom, calls=%fused_computation.6 | custom fusion | flops 2097152 | bytes 25166336 | tf_op jit(solution)/shard_map/scatter-add | solution.py:34
  296.3 18.6 %psum.79 = bf16[128,128]{1,0:T(8,128)(2,1)S(1)} all-reduce(bf16[128,128]{1,0:T(8,128)(2,1)S(1)} %fusion.58), channel_id=1, replica_groups=mesh['col'=8,'row'=4] {'row'}, use_global_device_ids=true, to_apply=%region_7.10 | all-reduce | flops 16384 | bytes 65536 | tf_op jit(solution)/shard_map/psum | solution.py:9
  323.8 26.5 %reduce-scatter.7.cloned.1.call-done = f32[256,128]{1,0:T(8,128)} async-done(((f32[2048,128]{1,0:T(8,128)}), f32[256,128]{1,0:T(8,128)}) %reduce-scatter.7.cloned.1.call-update) | async-done | bytes 131088 | tf_op jit(solution)/shard_map/reduce_scatter | solution.py:55
  351.6 11.7 %cholesky.85 = f32[128,128]{1,0:T(8,128)S(1)} custom-call(f32[128,128]{1,0:T(8,128)S(1)} %copy.82), custom_call_target="Cholesky" | custom-call | tf_op jit(solution)/shard_map/jit(cholesky)/cholesky | solution.py:67
  365.1 9.8 %custom-call.19 = f32[1,128,128]{1,2,0:T(8,128)S(1)} custom-call(f32[1,128,128]{2,1,0:T(8,128)S(1)} %get-tuple-element.27), custom_call_target="InvertDiagBlocksLowerTriangular" | custom-call | tf_op jit(solution)/shard_map/triangular_solve/custom-call.0 | solution.py:68
  382.7 9.0 %copy.86 = f32[128,128,128]{2,1,0:T(8,128)} copy(f32[128,128,128]{1,2,0:T(8,128)} %bitcast.236) | data formatting | bytes 16777216 | tf_op jit(solution)/shard_map/reshape | solution.py:35
  391.8 17.1 %scatter_fusion.3 = f32[16,128,128]{2,1,0:T(8,128)S(1)} fusion(f32[16,128,128]{2,1,0:T(8,128)S(1)} %broadcast.189.clone.1, s32[128]{0:T(128)S(1)} %add_bitcast_fusion.1, f32[128,128,128]{2,1,0:T(8,128)} %copy.86), kind=kCustom, calls=%fused_computation.8 | custom fusion | flops 2097152 | bytes 25166336 | tf_op jit(solution)/shard_map/scatter-add | solution.py:34
  411.7 17.9 %psum.82 = bf16[128,128]{1,0:T(8,128)(2,1)S(1)} all-reduce(bf16[128,128]{1,0:T(8,128)(2,1)S(1)} %fusion.57), channel_id=1, replica_groups=mesh['col'=8,'row'=4] {'row'}, use_global_device_ids=true, to_apply=%region_13.16 | all-reduce | flops 16384 | bytes 65536 | tf_op jit(solution)/shard_map/psum | solution.py:9
  438.4 28.2 %reduce-scatter.9.cloned.1.call-done = f32[256,128]{1,0:T(8,128)} async-done(((f32[2048,128]{1,0:T(8,128)}), f32[256,128]{1,0:T(8,128)}) %reduce-scatter.9.cloned.1.call-update) | async-done | bytes 131088 | tf_op jit(solution)/shard_map/reduce_scatter | solution.py:55
  467.7 11.7 %cholesky.96 = f32[128,128]{1,0:T(8,128)S(1)} custom-call(f32[128,128]{1,0:T(8,128)S(1)} %copy.88), custom_call_target="Cholesky" | custom-call | tf_op jit(solution)/shard_map/jit(cholesky)/cholesky | solution.py:67
  481.5 9.8 %custom-call.20 = f32[1,128,128]{1,2,0:T(8,128)S(1)} custom-call(f32[1,128,128]{2,1,0:T(8,128)S(1)} %get-tuple-element.25), custom_call_target="InvertDiagBlocksLowerTriangular" | custom-call | tf_op jit(solution)/shard_map/triangular_solve/custom-call.0 | solution.py:68
  499.2 9.0 %copy.92 = f32[128,128,128]{2,1,0:T(8,128)} copy(f32[128,128,128]{1,2,0:T(8,128)} %bitcast.233) | data formatting | bytes 16777216 | tf_op jit(solution)/shard_map/reshape | solution.py:35
  508.3 17.1 %scatter_fusion.5 = f32[16,128,128]{2,1,0:T(8,128)S(1)} fusion(f32[16,128,128]{2,1,0:T(8,128)S(1)} %broadcast.189.clone, s32[128]{0:T(128)S(1)} %add_bitcast_fusion, f32[128,128,128]{2,1,0:T(8,128)} %copy.92), kind=kCustom, calls=%fused_computation.10 | custom fusion | flops 2097152 | bytes 25166336 | tf_op jit(solution)/shard_map/scatter-add | solution.py:34
  528.0 17.8 %psum.85 = bf16[128,128]{1,0:T(8,128)(2,1)S(1)} all-reduce(bf16[128,128]{1,0:T(8,128)(2,1)S(1)} %fusion.56), channel_id=1, replica_groups=mesh['col'=8,'row'=4] {'row'}, use_global_device_ids=true, to_apply=%region_19.22 | all-reduce | flops 16384 | bytes 65536 | tf_op jit(solution)/shard_map/psum | solution.py:9
  548.4 33.7 %reduce-scatter.11.cloned.1.call-done = f32[256,128]{1,0:T(8,128)} async-done(((f32[2048,128]{1,0:T(8,128)}), f32[256,128]{1,0:T(8,128)}) %reduce-scatter.11.cloned.1.call-update) | async-done | bytes 131088 | tf_op jit(solution)/shard_map/reduce_scatter | solution.py:55
  583.2 11.7 %cholesky.107 = f32[128,128]{1,0:T(8,128)S(1)} custom-call(f32[128,128]{1,0:T(8,128)S(1)} %copy.94), custom_call_target="Cholesky" | custom-call | tf_op jit(solution)/shard_map/jit(cholesky)/cholesky | solution.py:67
  597.1 9.8 %custom-call.21 = f32[1,128,128]{1,2,0:T(8,128)S(1)} custom-call(f32[1,128,128]{2,1,0:T(8,128)S(1)} %get-tuple-element.23), custom_call_target="InvertDiagBlocksLowerTriangular" | custom-call | tf_op jit(solution)/shard_map/triangular_solve/custom-call.0 | solution.py:68
  607.8 34.7 %all-reduce.9.cloned.1.call-done = (f32[128,128]{1,0:T(8,128)}, f32[128,128]{1,0:T(8,128)}) async-done(((f32[128,128]{1,0:T(8,128)}, f32[128,128]{1,0:T(8,128)}), (f32[128,128]{1,0:T(8,128)}, f32[128,128]{1,0:T(8,128)})) %all-reduce.9.cloned.1.call-update) | async-done | bytes 131088 | tf_op jit(solution)/shard_map/psum | solution.py:9
  (166 shorter events, 98.7 us)
Async XLA Ops:
  6.5 3.3 copy-start.6
  6.5 3.6 copy-start
  6.5 155.8 %all-gather.3.cloned.1.call-start = ((), (), s32[]{:S(2)}) async-start(), calls=%async_computation.8 | async-start | bytes 10485760 | tf_op jit(solution)/shard_map/all_gather | solution.py:22
  9.8 225.2 %reduce-scatter.5.cloned.1.call-start = ((), (), s32[]{:S(2)}) async-start(), calls=%async_computation.4 | async-start | bytes 1179648 | tf_op jit(solution)/shard_map/reduce_scatter | solution.py:55
  10.1 3.7 copy-start.7
  182.4 18.2 %copy-start.9 = (s32[3,8]{1,0:T(4,128)S(1)}, s32[3,8]{1,0:T(4,128)}, u32[]{:S(2)}) copy-start(s32[3,8]{1,0:T(4,128)} %param.17) | copy-start | bytes 292
  182.4 29.9 %copy-start.8 = (s32[3,8,2]{1,2,0:T(2,128)S(1)}, s32[3,8,2]{1,2,0:T(2,128)}, u32[]{:S(2)}) copy-start(s32[3,8,2]{1,2,0:T(2,128)} %param.18) | copy-start | bytes 580
  199.5 1.1 copy-start.4
  199.5 35.5 %copy-start.5 = (f32[4,1,256,128]{3,2,1,0:T(8,128)S(1)}, f32[4,1,256,128]{3,2,1,0:T(8,128)}, u32[]{:S(2)}) copy-start(f32[4,1,256,128]{3,2,1,0:T(8,128)} %param.11) | copy-start | bytes 1572868
  200.6 94.5 %all-reduce.15.cloned.1.call-start = ((), (), s32[]{:S(2)}) async-start(), calls=%async_computation.12 | async-start | bytes 262144 | tf_op jit(solution)/shard_map/psum | solution.py:9
  260.4 89.9 %reduce-scatter.7.cloned.1.call-start = ((), (), s32[]{:S(2)}) async-start(), calls=%async_computation.5 | async-start | bytes 1179648 | tf_op jit(solution)/shard_map/reduce_scatter | solution.py:55
  315.7 1.1 copy-start.2
  316.8 93.7 %all-reduce.13.cloned.1.call-start = ((), (), s32[]{:S(2)}) async-start(), calls=%async_computation.11 | async-start | bytes 262144 | tf_op jit(solution)/shard_map/psum | solution.py:9
  375.8 90.8 %reduce-scatter.9.cloned.1.call-start = ((), (), s32[]{:S(2)}) async-start(), calls=%async_computation.6 | async-start | bytes 1179648 | tf_op jit(solution)/shard_map/reduce_scatter | solution.py:55
  430.4 1.1 copy-start.3
  431.5 95.4 %all-reduce.11.cloned.1.call-start = ((), (), s32[]{:S(2)}) async-start(), calls=%async_computation.10 | async-start | bytes 262144 | tf_op jit(solution)/shard_map/psum | solution.py:9
  492.2 89.9 %reduce-scatter.11.cloned.1.call-start = ((), (), s32[]{:S(2)}) async-start(), calls=%async_computation.7 | async-start | bytes 1179648 | tf_op jit(solution)/shard_map/reduce_scatter | solution.py:55
  546.6 1.0 copy-start.1
  547.7 94.8 %all-reduce.9.cloned.1.call-start = ((), (), s32[]{:S(2)}) async-start(), calls=%async_computation.9 | async-start | bytes 262144 | tf_op jit(solution)/shard_map/psum | solution.py:9
Sparse Core Ops, SparseCore 0:
  10.0 152.3 all-gather.2
  200.7 34.2 reduce-scatter.4
  260.6 34.5 all-reduce.14
  316.9 33.4 reduce-scatter.6
  375.9 34.5 all-reduce.12
  431.6 34.8 reduce-scatter.8
  492.3 34.5 all-reduce.10
  547.8 34.2 reduce-scatter.10
  607.8 34.5 all-reduce.8
where the time goes:
time: 663 us; the launch traced here: 652 us
  waiting for transfers between devices  294 us (44%)
  other arithmetic  171 us (26%)
  local copies, waits for them, and re-layouts  68.5 us (10%)
  blocking collectives  54.3 us (8%)
  matrix products  34.8 us (5%)
  between operations  28.8 us (4%)
    all_gather x1, waiting for transfers between devices, local(): column_heads = lax.all_gather(panels[:, 0][None], 'row', axis=0, tiled=True)  148 us
    reduce_scatter x4, waiting for transfers between devices, local(): lax.psum_scatter(slot_sums.reshape(col_count * local_blocks * block_width...  106 us
    scatter-add x4, other arithmetic, local(): jax.ops.segment_sum(source_products.reshape(src_count * local_blocks, blo...  68.2 us
    psum x3, blocking collectives, spread(): return lax.psum(block, axis)  54.3 us
    another operation x12, other arithmetic, local(): own_lower = jnp.linalg.cholesky(own_block)  49.7 us
    psum x4, waiting for transfers between devices, spread(): return lax.psum(block, axis)  39.4 us
    another operation x4, other arithmetic, local(): lax.linalg.triangular_solve(own_lower, identity, left_side=False, lower=T...  39.2 us
    reshape x4, local copies, waits for them, and re-layouts, local(): source_products.reshape(src_count * local_blocks, block_width, block_width)  36 us
  transfers between devices with their start and end apart: 9, of which 9 were waited for; matrix products, arithmetic and copies ran while one was open for 18% of the time, Pallas kernels for 0%

commit v1 on v0

v1 whole, which is shorter than its diff:
```python
import functools

import jax
import jax.numpy as jnp
from jax import lax
from jax.experimental import pallas as pl
from jax.experimental.pallas import tpu as pltpu
from jax.sharding import PartitionSpec as P

F32 = jnp.float32
BF16 = jnp.bfloat16
HIGHEST = lax.Precision.HIGHEST
CHUNK = 8
PANEL = 32
VMEM_LIMIT = 48 * 1024 * 1024


def vmem():
    return pl.BlockSpec(memory_space=pltpu.VMEM)


def smem():
    return pl.BlockSpec(memory_space=pltpu.SMEM)


def params():
    return pltpu.CompilerParams(vmem_limit_bytes=VMEM_LIMIT)


def cost(flops, size):
    return pl.CostEstimate(flops=flops, bytes_accessed=size, transcendentals=0)


def times_transposed(a, b, precision=None):
    return lax.dot_general(
        a, b, (((1,), (1,)), ((), ())), precision=precision, preferred_element_type=F32
    )


def transposed_times(a, b):
    return lax.dot_general(a, b, (((0,), (0,)), ((), ())), preferred_element_type=F32)


def slot_column(slot, chips, own):
    return own ^ (2 * (slot % chips) + slot // chips)


def swap(x, axis, size, mask):
    return lax.ppermute(x, axis, [(i, i ^ mask) for i in range(size)])


def gather_columns(x, col_count):
    chips = col_count // 2
    same = [x] + [swap(x, "col", col_count, 2 * m) for m in range(1, chips)]
    return same + [swap(y, "col", col_count, 1) for y in same]


def scatter_sum(other_half, own_half, col_count):
    chips = col_count // 2
    summed = own_half + swap(other_half, "col", col_count, 1)
    parts = [summed[0]]
    for m in range(1, chips):
        parts.append(swap(summed[m], "col", col_count, 2 * m))
    return parts


def spread(x, roots, row_index, row_count):
    roots = roots.reshape(roots.shape + (1,) * (x.ndim - 1))
    mine = roots == row_index
    up, down = x, x
    for _ in range(row_count - 1):
        up = jnp.where(mine, x, lax.ppermute(up, "row", [(i, i + 1) for i in range(row_count - 1)]))
        down = jnp.where(
            mine, x, lax.ppermute(down, "row", [(i + 1, i) for i in range(row_count - 1)])
        )
    return jnp.where(roots <= row_index, up, down)


def tables_kernel(col_count, place, diag, parent, chain, roots, picks, ahead, keep, into):
    sections = diag.shape[0]
    local_blocks = chain.shape[3]
    chips = col_count // 2
    own = place[0]
    row = place[1]

    def path(s, column):
        columns = [column]
        for t in range(s, sections - 1):
            columns.append(parent[t, columns[-1]])
        return columns

    def block_of(s, columns, j):
        if j == 0:
            return jnp.int32(0)
        if j == 1:
            return jnp.int32(1)
        wanted = block_of(s + 1, columns[1:], j - 1)
        group = diag[s + j, columns[j]]
        found = jnp.int32(0)
        for q in range(1, local_blocks):
            found = jnp.where(chain[group, s, columns[0], q] == wanted, q, found)
        return found

    for s in range(sections):
        columns = path(s, own)
        for j in range(sections):
            if j < sections - s:
                roots[s, j] = diag[s + j, columns[j]]
                picks[s, j] = block_of(s, columns, j)
            else:
                roots[s, j] = 0
                picks[s, j] = 0
    for s in range(1, sections):
        for slot in range(col_count):
            child = slot_column(slot, chips, own)
            hit = parent[s - 1, child] == own
            columns = path(s - 1, child)
            for j in range(sections):
                if j < sections - s:
                    block = block_of(s - 1, columns, j + 1)
                    group = diag[s + j, columns[j + 1]]
                    left_out = (block == 0) & (group == diag[s - 1, child])
                    ahead[s, slot, j] = jnp.where(hit & jnp.logical_not(left_out), 1, 0)
                else:
                    ahead[s, slot, j] = 0
            for q in range(local_blocks):
                left_out = (diag[s - 1, child] == row) & (q == 0)
                keep[s, slot, q] = jnp.where(hit & jnp.logical_not(left_out), 1, 0)
                into[s, slot, q] = chain[row, s - 1, child, q]


def source_kernel(local_blocks, col_count, step, table, live, panels, heads, other, own, total):
    g = pl.program_id(0)
    width = panels.shape[2]
    chips = col_count // 2

    @pl.when(g == 0)
    def _():
        total[...] = jnp.zeros_like(total)

    @pl.when(g * CHUNK < live[0])
    def _():
        for t in range(CHUNK):
            i = g * CHUNK + t
            slot = table[step, 0, i]
            head = heads[table[step, 1, i], t]
            product = times_transposed(panels[t], head)
            for q in range(local_blocks):
                p = table[step, 2 + q, i]
                total[slot, p] += product[q * width : (q + 1) * width]
            total[slot, local_blocks] += times_transposed(head, head)

    @pl.when(g == pl.num_programs(0) - 1)
    def _():
        own[...] = total[:chips]
        other[...] = total[chips : 2 * chips]


def source_sums(step, table, live, panels, heads, col_count):
    count, rows, width = panels.shape
    local_blocks = rows // width
    row_count = heads.shape[0]
    chips = col_count // 2
    half = (chips, local_blocks + 1, width, width)

    def chunk(g, table, live):
        return jnp.minimum(g, (live[0] - 1) // CHUNK)

    out = jax.ShapeDtypeStruct(half, F32)
    return pl.pallas_call(
        functools.partial(source_kernel, local_blocks, col_count, step),
        grid_spec=pltpu.PrefetchScalarGridSpec(
            num_scalar_prefetch=2,
            grid=(count // CHUNK,),
            in_specs=[
                pl.BlockSpec((CHUNK, rows, width), lambda g, a, b: (chunk(g, a, b), 0, 0)),
                pl.BlockSpec(
                    (row_count, CHUNK, width, width), lambda g, a, b: (0, chunk(g, a, b), 0, 0)
                ),
            ],
            out_specs=[pl.BlockSpec(half, lambda g, a, b: (0, 0, 0, 0))] * 2,
            scratch_shapes=[pltpu.VMEM((2 * chips + 1,) + half[1:], F32)],
        ),
        out_shape=[out, out],
        compiler_params=params(),
        cost_estimate=cost(count * (rows + width) * width * width * 2, count * rows * width * 4),
        name="source_sums",
    )(table, live, panels, heads)


def split(x):
    high = x.astype(BF16)
    rest = x - high.astype(F32)
    middle = rest.astype(BF16)
    low = (rest - middle.astype(F32)).astype(BF16)
    return high, middle, low


def factor_kernel(step, col_count, flags, start, *refs):
    children, (upper, inverse, work) = refs[:-3], refs[-3:]
    width = start.shape[0]
    work[:, :width] = start[...]
    for slot, child in enumerate(children):

        @pl.when(flags[step, slot, 0] > 0)
        def _(child=child):
            work[:, :width] -= times_transposed(child[0], child[0])

    rows = lax.broadcasted_iota(jnp.int32, (width, width), 0)
    columns = lax.broadcasted_iota(jnp.int32, (width, width), 1)
    work[:, width:] = (rows == columns).astype(F32)
    sub = lax.broadcasted_iota(jnp.int32, (PANEL, 1), 0)
    for first in range(0, width, PANEL):
        last = first + PANEL
        slab = work[first:last, :]
        spans = [
            jnp.broadcast_to(slab[:, first + k : first + k + 1], (PANEL, width))
            for k in range(PANEL)
        ]
        scale = jnp.zeros((PANEL, 1), F32)
        for j in range(PANEL):
            pivot = spans[j][j : j + 1, :]
            ratio = jnp.where(sub > j, spans[j] * (1.0 / pivot), 0.0)
            for k in range(j + 1, PANEL):
                spans[k] = spans[k] - ratio * spans[k][j : j + 1, :]
            slab = slab - jnp.concatenate([ratio, ratio], axis=1) * slab[j : j + 1, :]
            scale = jnp.where(sub == j, lax.rsqrt(pivot[:, 0:1]), scale)
        slab = slab * scale
        work[first:last, :] = slab
        if last < width:
            high, middle, low = split(slab)
            left = jnp.concatenate([high, high, middle, middle, high, low], axis=0)
            right = jnp.concatenate([high, middle, high, middle, low, high], axis=0)
            work[last:, :] = work[last:, :] - transposed_times(left[:, last:width], right)
    upper[...] = jnp.where(rows <= columns, work[:, :width], 0.0)
    inverse[...] = work[:, width:]


def factor(step, flags, start, children, col_count):
    width = start.shape[0]
    out = jax.ShapeDtypeStruct((width, width), F32)
    return pl.pallas_call(
        functools.partial(factor_kernel, step, col_count),
        in_specs=[smem(), vmem()] + [vmem()] * len(children),
        out_specs=[vmem(), vmem()],
        out_shape=[out, out],
        scratch_shapes=[pltpu.VMEM((width, 2 * width), F32)],
        compiler_params=params(),
        cost_estimate=cost(width * width * width * 200, 16 * width * width),
        name="factor",
    )(flags, start, *children)


def ahead_kernel(step, flags, start, inverse, *refs):
    children, (out, work) = refs[:-2], refs[-2:]
    work[...] = start[...]
    for j in range(start.shape[0]):
        for slot, child in enumerate(children):

            @pl.when(flags[step, slot, j + 1] > 0)
            def _(child=child, j=j):
                work[j] -= times_transposed(child[j + 1], child[0])

        out[j] = times_transposed(work[j], inverse[...], HIGHEST).astype(BF16)


def ahead_blocks(step, flags, start, inverse, children):
    return pl.pallas_call(
        functools.partial(ahead_kernel, step),
        in_specs=[smem(), vmem(), vmem()] + [vmem()] * len(children),
        out_specs=vmem(),
        out_shape=jax.ShapeDtypeStruct(start.shape, BF16),
        scratch_shapes=[pltpu.VMEM(start.shape, F32)],
        compiler_params=params(),
        cost_estimate=cost(start.size * 2000, start.size * 8),
        name="ahead_blocks",
    )(flags, start, inverse, *children)


def panel_kernel(step, child_count, place, roots, keep, into, start, inverse, upper, *refs):
    columns, panels = refs[:child_count], refs[child_count : 2 * child_count]
    out, rounded, work = refs[2 * child_count :]
    blocks, width = start.shape[0], start.shape[1]
    work[...] = start[...]
    for slot in range(child_count):
        for q in range(blocks):

            @pl.when(keep[step, slot, q] > 0)
            def _(slot=slot, q=q):
                work[into[step, slot, q]] -= times_transposed(panels[slot][q], columns[slot][0])

    for q in range(blocks):
        solved = times_transposed(work[q], inverse[...], HIGHEST)
        out[q * width : (q + 1) * width, :] = solved
        rounded[q] = solved.astype(BF16)

    @pl.when(place[1] == roots[step, 0])
    def _():
        out[:width, :] = upper[...].T


def panel_rows(step, place, roots, keep, into, start, inverse, upper, columns, panels):
    blocks, width, _ = start.shape
    return pl.pallas_call(
        functools.partial(panel_kernel, step, len(columns)),
        in_specs=[smem()] * 4 + [vmem()] * (3 + len(columns) + len(panels)),
        out_specs=[vmem(), vmem()],
        out_shape=[
            jax.ShapeDtypeStruct((blocks * width, width), F32),
            jax.ShapeDtypeStruct(start.shape, BF16),
        ],
        scratch_shapes=[pltpu.VMEM(start.shape, F32)],
        compiler_params=params(),
        cost_estimate=cost(start.size * 2000, start.size * 16),
        name="panel_rows",
    )(place, roots, keep, into, start, inverse, upper, *columns, *panels)


def local(targets, src_panels, live_counts, dest_owner, relative_map, diag_row, parent, chain_map):
    col_count = lax.axis_size("col")
    row_count = lax.axis_size("row")
    own = lax.axis_index("col")
    row_index = lax.axis_index("row")
    chips = col_count // 2
    src_count, _, width = src_panels.shape
    local_blocks = src_panels.shape[1] // width
    sections = targets.shape[0]
    targets = targets.reshape(sections, local_blocks, width, width)

    heads = lax.all_gather(src_panels[:, :width][None], "row", axis=0, tiled=True)

    place = jnp.stack([own, row_index]).astype(jnp.int32)
    chain = lax.all_gather(chain_map[None], "row", axis=0, tiled=True)
    tab = functools.partial(jax.ShapeDtypeStruct, dtype=jnp.int32)
    roots, picks, ahead, keep, into = pl.pallas_call(
        functools.partial(tables_kernel, col_count),
        in_specs=[smem()] * 4,
        out_specs=[smem()] * 5,
        out_shape=[
            tab((sections, sections)),
            tab((sections, sections)),
            tab((sections, col_count, sections)),
            tab((sections, col_count, local_blocks)),
            tab((sections, col_count, local_blocks)),
        ],
        name="tables",
    )(place, diag_row, parent, chain)

    alive = jnp.arange(src_count)[:, None] < live_counts[0]
    offset = jnp.bitwise_xor(dest_owner, own)
    slots = jnp.where(alive, (offset % 2) * chips + offset // 2, 2 * chips)
    source_root = diag_row[jnp.arange(sections)[None, :], dest_owner]
    table = jnp.concatenate(
        [slots.T[:, None], source_root.T[:, None], relative_map.transpose(1, 2, 0)], axis=1
    ).astype(jnp.int32)

    diagonal_targets = spread(targets[:, 0], roots[:, 0], row_index, row_count)

    starts = []
    for s in range(sections):
        other, mine = source_sums(s, table, live_counts, src_panels, heads, col_count)
        parts = scatter_sum(other, mine, col_count)
        total = functools.reduce(jnp.add, parts)
        panel = targets[s] - total[:local_blocks]
        diagonal = diagonal_targets[s] - total[local_blocks]
        later = None
        if s + 1 < sections:
            picked = panel[picks[s, 1 : sections - s]]
            later = spread(picked, roots[s, 1 : sections - s], row_index, row_count)
        starts.append((panel, diagonal, later))

    results = []
    columns, panels = [], []
    for s in range(sections):
        panel, diagonal, later = starts[s]
        upper, inverse = factor(s, ahead, diagonal, columns, col_count)
        rows, rounded = panel_rows(
            s, place, roots, keep, into, panel, inverse, upper, columns, panels
        )
        results.append(rows)
        if s + 1 < sections:
            needed = ahead_blocks(s, ahead, later, inverse, columns)
            columns = gather_columns(needed, col_count)
            panels = gather_columns(rounded, col_count)
    return jnp.stack(results)[:, None]


def solution(mesh):
    return jax.shard_map(
        local,
        mesh=mesh,
        in_specs=(
            P(None, "col", "row", None),
            P("col", "row", None),
            P("col"),
            P("col", None),
            P("col", None, "row"),
            P(),
            P(),
            P(None, None, "row"),
        ),
        out_specs=P(None, "col", "row", None),
        check_vma=False,
    )
```

time: 663 us -> 394 us (0.59); the launches traced: 652 us -> 392 us
  other arithmetic: 171 us -> 7.87 us
  waiting for transfers between devices: 294 us -> 154 us
  starting transfers between devices: 0.97 us -> 130 us
  local copies, waits for them, and re-layouts: 68.5 us -> 12.1 us
  Pallas kernels: 0 us -> 48.2 us
  matrix products: 34.8 us -> 0 us
  blocking collectives: 54.3 us -> 21.9 us
  between operations: 28.8 us -> 18 us
    ppermute x0 -> x82, starting transfers between devices: none -> 130 us  [the longest x58 61.3 us: swap(): return lax.ppermute(x, axis, [(i, i ^ mask) for i in range(size)])]
    reduce_scatter x4 -> x0, waiting for transfers between devices: 106 us -> none  [local(): lax.psum_scatter(slot_sums.reshape(col_count * local_blocks * block_width...]
    another operation x16 -> x1, other arithmetic: 88.9 us -> 0.56 us  [local(): place = jnp.stack([own, row_index]).astype(jnp.int32)]
    scatter-add x7 -> x0, other arithmetic: 70.1 us -> none  [the longest x4 68.2 us: local(): jax.ops.segment_sum(source_products.reshape(src_count * local_blocks, blo...]
    ppermute x0 -> x82, waiting for transfers between devices: none -> 57.5 us  [the longest x58 31.4 us: swap(): return lax.ppermute(x, axis, [(i, i ^ mask) for i in range(size)])]
    psum x3 -> x0, blocking collectives: 54.3 us -> none  [spread(): return lax.psum(block, axis)]
    all_gather x1, waiting for transfers between devices: 148 us -> 96 us  [local(): lax.all_gather(src_panels[:, :width][None], 'row', axis=0, tiled=True)]
    pallas_call x0 -> x16, Pallas kernels: none -> 48.2 us  [the longest x4 20.4 us: factor(): pl.pallas_call(functools.partial(factor_kernel, step, col_count), in_spec...]
  transfers between devices with their start and end apart: 9 -> 83, of which waited for: 9 -> 26; matrix products, arithmetic and copies ran while one was open for 18% -> 3% of each run, Pallas kernels for 0% -> 10%
where the time goes in v1:
time: 394 us; the launch traced here: 392 us
  waiting for transfers between devices  154 us (39%)
  starting transfers between devices  130 us (33%)
  Pallas kernels  48.2 us (12%)
  blocking collectives  21.9 us (6%)
  between operations  18 us (5%)
  local copies, waits for them, and re-layouts  12.1 us (3%)
  other arithmetic  7.87 us (2%)
    all_gather x1, waiting for transfers between devices, local(): lax.all_gather(src_panels[:, :width][None], 'row', axis=0, tiled=True)  96 us
    ppermute x58, starting transfers between devices, swap(): return lax.ppermute(x, axis, [(i, i ^ mask) for i in range(size)])  61.3 us
    ppermute x12, starting transfers between devices, spread(): lax.ppermute(up, 'row', [(i, i + 1) for i in range(row_count - 1)])  53.5 us
    ppermute x58, waiting for transfers between devices, swap(): return lax.ppermute(x, axis, [(i, i ^ mask) for i in range(size)])  31.4 us
    all_gather x1, blocking collectives, local(): chain = lax.all_gather(chain_map[None], 'row', axis=0, tiled=True)  21.9 us
    pallas_call x4, Pallas kernels, factor(): pl.pallas_call(functools.partial(factor_kernel, step, col_count), in_spec...  20.4 us
    ppermute x12, starting transfers between devices, spread(): lax.ppermute(down, 'row', [(i + 1, i) for i in range(row_count - 1)])  15.5 us
    ppermute x12, waiting for transfers between devices, spread(): lax.ppermute(down, 'row', [(i + 1, i) for i in range(row_count - 1)])  14.1 us
  transfers between devices with their start and end apart: 83, of which 26 were waited for; matrix products, arithmetic and copies ran while one was open for 3% of the time, Pallas kernels for 10%

profile of v1, /device:TPU:0, one launch (start us, length us, event | category | flops | bytes accessed | tf_op | source)
XLA Modules:
  0.0 391.9 jit_solution(15530308837050528119)
XLA Ops:
  9.8 4.9 %collective-permute-start.4 = (f32[4,128,128]{2,1,0:T(8,128)S(1)}, f32[4,128,128]{2,1,0:T(8,128)S(1)}, u32[]{:S(2)}, u32[]{:S(2)}) collective-permute-start(f32[4,128,128]{2,1,0:T(8,128)S(1)} %slice_bitcast_fusion), channel_id=1, source_target_pairs={{0,1},{1,2},{2,3},{4,5},{5,6},{6,7},{8,9},{9,10},{10,11},{12,13},{... | collective-permute-start | bytes 786440 | tf_op jit(solution)/shard_map/ppermute | solution.py:72
  16.1 21.9 %all-gather = s32[12,8,2]{1,2,0:T(2,128)S(1)} all-gather(s32[3,8,2]{1,2,0:T(2,128)S(1)} %copy-done.10), channel_id=2, replica_groups=mesh['col'=8,'row'=4] {'row'}, dimensions={0}, use_global_device_ids=true | all-gather | bytes 960 | tf_op jit(solution)/shard_map/all_gather | solution.py:333
  55.4 6.1 %collective-permute-done.5 = f32[4,128,128]{2,1,0:T(8,128)S(1)} collective-permute-done((f32[4,128,128]{2,1,0:T(8,128)S(1)}, f32[4,128,128]{2,1,0:T(8,128)S(1)}, u32[]{:S(2)}, u32[]{:S(2)}) %collective-permute-start.5) | collective-permute-done | bytes 262176 | tf_op jit(solution)/shard_map/ppermute | solution.py:72
  63.0 10.4 %collective-permute-start.6 = (f32[4,128,128]{2,1,0:T(8,128)S(1)}, f32[4,128,128]{2,1,0:T(8,128)S(1)}, u32[]{:S(2)}, u32[]{:S(2)}) collective-permute-start(f32[4,128,128]{2,1,0:T(8,128)S(1)} %get-tuple-element.86), channel_id=1, source_target_pairs={{0,1},{1,2},{2,3},{4,5},{5,6},{6,7},{8,9},{9,10},{10,11},{12,13},{... | collective-permute-start | bytes 786440 | tf_op jit(solution)/shard_map/ppermute | solution.py:72
  73.4 96.0 %all-gather.4.cloned.1.call-done = bf16[256,128,128]{2,1,0:T(8,128)(2,1)} async-done(((bf16[64,128,128]{2,1,0:T(8,128)(2,1)}), bf16[256,128,128]{2,1,0:T(8,128)(2,1)}) %all-gather.4.cloned.1.call-update) | async-done | bytes 8388624 | tf_op jit(solution)/shard_map/all_gather | solution.py:330
  191.3 3.9 collective-permute-start
  198.3 3.9 collective-permute-start.58
  202.5 8.5 %collective-permute-start.11 = (f32[3,128,128]{2,1,0:T(8,128)S(1)}, f32[3,128,128]{2,1,0:T(8,128)S(1)}, u32[]{:S(2)}, u32[]{:S(2)}) collective-permute-start(f32[3,128,128]{2,1,0:T(8,128)S(1)} %get-tuple-element.77), channel_id=1, source_target_pairs={{0,8},{4,12},{8,0},{12,4},{16,24},{20,28},{24,16},{28,20},{1,9},{5... | collective-permute-start | bytes 589832 | tf_op jit(solution)/shard_map/ppermute | solution.py:49
  218.1 5.0 %collective-permute-done.12 = f32[3,128,128]{2,1,0:T(8,128)S(1)} collective-permute-done((f32[3,128,128]{2,1,0:T(8,128)S(1)}, f32[3,128,128]{2,1,0:T(8,128)S(1)}, u32[]{:S(2)}, u32[]{:S(2)}) %collective-permute-start.12) | collective-permute-done | bytes 196640 | tf_op jit(solution)/shard_map/ppermute | solution.py:49
  226.6 4.8 %collective-permute-done.36 = f32[3,128,128]{2,1,0:T(8,128)S(1)} collective-permute-done((f32[3,128,128]{2,1,0:T(8,128)S(1)}, f32[3,128,128]{2,1,0:T(8,128)S(1)}, u32[]{:S(2)}, u32[]{:S(2)}) %collective-permute-start.36) | collective-permute-done | bytes 196640 | tf_op jit(solution)/shard_map/ppermute | solution.py:49
  235.1 4.8 %collective-permute-done.2 = f32[3,128,128]{2,1,0:T(8,128)S(1)} collective-permute-done((f32[3,128,128]{2,1,0:T(8,128)S(1)}, f32[3,128,128]{2,1,0:T(8,128)S(1)}, u32[]{:S(2)}, u32[]{:S(2)}) %collective-permute-start.2) | collective-permute-done | bytes 196640 | tf_op jit(solution)/shard_map/ppermute | solution.py:49
  242.2 5.3 %collective-permute-done.60 = f32[3,128,128]{2,1,0:T(8,128)S(1)} collective-permute-done((f32[3,128,128]{2,1,0:T(8,128)S(1)}, f32[3,128,128]{2,1,0:T(8,128)S(1)}, u32[]{:S(2)}, u32[]{:S(2)}) %collective-permute-start.60) | collective-permute-done | bytes 196640 | tf_op jit(solution)/shard_map/ppermute | solution.py:49
  247.7 5.0 %factor.4 = (f32[128,128]{1,0:T(8,128)S(1)}, f32[128,128]{1,0:T(8,128)S(1)}) custom-call(s32[4,8,4]{2,1,0:T(8,128)S(1)} %copy-done.3, f32[128,128]{1,0:T(8,128)S(1)} %get-tuple-element.92.start), custom_call_target="tpu_custom_call" | custom-call | flops 419430400 | bytes 262144 | tf_op jit(solution)/shard_map/factor/pallas_call | solution.py:242
  258.3 5.2 %collective-permute-start.14 = (f32[3,128,128]{2,1,0:T(8,128)S(1)}, f32[3,128,128]{2,1,0:T(8,128)S(1)}, u32[]{:S(2)}, u32[]{:S(2)}) collective-permute-start(f32[3,128,128]{2,1,0:T(8,128)S(1)} %gather_fusion.1), channel_id=1, source_target_pairs={{0,1},{1,2},{2,3},{4,5},{5,6},{6,7},{8,9},{9,10},{10,11},{12,13},{... | collective-permute-start | bytes 589832 | tf_op jit(solution)/shard_map/ppermute | solution.py:72
  266.7 4.4 %collective-permute-start.62 = (f32[1,128,128]{2,1,0:T(8,128)S(1)}, f32[1,128,128]{2,1,0:T(8,128)S(1)}, u32[]{:S(2)}, u32[]{:S(2)}) collective-permute-start(f32[1,128,128]{2,1,0:T(8,128)S(1)} %constant_dynamic-slice_fusion), channel_id=1, source_target_pairs={{0,1},{1,2},{2,3},{4,5},{5,6},{6,7},{8,9},{9,10},{10,11},{12,13},{... | collective-permute-start | bytes 196616 | tf_op jit(solution)/shard_map/ppermute | solution.py:72
  273.0 4.3 %collective-permute-start.15 = (f32[3,128,128]{2,1,0:T(8,128)S(1)}, f32[3,128,128]{2,1,0:T(8,128)S(1)}, u32[]{:S(2)}, u32[]{:S(2)}) collective-permute-start(f32[3,128,128]{2,1,0:T(8,128)S(1)} %broadcast_select_fusion.7), channel_id=1, source_target_pairs={{0,1},{1,2},{2,3},{4,5},{5,6},{6,7},{8,9},{9,10},{10,11},{12,13},{... | collective-permute-start | bytes 589832 | tf_op jit(solution)/shard_map/ppermute | solution.py:72
  277.3 3.9 %collective-permute-start.38 = (f32[2,128,128]{2,1,0:T(8,128)S(1)}, f32[2,128,128]{2,1,0:T(8,128)S(1)}, u32[]{:S(2)}, u32[]{:S(2)}) collective-permute-start(f32[2,128,128]{2,1,0:T(8,128)S(1)} %gather_fusion.2), channel_id=1, source_target_pairs={{0,1},{1,2},{2,3},{4,5},{5,6},{6,7},{8,9},{9,10},{10,11},{12,13},{... | collective-permute-start | bytes 393224 | tf_op jit(solution)/shard_map/ppermute | solution.py:72
  285.1 6.6 %collective-permute-done.18 = f32[3,128,128]{2,1,0:T(8,128)S(1)} collective-permute-done((f32[3,128,128]{2,1,0:T(8,128)S(1)}, f32[3,128,128]{2,1,0:T(8,128)S(1)}, u32[]{:S(2)}, u32[]{:S(2)}) %collective-permute-start.18) | collective-permute-done | bytes 196640 | tf_op jit(solution)/shard_map/ppermute | solution.py:74
  291.7 4.1 %collective-permute-start.39 = (f32[2,128,128]{2,1,0:T(8,128)S(1)}, f32[2,128,128]{2,1,0:T(8,128)S(1)}, u32[]{:S(2)}, u32[]{:S(2)}) collective-permute-start(f32[2,128,128]{2,1,0:T(8,128)S(1)} %broadcast_select_fusion.11), channel_id=1, source_target_pairs={{0,1},{1,2},{2,3},{4,5},{5,6},{6,7},{8,9},{9,10},{10,11},{12,13},{... | collective-permute-start | bytes 393224 | tf_op jit(solution)/shard_map/ppermute | solution.py:72
  323.8 3.9 collective-permute-start.40
  329.1 5.2 %factor.5 = (f32[128,128]{1,0:T(8,128)S(1)}, f32[128,128]{1,0:T(8,128)S(1)}) custom-call(s32[4,8,4]{2,1,0:T(8,128)S(1)} %copy-done.3, f32[128,128]{1,0:T(8,128)S(1)} %get-tuple-element.95.start, bf16[3,128,128]{2,1,0:T(8,128)(2,1)S(1)} %ahead_blocks.3.refs_0_, bf16[3,128,128]{2,1,0:T(8,128)(2,1)S(1)} %collective-permute-done.20.refs_1_, ...), custom_call_target="tpu_custom_call" | custom-call | flops 419430400 | bytes 262144 | tf_op jit(solution)/shard_map/factor/pallas_call | solution.py:242
  334.2 4.5 %collective-permute-start.64 = (f32[1,128,128]{2,1,0:T(8,128)S(1)}, f32[1,128,128]{2,1,0:T(8,128)S(1)}, u32[]{:S(2)}, u32[]{:S(2)}) collective-permute-start(f32[1,128,128]{2,1,0:T(8,128)S(1)} %get-tuple-element.100), channel_id=1, source_target_pairs={{0,1},{1,2},{2,3},{4,5},{5,6},{6,7},{8,9},{9,10},{10,11},{12,13},{... | collective-permute-start | bytes 196616 | tf_op jit(solution)/shard_map/ppermute | solution.py:72
  356.3 5.1 %factor.6 = (f32[128,128]{1,0:T(8,128)S(1)}, f32[128,128]{1,0:T(8,128)S(1)}) custom-call(s32[4,8,4]{2,1,0:T(8,128)S(1)} %copy-done.3, f32[128,128]{1,0:T(8,128)S(1)} %get-tuple-element.94.start, bf16[2,128,128]{2,1,0:T(8,128)(2,1)S(1)} %ahead_blocks.4.refs_0_, bf16[2,128,128]{2,1,0:T(8,128)(2,1)S(1)} %collective-permute-done.44.refs_1_, ...), custom_call_target="tpu_custom_call" | custom-call | flops 419430400 | bytes 262144 | tf_op jit(solution)/shard_map/factor/pallas_call | solution.py:242
  376.7 5.2 %factor.7 = (f32[128,128]{1,0:T(8,128)S(1)}, f32[128,128]{1,0:T(8,128)S(1)}) custom-call(s32[4,8,4]{2,1,0:T(8,128)S(1)} %copy-done.3, f32[128,128]{1,0:T(8,128)S(1)} %get-tuple-element.93.start, bf16[1,128,128]{2,1,0:T(8,128)(2,1)S(1)} %ahead_blocks.5.refs_0_, bf16[1,128,128]{2,1,0:T(8,128)(2,1)S(1)} %collective-permute-done.68.refs_1_, ...), custom_call_target="tpu_custom_call" | custom-call | flops 419430400 | bytes 262144 | tf_op jit(solution)/shard_map/factor/pallas_call | solution.py:242
  (242 shorter events, 140.9 us)
Async XLA Ops:
  6.5 162.9 %all-gather.4.cloned.1.call-start = ((), (), s32[]{:S(2)}) async-start(), calls=%async_computation | async-start | bytes 10485760 | tf_op jit(solution)/shard_map/all_gather | solution.py:330
  9.8 39.8 %collective-permute-start.4 = (f32[4,128,128]{2,1,0:T(8,128)S(1)}, f32[4,128,128]{2,1,0:T(8,128)S(1)}, u32[]{:S(2)}, u32[]{:S(2)}) collective-permute-start(f32[4,128,128]{2,1,0:T(8,128)S(1)} %slice_bitcast_fusion), channel_id=1, source_target_pairs={{0,1},{1,2},{2,3},{4,5},{5,6},{6,7},{8,9},{9,10},{10,11},{12,13},{... | collective-permute-start | bytes 786440 | tf_op jit(solution)/shard_map/ppermute | solution.py:72
  14.8 40.6 %collective-permute-start.7 = (f32[4,128,128]{2,1,0:T(8,128)S(1)}, f32[4,128,128]{2,1,0:T(8,128)S(1)}, u32[]{:S(2)}, u32[]{:S(2)}) collective-permute-start(f32[4,128,128]{2,1,0:T(8,128)S(1)} %slice_bitcast_fusion), channel_id=1, source_target_pairs={{1,0},{2,1},{3,2},{5,4},{6,5},{7,6},{9,8},{10,9},{11,10},{13,12},{... | collective-permute-start | bytes 786440 | tf_op jit(solution)/shard_map/ppermute | solution.py:74
  61.7 124.0 %collective-permute-start.8 = (f32[4,128,128]{2,1,0:T(8,128)S(1)}, f32[4,128,128]{2,1,0:T(8,128)}, u32[]{:S(2)}, u32[]{:S(2)}) collective-permute-start(f32[4,128,128]{2,1,0:T(8,128)S(1)} %get-tuple-element.87), channel_id=1, source_target_pairs={{1,0},{2,1},{3,2},{5,4},{6,5},{7,6},{9,8},{10,9},{11,10},{13,12},{... | collective-permute-start | bytes 786440 | tf_op jit(solution)/shard_map/ppermute | solution.py:74
  63.0 135.3 %collective-permute-start.6 = (f32[4,128,128]{2,1,0:T(8,128)S(1)}, f32[4,128,128]{2,1,0:T(8,128)S(1)}, u32[]{:S(2)}, u32[]{:S(2)}) collective-permute-start(f32[4,128,128]{2,1,0:T(8,128)S(1)} %get-tuple-element.86), channel_id=1, source_target_pairs={{0,1},{1,2},{2,3},{4,5},{5,6},{6,7},{8,9},{9,10},{10,11},{12,13},{... | collective-permute-start | bytes 786440 | tf_op jit(solution)/shard_map/ppermute | solution.py:72
  174.8 27.6 %collective-permute-start.10 = (f32[4,3,128,128]{3,2,1,0:T(8,128)S(1)}, f32[4,3,128,128]{3,2,1,0:T(8,128)S(1)}, u32[]{:S(2)}, u32[]{:S(2)}) collective-permute-start(f32[4,3,128,128]{3,2,1,0:T(8,128)S(1)} %get-tuple-element.43), channel_id=1, source_target_pairs={{0,4},{4,0},{8,12},{12,8},{16,20},{20,16},{24,28},{28,24},{1,5},{5... | collective-permute-start | bytes 2359304 | tf_op jit(solution)/shard_map/ppermute | solution.py:49
  181.8 29.2 %collective-permute-start.34 = (f32[4,3,128,128]{3,2,1,0:T(8,128)S(1)}, f32[4,3,128,128]{3,2,1,0:T(8,128)S(1)}, u32[]{:S(2)}, u32[]{:S(2)}) collective-permute-start(f32[4,3,128,128]{3,2,1,0:T(8,128)S(1)} %get-tuple-element.50), channel_id=1, source_target_pairs={{0,4},{4,0},{8,12},{12,8},{16,20},{20,16},{24,28},{28,24},{1,5},{5... | collective-permute-start | bytes 2359304 | tf_op jit(solution)/shard_map/ppermute | solution.py:49
  186.8 15.5 %collective-permute-start.9 = (f32[4,128,128]{2,1,0:T(8,128)S(1)}, f32[4,128,128]{2,1,0:T(8,128)S(1)}, u32[]{:S(2)}, u32[]{:S(2)}) collective-permute-start(f32[4,128,128]{2,1,0:T(8,128)S(1)} %broadcast_select_fusion), channel_id=1, source_target_pairs={{1,0},{2,1},{3,2},{5,4},{6,5},{7,6},{9,8},{10,9},{11,10},{13,12},{... | collective-permute-start | bytes 786440 | tf_op jit(solution)/shard_map/ppermute | solution.py:74
  191.3 21.5 %collective-permute-start = (f32[4,3,128,128]{3,2,1,0:T(8,128)S(1)}, f32[4,3,128,128]{3,2,1,0:T(8,128)S(1)}, u32[]{:S(2)}, u32[]{:S(2)}) collective-permute-start(f32[4,3,128,128]{3,2,1,0:T(8,128)S(1)} %get-tuple-element.37), channel_id=1, source_target_pairs={{0,4},{4,0},{8,12},{12,8},{16,20},{20,16},{24,28},{28,24},{1,5},{5... | collective-permute-start | bytes 2359304 | tf_op jit(solution)/shard_map/ppermute | solution.py:49
  198.3 16.6 %collective-permute-start.58 = (f32[4,3,128,128]{3,2,1,0:T(8,128)S(1)}, f32[4,3,128,128]{3,2,1,0:T(8,128)S(1)}, u32[]{:S(2)}, u32[]{:S(2)}) collective-permute-start(f32[4,3,128,128]{3,2,1,0:T(8,128)S(1)} %get-tuple-element.56), channel_id=1, source_target_pairs={{0,4},{4,0},{8,12},{12,8},{16,20},{20,16},{24,28},{28,24},{1,5},{5... | collective-permute-start | bytes 2359304 | tf_op jit(solution)/shard_map/ppermute | solution.py:49
  202.5 14.3 %collective-permute-start.11 = (f32[3,128,128]{2,1,0:T(8,128)S(1)}, f32[3,128,128]{2,1,0:T(8,128)S(1)}, u32[]{:S(2)}, u32[]{:S(2)}) collective-permute-start(f32[3,128,128]{2,1,0:T(8,128)S(1)} %get-tuple-element.77), channel_id=1, source_target_pairs={{0,8},{4,12},{8,0},{12,4},{16,24},{20,28},{24,16},{28,20},{1,9},{5... | collective-permute-start | bytes 589832 | tf_op jit(solution)/shard_map/ppermute | solution.py:49
  214.9 16.5 %collective-permute-start.36 = (f32[3,128,128]{2,1,0:T(8,128)S(1)}, f32[3,128,128]{2,1,0:T(8,128)S(1)}, u32[]{:S(2)}, u32[]{:S(2)}) collective-permute-start(f32[3,128,128]{2,1,0:T(8,128)S(1)} %get-tuple-element.82), channel_id=1, source_target_pairs={{0,16},{4,20},{8,24},{12,28},{16,0},{20,4},{24,8},{28,12},{1,17},{... | collective-permute-start | bytes 589832 | tf_op jit(solution)/shard_map/ppermute | solution.py:49
  216.8 14.7 %collective-permute-start.37 = (f32[3,128,128]{2,1,0:T(8,128)S(1)}, f32[3,128,128]{2,1,0:T(8,128)S(1)}, u32[]{:S(2)}, u32[]{:S(2)}) collective-permute-start(f32[3,128,128]{2,1,0:T(8,128)S(1)} %get-tuple-element.81), channel_id=1, source_target_pairs={{0,24},{4,28},{8,16},{12,20},{16,8},{20,12},{24,0},{28,4},{1,25},{... | collective-permute-start | bytes 589832 | tf_op jit(solution)/shard_map/ppermute | solution.py:49
  223.0 16.8 %collective-permute-start.2 = (f32[3,128,128]{2,1,0:T(8,128)S(1)}, f32[3,128,128]{2,1,0:T(8,128)S(1)}, u32[]{:S(2)}, u32[]{:S(2)}) collective-permute-start(f32[3,128,128]{2,1,0:T(8,128)S(1)} %get-tuple-element.76), channel_id=1, source_target_pairs={{0,16},{4,20},{8,24},{12,28},{16,0},{20,4},{24,8},{28,12},{1,17},{... | collective-permute-start | bytes 589832 | tf_op jit(solution)/shard_map/ppermute | solution.py:49
  225.3 14.6 %collective-permute-start.3 = (f32[3,128,128]{2,1,0:T(8,128)S(1)}, f32[3,128,128]{2,1,0:T(8,128)S(1)}, u32[]{:S(2)}, u32[]{:S(2)}) collective-permute-start(f32[3,128,128]{2,1,0:T(8,128)S(1)} %get-tuple-element.75), channel_id=1, source_target_pairs={{0,24},{4,28},{8,16},{12,20},{16,8},{20,12},{24,0},{28,4},{1,25},{... | collective-permute-start | bytes 589832 | tf_op jit(solution)/shard_map/ppermute | solution.py:49
  231.5 16.1 %collective-permute-start.60 = (f32[3,128,128]{2,1,0:T(8,128)S(1)}, f32[3,128,128]{2,1,0:T(8,128)S(1)}, u32[]{:S(2)}, u32[]{:S(2)}) collective-permute-start(f32[3,128,128]{2,1,0:T(8,128)S(1)} %get-tuple-element.85), channel_id=1, source_target_pairs={{0,16},{4,20},{8,24},{12,28},{16,0},{20,4},{24,8},{28,12},{1,17},{... | collective-permute-start | bytes 589832 | tf_op jit(solution)/shard_map/ppermute | solution.py:49
  254.2 57.3 %collective-permute-start.27 = (bf16[2,128,128]{2,1,0:T(8,128)(2,1)S(1)}, bf16[2,128,128]{2,1,0:T(8,128)(2,1)S(1)}, u32[]{:S(2)}, u32[]{:S(2)}) collective-permute-start(bf16[2,128,128]{2,1,0:T(8,128)(2,1)S(1)} %get-tuple-element.47.refs_8_), channel_id=1, source_target_pairs={{0,8},{4,12},{8,0},{12,4},{16,24},{20,28},{24,16},{28,20},{1,9},{5... | collective-permute-start | bytes 196616 | tf_op jit(solution)/shard_map/ppermute | solution.py:49
  254.6 56.9 %collective-permute-start.28 = (bf16[2,128,128]{2,1,0:T(8,128)(2,1)S(1)}, bf16[2,128,128]{2,1,0:T(8,128)(2,1)S(1)}, u32[]{:S(2)}, u32[]{:S(2)}) collective-permute-start(bf16[2,128,128]{2,1,0:T(8,128)(2,1)S(1)} %get-tuple-element.47.refs_8_), channel_id=1, source_target_pairs={{0,16},{4,20},{8,24},{12,28},{16,0},{20,4},{24,8},{28,12},{1,17},{... | collective-permute-start | bytes 196616 | tf_op jit(solution)/shard_map/ppermute | solution.py:49
  256.1 56.7 %collective-permute-start.29 = (bf16[2,128,128]{2,1,0:T(8,128)(2,1)S(1)}, bf16[2,128,128]{2,1,0:T(8,128)(2,1)S(1)}, u32[]{:S(2)}, u32[]{:S(2)}) collective-permute-start(bf16[2,128,128]{2,1,0:T(8,128)(2,1)S(1)} %get-tuple-element.47.refs_8_), channel_id=1, source_target_pairs={{0,24},{4,28},{8,16},{12,20},{16,8},{20,12},{24,0},{28,4},{1,25},{... | collective-permute-start | bytes 196616 | tf_op jit(solution)/shard_map/ppermute | solution.py:49
  281.2 14.7 %collective-permute-start.41 = (f32[2,128,128]{2,1,0:T(8,128)S(1)}, f32[2,128,128]{2,1,0:T(8,128)S(1)}, u32[]{:S(2)}, u32[]{:S(2)}) collective-permute-start(f32[2,128,128]{2,1,0:T(8,128)S(1)} %gather_fusion.2), channel_id=1, source_target_pairs={{1,0},{2,1},{3,2},{5,4},{6,5},{7,6},{9,8},{10,9},{11,10},{13,12},{... | collective-permute-start | bytes 393224 | tf_op jit(solution)/shard_map/ppermute | solution.py:74
  323.2 15.6 %collective-permute-start.32 = (bf16[2,128,128]{2,1,0:T(8,128)(2,1)S(1)}, bf16[2,128,128]{2,1,0:T(8,128)(2,1)S(1)}, u32[]{:S(2)}, u32[]{:S(2)}) collective-permute-start(bf16[2,128,128]{2,1,0:T(8,128)(2,1)S(1)} %collective-permute-done.28.refs_10_), channel_id=1, source_target_pairs={{0,4},{4,0},{8,12},{12,8},{16,20},{20,16},{24,28},{28,24},{1,5},{5... | collective-permute-start | bytes 196616 | tf_op jit(solution)/shard_map/ppermute | solution.py:49
  323.7 16.4 %collective-permute-start.33 = (bf16[2,128,128]{2,1,0:T(8,128)(2,1)S(1)}, bf16[2,128,128]{2,1,0:T(8,128)(2,1)S(1)}, u32[]{:S(2)}, u32[]{:S(2)}) collective-permute-start(bf16[2,128,128]{2,1,0:T(8,128)(2,1)S(1)} %collective-permute-done.29.refs_11_), channel_id=1, source_target_pairs={{0,4},{4,0},{8,12},{12,8},{16,20},{20,16},{24,28},{28,24},{1,5},{5... | collective-permute-start | bytes 196616 | tf_op jit(solution)/shard_map/ppermute | solution.py:49
  323.8 18.3 %collective-permute-start.40 = (f32[2,128,128]{2,1,0:T(8,128)S(1)}, f32[2,128,128]{2,1,0:T(8,128)S(1)}, u32[]{:S(2)}, u32[]{:S(2)}) collective-permute-start(f32[2,128,128]{2,1,0:T(8,128)S(1)} %get-tuple-element.98), channel_id=1, source_target_pairs={{0,1},{1,2},{2,3},{4,5},{5,6},{6,7},{8,9},{9,10},{10,11},{12,13},{... | collective-permute-start | bytes 393224 | tf_op jit(solution)/shard_map/ppermute | solution.py:72
  327.7 14.4 %collective-permute-start.43 = (f32[2,128,128]{2,1,0:T(8,128)S(1)}, f32[2,128,128]{2,1,0:T(8,128)S(1)}, u32[]{:S(2)}, u32[]{:S(2)}) collective-permute-start(f32[2,128,128]{2,1,0:T(8,128)S(1)} %broadcast_select_fusion.8), channel_id=1, source_target_pairs={{1,0},{2,1},{3,2},{5,4},{6,5},{7,6},{9,8},{10,9},{11,10},{13,12},{... | collective-permute-start | bytes 393224 | tf_op jit(solution)/shard_map/ppermute | solution.py:74
  (70 other events, 681.4 us)
Sparse Core Ops, SparseCore 0:
  9.9 159.4 all-gather.3

commit v2 on v1

v2 whole, which is shorter than its diff:
```python
import functools

import jax
import jax.numpy as jnp
from jax import lax
from jax.experimental import pallas as pl
from jax.experimental.pallas import tpu as pltpu
from jax.sharding import PartitionSpec as P

F32 = jnp.float32
BF16 = jnp.bfloat16
HIGHEST = lax.Precision.HIGHEST
CHUNK = 8
PANEL = 32
MIB = 1024 * 1024


def vmem():
    return pl.BlockSpec(memory_space=pltpu.VMEM)


def smem():
    return pl.BlockSpec(memory_space=pltpu.SMEM)


def params(mib):
    return pltpu.CompilerParams(vmem_limit_bytes=mib * MIB)


def cost(flops, size):
    return pl.CostEstimate(flops=flops, bytes_accessed=size, transcendentals=0)


def times_transposed(a, b, precision=None):
    return lax.dot_general(
        a, b, (((1,), (1,)), ((), ())), precision=precision, preferred_element_type=F32
    )


def transposed_times(a, b):
    return lax.dot_general(a, b, (((0,), (0,)), ((), ())), preferred_element_type=F32)


def slot_column(slot, chips, own):
    return own ^ (2 * (slot % chips) + slot // chips)


def swap(x, axis, size, mask):
    return lax.ppermute(x, axis, [(i, i ^ mask) for i in range(size)])


def gather_columns(x, col_count):
    chips = col_count // 2
    same = [x] + [swap(x, "col", col_count, 2 * m) for m in range(1, chips)]
    return same + [swap(y, "col", col_count, 1) for y in same]


def scatter_sum(other_half, own_half, col_count):
    chips = col_count // 2
    halves = own_half + swap(other_half, "col", col_count, 1)
    whole = halves[0]
    for m in range(1, chips):
        whole = whole + swap(halves[m], "col", col_count, 2 * m)
    return halves, whole


def tables_kernel(col_count, place, diag, parent, chain, roots, picks, ahead, keep, into):
    sections = diag.shape[0]
    local_blocks = chain.shape[3]
    chips = col_count // 2
    own = place[0]
    row = place[1]

    def path(s, column):
        columns = [column]
        for t in range(s, sections - 1):
            columns.append(parent[t, columns[-1]])
        return columns

    def block_of(s, columns, j):
        if j == 0:
            return jnp.int32(0)
        if j == 1:
            return jnp.int32(1)
        wanted = block_of(s + 1, columns[1:], j - 1)
        group = diag[s + j, columns[j]]
        found = jnp.int32(0)
        for q in range(1, local_blocks):
            found = jnp.where(chain[group, s, columns[0], q] == wanted, q, found)
        return found

    for s in range(sections):
        columns = path(s, own)
        for j in range(sections):
            if j < sections - s:
                roots[s, j] = diag[s + j, columns[j]]
                picks[s, j] = block_of(s, columns, j)
            else:
                roots[s, j] = 0
                picks[s, j] = 0
    for s in range(1, sections):
        for slot in range(col_count):
            child = slot_column(slot, chips, own)
            hit = parent[s - 1, child] == own
            columns = path(s - 1, child)
            for j in range(sections):
                if j < sections - s:
                    block = block_of(s - 1, columns, j + 1)
                    group = diag[s + j, columns[j + 1]]
                    left_out = (block == 0) & (group == diag[s - 1, child])
                    ahead[s, slot, j] = jnp.where(hit & jnp.logical_not(left_out), 1, 0)
                else:
                    ahead[s, slot, j] = 0
            for q in range(local_blocks):
                left_out = (diag[s - 1, child] == row) & (q == 0)
                keep[s, slot, q] = jnp.where(hit & jnp.logical_not(left_out), 1, 0)
                into[s, slot, q] = chain[row, s - 1, child, q]


def pick_kernel(index, source, out):
    for i in range(out.shape[0]):
        out[i] = source[index[i]]


def pick(source, index, block, rows):
    count, width = index.shape[0], source.shape[2]
    return pl.pallas_call(
        pick_kernel,
        grid_spec=pltpu.PrefetchScalarGridSpec(
            num_scalar_prefetch=1,
            grid=(1,),
            in_specs=[pl.BlockSpec((source.shape[0], rows, width), lambda g, a: (0, block, 0))],
            out_specs=pl.BlockSpec((count, rows, width), lambda g, a: (0, 0, 0)),
        ),
        out_shape=jax.ShapeDtypeStruct((count, rows, width), source.dtype),
        compiler_params=params(12),
        cost_estimate=cost(0, 4 * count * rows * width),
        name="pick",
    )(index, source)


def diagonal_kernel(table, heads, other, own, total):
    g = pl.program_id(0)
    chips = own.shape[0]
    sections = table.shape[0]

    @pl.when(g == 0)
    def _():
        total[...] = jnp.zeros_like(total)

    for t in range(heads.shape[0]):
        product = times_transposed(heads[t], heads[t])
        for s in range(sections):
            total[table[s, 0, g * heads.shape[0] + t], s] += product

    @pl.when(g == pl.num_programs(0) - 1)
    def _():
        own[...] = total[:chips]
        other[...] = total[chips : 2 * chips]


def diagonal_sums(table, heads, chips):
    count, width, _ = heads.shape
    sections = table.shape[0]
    chunk = min(CHUNK, count)
    half = (chips, sections, width, width)
    out = jax.ShapeDtypeStruct(half, F32)
    return pl.pallas_call(
        diagonal_kernel,
        grid_spec=pltpu.PrefetchScalarGridSpec(
            num_scalar_prefetch=1,
            grid=(count // chunk,),
            in_specs=[pl.BlockSpec((chunk, width, width), lambda g, a: (g, 0, 0))],
            out_specs=[pl.BlockSpec(half, lambda g, a: (0, 0, 0, 0))] * 2,
            scratch_shapes=[pltpu.VMEM((2 * chips + 1,) + half[1:], F32)],
        ),
        out_shape=[out, out],
        compiler_params=params(6 * chips * sections * width * width * 4 // MIB + 8),
        cost_estimate=cost(count * width * width * width * 4, count * width * width * 4),
        name="diagonal_sums",
    )(table, heads)


def source_kernel(table, first, second, heads, after, other, own, total):
    del after
    g = pl.program_id(0)
    chunk, width, _ = first.shape
    chips = own.shape[0]
    blocks = second.shape[1] + 1
    sections = table.shape[0]

    @pl.when(g == 0)
    def _():
        total[...] = jnp.zeros_like(total)

    for t in range(chunk):
        i = g * chunk + t
        panel = jnp.concatenate([first[t]] + [second[t, q] for q in range(blocks - 1)], axis=0)
        for begin in range(0, sections, 2):
            steps = range(begin, min(begin + 2, sections))
            stacked = jnp.concatenate([heads[table[s, 1, i], t] for s in steps], axis=0)
            product = times_transposed(panel, stacked)
            for k, s in enumerate(steps):
                slot = table[s, 0, i]
                for q in range(blocks):
                    total[slot, s * blocks + table[s, 2 + q, i]] += product[
                        q * width : (q + 1) * width, k * width : (k + 1) * width
                    ]

    @pl.when(g == pl.num_programs(0) - 1)
    def _():
        other[...] = total[chips : 2 * chips]
        own[...] = total[:chips]


def source_sums(table, first, second, heads, after, chips):
    count, width, _ = first.shape
    blocks = 1 + second.shape[1]
    sections = table.shape[0]
    chunk = min(CHUNK, count)
    half = (chips, sections * blocks, width, width)
    out = jax.ShapeDtypeStruct(half, F32)
    size = 4 * chips * sections * blocks * width * width
    return pl.pallas_call(
        source_kernel,
        grid_spec=pltpu.PrefetchScalarGridSpec(
            num_scalar_prefetch=1,
            grid=(count // chunk,),
            in_specs=[
                pl.BlockSpec((chunk, width, width), lambda g, a: (g, 0, 0)),
                pl.BlockSpec((chunk, blocks - 1, width, width), lambda g, a: (g, 0, 0, 0)),
                pl.BlockSpec((heads.shape[0], chunk, width, width), lambda g, a: (0, g, 0, 0)),
                pl.BlockSpec(memory_space=pl.ANY),
            ],
            out_specs=[pl.BlockSpec(half, lambda g, a: (0, 0, 0, 0))] * 2,
            scratch_shapes=[pltpu.VMEM((2 * chips,) + half[1:], F32)],
        ),
        out_shape=[out, out],
        compiler_params=params(6 * size // MIB + 12),
        cost_estimate=cost(
            count * blocks * width * width * width * 2 * sections, count * width * width * 12
        ),
        name="source_sums",
    )(table, first, second, heads, after)


def split(x):
    high = x.astype(BF16)
    rest = x - high.astype(F32)
    middle = rest.astype(BF16)
    low = (rest - middle.astype(F32)).astype(BF16)
    return high, middle, low


def factor_kernel(step, col_count, flags, start, *refs):
    children, (upper, inverse, work) = refs[:-3], refs[-3:]
    width = start.shape[0]
    work[:, :width] = start[...]
    for slot, child in enumerate(children):

        @pl.when(flags[step, slot, 0] > 0)
        def _(child=child):
            work[:, :width] -= times_transposed(child[0], child[0])

    rows = lax.broadcasted_iota(jnp.int32, (width, width), 0)
    columns = lax.broadcasted_iota(jnp.int32, (width, width), 1)
    work[:, width:] = (rows == columns).astype(F32)
    sub = lax.broadcasted_iota(jnp.int32, (PANEL, 1), 0)
    for first in range(0, width, PANEL):
        last = first + PANEL
        slab = work[first:last, :]
        spans = [
            jnp.broadcast_to(slab[:, first + k : first + k + 1], (PANEL, width))
            for k in range(PANEL)
        ]
        scale = jnp.zeros((PANEL, 1), F32)
        for j in range(PANEL):
            pivot = spans[j][j : j + 1, :]
            ratio = jnp.where(sub > j, spans[j] * (1.0 / pivot), 0.0)
            for k in range(j + 1, PANEL):
                spans[k] = spans[k] - ratio * spans[k][j : j + 1, :]
            slab = slab - jnp.concatenate([ratio, ratio], axis=1) * slab[j : j + 1, :]
            scale = jnp.where(sub == j, lax.rsqrt(pivot[:, 0:1]), scale)
        slab = slab * scale
        work[first:last, :] = slab
        if last < width:
            high, middle, low = split(slab)
            left = jnp.concatenate([high, high, middle, middle, high, low], axis=0)
            right = jnp.concatenate([high, middle, high, middle, low, high], axis=0)
            work[last:, :] = work[last:, :] - transposed_times(left[:, last:width], right)
    upper[...] = jnp.where(rows <= columns, work[:, :width], 0.0)
    inverse[...] = work[:, width:]


def factor(step, flags, start, children, col_count):
    width = start.shape[0]
    out = jax.ShapeDtypeStruct((width, width), F32)
    return pl.pallas_call(
        functools.partial(factor_kernel, step, col_count),
        in_specs=[smem(), vmem()] + [vmem()] * len(children),
        out_specs=[vmem(), vmem()],
        out_shape=[out, out],
        scratch_shapes=[pltpu.VMEM((width, 2 * width), F32)],
        compiler_params=params(8),
        cost_estimate=cost(width * width * width * 200, 16 * width * width),
        name="factor",
    )(flags, start, *children)


def blocks_kernel(
    step, ahead, send, place, roots, flags, keep, into, after, start, inverse, upper, *refs
):
    del after
    work, refs = refs[-1], refs[:-1]
    rounded, refs = (refs[-1], refs[:-1]) if send else (None, refs)
    out, refs = refs[-1], refs[:-1]
    later, children = (refs[0], refs[1:]) if ahead else (None, refs)
    blocks, width = start.shape[0], start.shape[1]
    for j in range(ahead):
        work[j] = later[j]
    work[ahead:] = start[...]
    for slot, child in enumerate(children):
        skipped = child.shape[0] - blocks
        for j in range(ahead):

            @pl.when(flags[step, slot, j + 1] > 0)
            def _(slot=slot, child=child, j=j):
                work[j] -= times_transposed(child[j + 1], child[0])

        for q in range(blocks):

            @pl.when(keep[step, slot, q] > 0)
            def _(slot=slot, child=child, q=q):
                work[ahead + into[step, slot, q]] -= times_transposed(
                    child[skipped + q], child[0]
                )

    solved = times_transposed(
        work[...].reshape((ahead + blocks) * width, width), inverse[...], HIGHEST
    )
    out[...] = solved[ahead * width :]
    if send:
        rounded[...] = solved.astype(BF16).reshape(ahead + blocks, width, width)

    @pl.when(place[1] == roots[step, 0])
    def _():
        out[:width, :] = upper[...].T


def panel_blocks(step, tables, after, start, later, send, inverse, upper, children):
    blocks, width, _ = start.shape
    ahead = 0 if later is None else later.shape[0]
    arrays = [start, inverse, upper] + ([later] if ahead else []) + list(children)
    out = [jax.ShapeDtypeStruct((blocks * width, width), F32)]
    if send:
        out.append(jax.ShapeDtypeStruct((ahead + blocks, width, width), BF16))
    return pl.pallas_call(
        functools.partial(blocks_kernel, step, ahead, send),
        in_specs=[smem()] * len(tables)
        + [pl.BlockSpec(memory_space=pl.ANY)]
        + [vmem()] * len(arrays),
        out_specs=[vmem()] * len(out),
        out_shape=out,
        scratch_shapes=[pltpu.VMEM((blocks + ahead, width, width), F32)],
        compiler_params=params(12),
        cost_estimate=cost(start.size * 2000, start.size * 16),
        name="panel_blocks",
    )(*tables, after, *arrays)


def local(targets, src_panels, live_counts, dest_owner, relative_map, diag_row, parent, chain_map):
    col_count = lax.axis_size("col")
    row_count = lax.axis_size("row")
    own = lax.axis_index("col")
    row_index = lax.axis_index("row")
    chips = col_count // 2
    src_count, _, width = src_panels.shape
    local_blocks = src_panels.shape[1] // width
    sections = targets.shape[0]
    targets = targets.reshape(sections, local_blocks, width, width)

    place = jnp.stack([own, row_index]).astype(jnp.int32)

    dealt = src_count // 2
    share = src_count // col_count
    facts = jnp.concatenate(
        [
            dest_owner.T,
            relative_map.transpose(1, 2, 0).reshape(sections * local_blocks, src_count),
            jnp.broadcast_to(live_counts, (1, src_count)),
        ],
        axis=0,
    ).astype(jnp.int32)
    facts = lax.all_gather(facts, "col", axis=0)
    counts = facts[:, -1, 0]
    columns_of = jnp.arange(col_count)
    offsets = jnp.sum(jnp.where(columns_of[None, :] < columns_of[:, None], counts[None, :], 0), axis=1)
    own_offset = jnp.sum(jnp.where(columns_of == own, offsets, 0))
    sent = (
        jnp.mod(columns_of - own_offset, col_count)[:, None]
        + col_count * jnp.arange(share)[None, :]
    ).reshape(-1)
    number = jnp.arange(dealt) * col_count + own
    source_column = jnp.sum(
        (offsets[None, :] <= number[:, None]).astype(jnp.int32), axis=1
    ) - 1
    index = number - jnp.sum(
        jnp.where(columns_of[None, :] == source_column[:, None], offsets[None, :], 0), axis=1
    )
    kept = source_column * share + index // col_count

    def deal(block):
        mixed = lax.all_to_all(pick(src_panels, sent, block, width), "col", 0, 0, tiled=True)
        return pick(mixed, kept, 0, width)

    first = deal(0)
    heads = lax.all_gather(first, "row", axis=0)
    second = jnp.stack([deal(q) for q in range(1, local_blocks)], axis=1)

    chain = lax.all_gather(chain_map[None], "row", axis=0, tiled=True)
    tab = functools.partial(jax.ShapeDtypeStruct, dtype=jnp.int32)
    roots, picks, ahead, keep, into = pl.pallas_call(
        functools.partial(tables_kernel, col_count),
        in_specs=[smem()] * 4,
        out_specs=[smem()] * 5,
        out_shape=[
            tab((sections, sections)),
            tab((sections, sections)),
            tab((sections, col_count, sections)),
            tab((sections, col_count, local_blocks)),
            tab((sections, col_count, local_blocks)),
        ],
        name="tables",
    )(place, diag_row, parent, chain)

    facts = facts.transpose(0, 2, 1).reshape(col_count * src_count, -1)
    facts = facts[source_column * src_count + index]
    dest = facts[:, :sections].T
    target_blocks = facts[:, sections:-1].T.reshape(sections, local_blocks, dealt)
    offset = jnp.bitwise_xor(dest, own)
    slots = (offset % 2) * chips + offset // 2
    source_root = jnp.sum(
        jnp.where(dest[:, :, None] == columns_of, diag_row[:, None, :], 0), axis=-1
    )
    table = jnp.concatenate([slots[:, None], source_root[:, None], target_blocks], axis=1)
    held = jnp.where(source_root == row_index, slots, 2 * chips)[:, None]

    other, mine = diagonal_sums(held, first, chips)
    _, total = scatter_sum(other, mine, col_count)

    def known(items):
        return jnp.stack([jnp.where(root == row_index, x, 0.0) for root, x in items])

    def share(x):
        return jnp.sum(lax.all_gather(x, "row", axis=0), axis=0)

    last = sections - 1
    soon = min(2, sections)
    items = [(roots[s, 0], targets[s, 0] - total[s]) for s in range(sections)]
    diagonals = share(known(items[:soon]))
    diagonals = [diagonals[s] for s in range(soon)]
    factored = factor(0, ahead, diagonals[0], [], col_count)

    sums = source_sums(table, first, second, heads, factored[0], chips)
    _, whole = scatter_sum(*sums, col_count)
    starts = targets - whole.reshape(targets.shape)

    later = [None] * sections
    pairs = [(s, j) for s in range(1, last) for j in range(1, sections - s)]
    group = known([(roots[s, j], starts[s][picks[s, j]]) for s, j in pairs] + items[soon:])
    whole = share(group)
    for s in range(1, last):
        at = pairs.index((s, 1))
        later[s] = whole[at : at + last - s]
    diagonals += [whole[len(pairs) + n] for n in range(sections - soon)]

    results, children = [], []
    tables = (place, roots, ahead, keep, into)
    for s in range(sections):
        upper, inverse = factored
        if s > 0:
            upper, inverse = factor(s, ahead, diagonals[s], children, col_count)
        made = panel_blocks(
            s, tables, group if s == 0 else place, starts[s], later[s], s < last, inverse, upper, children
        )
        results.append(made[0])
        if s < last:
            message = made[1]
            if s == 0:
                whole = lax.all_gather(message, "row", axis=0)
                needed = [whole[roots[0, j], picks[0, j]] for j in range(1, sections)]
                message = jnp.concatenate([jnp.stack(needed), message], axis=0)
            children = gather_columns(message, col_count)
    return jnp.stack(results)[:, None]


def solution(mesh):
    return jax.shard_map(
        local,
        mesh=mesh,
        in_specs=(
            P(None, "col", "row", None),
            P("col", "row", None),
            P("col"),
            P("col", None),
            P("col", None, "row"),
            P(),
            P(),
            P(None, None, "row"),
        ),
        out_specs=P(None, "col", "row", None),
        check_vma=False,
    )
```

time: 394 us -> 282 us (0.72)
  starting transfers between devices: 130 us -> 27.2 us
  waiting for transfers between devices: 154 us -> 78.8 us
  blocking collectives: 21.9 us -> 63.1 us
  between operations: 18 us -> 35.2 us
    all_gather x1 -> x2, waiting for transfers between devices: 96 us -> 5.23 us  [the longest x1 5.23 us: local(): heads = lax.all_gather(first, 'row', axis=0)]
    ppermute x24 -> x0, starting transfers between devices: 69 us -> none  [the longest x12 53.5 us: spread(): lax.ppermute(up, 'row', [(i, i + 1) for i in range(row_count - 1)])]
    all_gather x0 -> x3, blocking collectives: none -> 49.7 us  [the longest x1 23.1 us: share(): return jnp.sum(lax.all_gather(x, 'row', axis=0), axis=0)]
    ppermute x58 -> x29, starting transfers between devices: 61.3 us -> 19.7 us  [swap(): return lax.ppermute(x, axis, [(i, i ^ mask) for i in range(size)])]
    all_to_all x0 -> x2, waiting for transfers between devices: none -> 26.3 us  [deal(): lax.all_to_all(pick(src_panels, sent, block, width), 'col', 0, 0, tiled=T...]
    ppermute x24 -> x0, waiting for transfers between devices: 26.1 us -> none  [the longest x12 14.1 us: spread(): lax.ppermute(down, 'row', [(i + 1, i) for i in range(row_count - 1)])]
    ppermute x58 -> x29, waiting for transfers between devices: 31.4 us -> 47.3 us  [swap(): return lax.ppermute(x, axis, [(i, i ^ mask) for i in range(size)])]
    all_gather x1, blocking collectives: 21.9 us -> 13.4 us  [local(): chain = lax.all_gather(chain_map[None], 'row', axis=0, tiled=True)]
  transfers between devices with their start and end apart: 83 -> 33, of which waited for: 26 -> 23; matrix products, arithmetic and copies ran while one was open for 3% -> 3% of each run, Pallas kernels for 10% -> 8%
where the time goes in v2:
time: 282 us; the launch traced here: 280 us
  waiting for transfers between devices  78.8 us (28%)
  blocking collectives  63.1 us (22%)
  Pallas kernels  49.5 us (18%)
  between operations  35.2 us (12%)
  starting transfers between devices  27.2 us (10%)
  local copies, waits for them, and re-layouts  15.5 us (5%)
  other arithmetic  11 us (4%)
    ppermute x29, waiting for transfers between devices, swap(): return lax.ppermute(x, axis, [(i, i ^ mask) for i in range(size)])  47.3 us
    all_to_all x2, waiting for transfers between devices, deal(): lax.all_to_all(pick(src_panels, sent, block, width), 'col', 0, 0, tiled=T...  26.3 us
    all_gather x1, blocking collectives, share(): return jnp.sum(lax.all_gather(x, 'row', axis=0), axis=0)  23.1 us
    pallas_call x4, Pallas kernels, factor(): pl.pallas_call(functools.partial(factor_kernel, step, col_count), in_spec...  20.7 us
    ppermute x29, starting transfers between devices, swap(): return lax.ppermute(x, axis, [(i, i ^ mask) for i in range(size)])  19.7 us
    all_gather x1, blocking collectives, local(): whole = lax.all_gather(message, 'row', axis=0)  15.9 us
    all_gather x1, blocking collectives, local(): chain = lax.all_gather(chain_map[None], 'row', axis=0, tiled=True)  13.4 us
    all_gather x1, blocking collectives, local(): facts = lax.all_gather(facts, 'col', axis=0)  10.7 us
  transfers between devices with their start and end apart: 33, of which 23 were waited for; matrix products, arithmetic and copies ran while one was open for 3% of the time, Pallas kernels for 8%

profile of v2, /device:TPU:0, one launch (start us, length us, event | category | flops | bytes accessed | tf_op | source)
XLA Modules:
  0.0 280.3 jit_solution(7325465184559385005)
XLA Ops:
  8.0 10.7 %all-gather.6 = s32[8,13,64]{2,1,0:T(8,128)S(1)} all-gather(s32[1,13,64]{2,1,0:T(8,128)S(1)} %add_bitcast_fusion), channel_id=3, replica_groups=mesh['col'=8,'row'=4] {'col'}, dimensions={0}, use_global_device_ids=true | all-gather | bytes 29952 | tf_op jit(solution)/shard_map/all_gather | solution.py:394
  24.9 3.6 %all-to-all-start = ((bf16[64,128,128]{2,1,0:T(8,128)(2,1)}), bf16[64,128,128]{2,1,0:T(8,128)(2,1)S(1)}, u32[]{:S(2)}, u32[]{:S(2)}) async-start(bf16[64,128,128]{2,1,0:T(8,128)(2,1)} %pick.4), calls=%async_computation | async-start | bytes 4194304 | tf_op jit(solution)/shard_map/all_to_all | solution.py:413
  28.7 26.3 %all-to-all-done.source = bf16[64,128,128]{2,1,0:T(8,128)(2,1)S(1)} async-done(((bf16[64,128,128]{2,1,0:T(8,128)(2,1)}), bf16[64,128,128]{2,1,0:T(8,128)(2,1)S(1)}, u32[]{:S(2)}, u32[]{:S(2)}) %all-to-all-start) | async-done | bytes 2097184 | tf_op jit(solution)/shard_map/all_to_all | solution.py:413
  61.0 3.8 %all-to-all-start.1 = ((bf16[64,128,128]{2,1,0:T(8,128)(2,1)}), bf16[64,128,128]{2,1,0:T(8,128)(2,1)S(1)}, u32[]{:S(2)}, u32[]{:S(2)}) async-start(bf16[64,128,128]{2,1,0:T(8,128)(2,1)} %pick.6), calls=%async_computation.1 | async-start | bytes 4194304 | tf_op jit(solution)/shard_map/all_to_all | solution.py:413
  66.0 5.1 %diagonal_sums.1 = (f32[4,4,128,128]{3,2,1,0:T(8,128)}, f32[4,4,128,128]{3,2,1,0:T(8,128)S(1)}) custom-call(s32[4,1,32]{2,1,0:T(1,128)S(1)} %copy.62.table, bf16[32,128,128]{2,1,0:T(8,128)(2,1)} %pick.5.heads.first), custom_call_target="tpu_custom_call" | custom-call | flops 268435456 | bytes 2097152 | tf_op jit(solution)/shard_map/diagonal_sums/pallas_call | solution.py:168
  71.4 13.4 %all-gather = s32[12,8,2]{1,2,0:T(2,128)S(1)} all-gather(s32[3,8,2]{1,2,0:T(2,128)S(1)} %copy-done.13), channel_id=2, replica_groups=mesh['col'=8,'row'=4] {'row'}, dimensions={0}, use_global_device_ids=true | all-gather | bytes 960 | tf_op jit(solution)/shard_map/all_gather | solution.py:420
  86.2 3.2 %tables.1 = (s32[4,4]{1,0:T(4,128)}, s32[4,4]{1,0:T(4,128)}, s32[4,8,4]{2,1,0:T(8,128)}, s32[4,8,2]{2,1,0:T(8,128)}, s32[4,8,2]{2,1,0:T(8,128)}) custom-call(s32[2]{0:T(128)} %pad_add_fusion.1.place.after, s32[4,8]{1,0:T(4,128)} %diag.1, s32[3,8]{1,0:T(4,128)} %parent.1, s32[4,3,8,2]{3,2,1,0:T(8,128)} %bitcast.159), custom_call_target="tpu_custom_call" | custom-call | tf_op jit(solution)/shard_map/tables/pallas_call | solution.py:422
  100.0 4.6 %collective-permute-done.1 = f32[4,128,128]{2,1,0:T(8,128)} collective-permute-done((f32[4,128,128]{2,1,0:T(8,128)}, f32[4,128,128]{2,1,0:T(8,128)}, u32[]{:S(2)}, u32[]{:S(2)}) %collective-permute-start.1) | collective-permute-done | bytes 262176 | tf_op jit(solution)/shard_map/ppermute | solution.py:49
  104.6 4.1 %collective-permute-done.3 = f32[4,128,128]{2,1,0:T(8,128)} collective-permute-done((f32[4,128,128]{2,1,0:T(8,128)}, f32[4,128,128]{2,1,0:T(8,128)}, u32[]{:S(2)}, u32[]{:S(2)}) %collective-permute-start.3) | collective-permute-done | bytes 262176 | tf_op jit(solution)/shard_map/ppermute | solution.py:49
  112.0 23.1 %all-gather.3 = f32[8,128,128]{2,1,0:T(8,128)S(1)} all-gather(f32[2,128,128]{2,1,0:T(8,128)S(1)} %pad_maximum_fusion.1), channel_id=5, replica_groups=mesh['col'=8,'row'=4] {'row'}, dimensions={0}, use_global_device_ids=true | all-gather | bytes 655360 | tf_op jit(solution)/shard_map/all_gather | solution.py:455
  135.2 5.0 %factor.4 = (f32[128,128]{1,0:T(8,128)S(1)}, f32[128,128]{1,0:T(8,128)S(1)}) custom-call(s32[4,8,4]{2,1,0:T(8,128)S(1)} %copy-done.5, f32[128,128]{1,0:T(8,128)S(1)} %get-tuple-element.72.start), custom_call_target="tpu_custom_call" | custom-call | flops 419430400 | bytes 262144 | tf_op jit(solution)/shard_map/factor/pallas_call | solution.py:298
  140.2 5.2 %all-gather.10.cloned.1.call-done = bf16[128,128,128]{2,1,0:T(8,128)(2,1)} async-done(((bf16[32,128,128]{2,1,0:T(8,128)(2,1)}), bf16[128,128,128]{2,1,0:T(8,128)(2,1)}) %all-gather.10.cloned.1.call-update) | async-done | bytes 4194320 | tf_op jit(solution)/shard_map/all_gather | solution.py:417
  147.6 5.7 %source_sums.1 = (f32[4,8,128,128]{3,2,1,0:T(8,128)S(1)}, f32[4,8,128,128]{3,2,1,0:T(8,128)S(1)}) custom-call(s32[4,4,32]{2,1,0:T(4,128)S(1)} %pad_add_fusion.table, bf16[32,128,128]{2,1,0:T(8,128)(2,1)} %pick.5.heads.first, bf16[32,1,128,128]{3,2,1,0:T(8,128)(2,1)S(1)} %bitcast.143, bf16[4,32,128,128]{3,2,1,0:T(8,128)(2,1)S(1)} %bitcast.144, ...), custom_call_target="tpu_custom_call" | custom-call | flops 1073741824 | bytes 6291456 | tf_op jit(solution)/shard_map/source_sums/pallas_call | solution.py:224
  153.4 4.1 %collective-permute-done.4 = f32[4,8,128,128]{3,2,1,0:T(8,128)S(1)} collective-permute-done((f32[4,8,128,128]{3,2,1,0:T(8,128)S(1)}, f32[4,8,128,128]{3,2,1,0:T(8,128)S(1)}, u32[]{:S(2)}, u32[]{:S(2)}) %collective-permute-start.4) | collective-permute-done | bytes 2097184 | tf_op jit(solution)/shard_map/ppermute | solution.py:49
  171.3 2.8 %collective-permute-done.5 = f32[8,128,128]{2,1,0:T(8,128)} collective-permute-done((f32[8,128,128]{2,1,0:T(8,128)}, f32[8,128,128]{2,1,0:T(8,128)}, u32[]{:S(2)}, u32[]{:S(2)}) %collective-permute-start.5) | collective-permute-done | bytes 524320 | tf_op jit(solution)/shard_map/ppermute | solution.py:49
  174.1 11.5 %collective-permute-done.7 = f32[8,128,128]{2,1,0:T(8,128)} collective-permute-done((f32[8,128,128]{2,1,0:T(8,128)}, f32[8,128,128]{2,1,0:T(8,128)}, u32[]{:S(2)}, u32[]{:S(2)}) %collective-permute-start.7) | collective-permute-done | bytes 524320 | tf_op jit(solution)/shard_map/ppermute | solution.py:49
  202.9 15.9 %all-gather.4 = bf16[8,128,128]{2,1,0:T(8,128)(2,1)S(1)} all-gather(bf16[2,128,128]{2,1,0:T(8,128)(2,1)S(1)} %get-tuple-element.40), channel_id=6, replica_groups=mesh['col'=8,'row'=4] {'row'}, dimensions={0}, use_global_device_ids=true | all-gather | bytes 327680 | tf_op jit(solution)/shard_map/all_gather | solution.py:490
  222.4 2.8 %collective-permute-done.10.refs_3_.refs_4_ = bf16[5,128,128]{2,1,0:T(8,128)(2,1)S(1)} collective-permute-done((bf16[5,128,128]{2,1,0:T(8,128)(2,1)S(1)}, bf16[5,128,128]{2,1,0:T(8,128)(2,1)S(1)}, u32[]{:S(2)}, u32[]{:S(2)}) %collective-permute-start.10) | collective-permute-done | bytes 163872 | tf_op jit(solution)/shard_map/ppermute | solution.py:49
  228.5 5.2 %factor.5 = (f32[128,128]{1,0:T(8,128)S(1)}, f32[128,128]{1,0:T(8,128)S(1)}) custom-call(s32[4,8,4]{2,1,0:T(8,128)S(1)} %copy-done.5, f32[128,128]{1,0:T(8,128)S(1)} %get-tuple-element.71.start, bf16[5,128,128]{2,1,0:T(8,128)(2,1)S(1)} %pad_maximum_fusion.refs_0_.refs_1_, bf16[5,128,128]{2,1,0:T(8,128)(2,1)S(1)} %collective-permute-done.8.refs_1_.refs_2_, ...), custom_call_target="tpu_custom_call" | custom-call | flops 419430400 | bytes 262144 | tf_op jit(solution)/shard_map/factor/pallas_call | solution.py:298
  241.3 3.2 %collective-permute-done.17.refs_3_.refs_4_ = bf16[4,128,128]{2,1,0:T(8,128)(2,1)S(1)} collective-permute-done((bf16[4,128,128]{2,1,0:T(8,128)(2,1)S(1)}, bf16[4,128,128]{2,1,0:T(8,128)(2,1)S(1)}, u32[]{:S(2)}, u32[]{:S(2)}) %collective-permute-start.17) | collective-permute-done | bytes 131104 | tf_op jit(solution)/shard_map/ppermute | solution.py:49
  244.6 2.6 collective-permute-done.16.refs_2_.refs_3_
  248.8 5.3 %factor.6 = (f32[128,128]{1,0:T(8,128)S(1)}, f32[128,128]{1,0:T(8,128)S(1)}) custom-call(s32[4,8,4]{2,1,0:T(8,128)S(1)} %copy-done.5, f32[128,128]{1,0:T(8,128)S(1)} %get-tuple-element.67.start, bf16[4,128,128]{2,1,0:T(8,128)(2,1)S(1)} %get-tuple-element.44.refs_0_.refs_1_, bf16[4,128,128]{2,1,0:T(8,128)(2,1)S(1)} %collective-permute-done.15.refs_1_.refs_2_, ...), custom_call_target="tpu_custom_call" | custom-call | flops 419430400 | bytes 262144 | tf_op jit(solution)/shard_map/factor/pallas_call | solution.py:298
  254.1 2.5 panel_blocks.6
  265.4 5.3 %factor.7 = (f32[128,128]{1,0:T(8,128)S(1)}, f32[128,128]{1,0:T(8,128)S(1)}) custom-call(s32[4,8,4]{2,1,0:T(8,128)S(1)} %copy-done.5, f32[128,128]{1,0:T(8,128)S(1)} %get-tuple-element.66.start, bf16[3,128,128]{2,1,0:T(8,128)(2,1)S(1)} %get-tuple-element.48.refs_0_, bf16[3,128,128]{2,1,0:T(8,128)(2,1)S(1)} %collective-permute-done.22.refs_1_, ...), custom_call_target="tpu_custom_call" | custom-call | flops 419430400 | bytes 262144 | tf_op jit(solution)/shard_map/factor/pallas_call | solution.py:298
  (144 shorter events, 70.0 us)
Async XLA Ops:
  24.9 30.2 %all-to-all-start = ((bf16[64,128,128]{2,1,0:T(8,128)(2,1)}), bf16[64,128,128]{2,1,0:T(8,128)(2,1)S(1)}, u32[]{:S(2)}, u32[]{:S(2)}) async-start(bf16[64,128,128]{2,1,0:T(8,128)(2,1)} %pick.4), calls=%async_computation | async-start | bytes 4194304 | tf_op jit(solution)/shard_map/all_to_all | solution.py:413
  28.5 116.9 %all-gather.10.cloned.1.call-start = ((), (), s32[]{:S(2)}) async-start(), calls=%async_computation.2 | async-start | bytes 5242880 | tf_op jit(solution)/shard_map/all_gather | solution.py:417
  61.0 38.4 %all-to-all-start.1 = ((bf16[64,128,128]{2,1,0:T(8,128)(2,1)}), bf16[64,128,128]{2,1,0:T(8,128)(2,1)S(1)}, u32[]{:S(2)}, u32[]{:S(2)}) async-start(bf16[64,128,128]{2,1,0:T(8,128)(2,1)} %pick.6), calls=%async_computation.1 | async-start | bytes 4194304 | tf_op jit(solution)/shard_map/all_to_all | solution.py:413
  64.8 168.9 %all-gather.12.cloned.1.call-start = ((), (), s32[]{:S(2)}) async-start(), calls=%async_computation.3 | async-start | bytes 1638400 | tf_op jit(solution)/shard_map/all_gather | solution.py:455
  71.1 21.3 %collective-permute-start = (f32[4,4,128,128]{3,2,1,0:T(8,128)}, f32[4,4,128,128]{3,2,1,0:T(8,128)}, u32[]{:S(2)}, u32[]{:S(2)}) collective-permute-start(f32[4,4,128,128]{3,2,1,0:T(8,128)} %get-tuple-element.33), channel_id=1, source_target_pairs={{0,4},{4,0},{8,12},{12,8},{16,20},{20,16},{24,28},{28,24},{1,5},{5... | collective-permute-start | bytes 3145736 | tf_op jit(solution)/shard_map/ppermute | solution.py:49
  95.6 9.0 %collective-permute-start.1 = (f32[4,128,128]{2,1,0:T(8,128)}, f32[4,128,128]{2,1,0:T(8,128)}, u32[]{:S(2)}, u32[]{:S(2)}) collective-permute-start(f32[4,128,128]{2,1,0:T(8,128)} %get-tuple-element.54), channel_id=1, source_target_pairs={{0,8},{4,12},{8,0},{12,4},{16,24},{20,28},{24,16},{28,20},{1,9},{5... | collective-permute-start | bytes 786440 | tf_op jit(solution)/shard_map/ppermute | solution.py:49
  97.3 11.4 %collective-permute-start.3 = (f32[4,128,128]{2,1,0:T(8,128)}, f32[4,128,128]{2,1,0:T(8,128)}, u32[]{:S(2)}, u32[]{:S(2)}) collective-permute-start(f32[4,128,128]{2,1,0:T(8,128)} %get-tuple-element.55), channel_id=1, source_target_pairs={{0,24},{4,28},{8,16},{12,20},{16,8},{20,12},{24,0},{28,4},{1,25},{... | collective-permute-start | bytes 786440 | tf_op jit(solution)/shard_map/ppermute | solution.py:49
  98.8 11.1 %collective-permute-start.2 = (f32[4,128,128]{2,1,0:T(8,128)S(1)}, f32[4,128,128]{2,1,0:T(8,128)}, u32[]{:S(2)}, u32[]{:S(2)}) collective-permute-start(f32[4,128,128]{2,1,0:T(8,128)S(1)} %get-tuple-element.56), channel_id=1, source_target_pairs={{0,16},{4,20},{8,24},{12,28},{16,0},{20,4},{24,8},{28,12},{1,17},{... | collective-permute-start | bytes 786440 | tf_op jit(solution)/shard_map/ppermute | solution.py:49
  153.3 4.2 %collective-permute-start.4 = (f32[4,8,128,128]{3,2,1,0:T(8,128)S(1)}, f32[4,8,128,128]{3,2,1,0:T(8,128)S(1)}, u32[]{:S(2)}, u32[]{:S(2)}) collective-permute-start(f32[4,8,128,128]{3,2,1,0:T(8,128)S(1)} %get-tuple-element.36), channel_id=1, source_target_pairs={{0,4},{4,0},{8,12},{12,8},{16,20},{20,16},{24,28},{28,24},{1,5},{5... | collective-permute-start | bytes 6291464 | tf_op jit(solution)/shard_map/ppermute | solution.py:49
  159.0 15.1 %collective-permute-start.5 = (f32[8,128,128]{2,1,0:T(8,128)}, f32[8,128,128]{2,1,0:T(8,128)}, u32[]{:S(2)}, u32[]{:S(2)}) collective-permute-start(f32[8,128,128]{2,1,0:T(8,128)} %get-tuple-element.51), channel_id=1, source_target_pairs={{0,8},{4,12},{8,0},{12,4},{16,24},{20,28},{24,16},{28,20},{1,9},{5... | collective-permute-start | bytes 1572872 | tf_op jit(solution)/shard_map/ppermute | solution.py:49
  160.5 25.1 %collective-permute-start.7 = (f32[8,128,128]{2,1,0:T(8,128)}, f32[8,128,128]{2,1,0:T(8,128)}, u32[]{:S(2)}, u32[]{:S(2)}) collective-permute-start(f32[8,128,128]{2,1,0:T(8,128)} %get-tuple-element.52), channel_id=1, source_target_pairs={{0,24},{4,28},{8,16},{12,20},{16,8},{20,12},{24,0},{28,4},{1,25},{... | collective-permute-start | bytes 1572872 | tf_op jit(solution)/shard_map/ppermute | solution.py:49
  162.0 25.0 %collective-permute-start.6 = (f32[8,128,128]{2,1,0:T(8,128)}, f32[8,128,128]{2,1,0:T(8,128)}, u32[]{:S(2)}, u32[]{:S(2)}) collective-permute-start(f32[8,128,128]{2,1,0:T(8,128)} %get-tuple-element.53), channel_id=1, source_target_pairs={{0,16},{4,20},{8,24},{12,28},{16,0},{20,4},{24,8},{28,12},{1,17},{... | collective-permute-start | bytes 1572872 | tf_op jit(solution)/shard_map/ppermute | solution.py:49
  218.8 6.4 %collective-permute-start.10 = (bf16[5,128,128]{2,1,0:T(8,128)(2,1)S(1)}, bf16[5,128,128]{2,1,0:T(8,128)(2,1)S(1)}, u32[]{:S(2)}, u32[]{:S(2)}) collective-permute-start(bf16[5,128,128]{2,1,0:T(8,128)(2,1)S(1)} %pad_maximum_fusion.refs_0_.refs_1_), channel_id=1, source_target_pairs={{0,24},{4,28},{8,16},{12,20},{16,8},{20,12},{24,0},{28,4},{1,25},{... | collective-permute-start | bytes 491528 | tf_op jit(solution)/shard_map/ppermute | solution.py:49
  220.3 6.6 %collective-permute-start.9 = (bf16[5,128,128]{2,1,0:T(8,128)(2,1)S(1)}, bf16[5,128,128]{2,1,0:T(8,128)(2,1)S(1)}, u32[]{:S(2)}, u32[]{:S(2)}) collective-permute-start(bf16[5,128,128]{2,1,0:T(8,128)(2,1)S(1)} %pad_maximum_fusion.refs_0_.refs_1_), channel_id=1, source_target_pairs={{0,16},{4,20},{8,24},{12,28},{16,0},{20,4},{24,8},{28,12},{1,17},{... | collective-permute-start | bytes 491528 | tf_op jit(solution)/shard_map/ppermute | solution.py:49
  221.8 5.3 %collective-permute-start.8 = (bf16[5,128,128]{2,1,0:T(8,128)(2,1)S(1)}, bf16[5,128,128]{2,1,0:T(8,128)(2,1)S(1)}, u32[]{:S(2)}, u32[]{:S(2)}) collective-permute-start(bf16[5,128,128]{2,1,0:T(8,128)(2,1)S(1)} %pad_maximum_fusion.refs_0_.refs_1_), channel_id=1, source_target_pairs={{0,8},{4,12},{8,0},{12,4},{16,24},{20,28},{24,16},{28,20},{1,9},{5... | collective-permute-start | bytes 491528 | tf_op jit(solution)/shard_map/ppermute | solution.py:49
  222.4 5.0 %collective-permute-start.11 = (bf16[5,128,128]{2,1,0:T(8,128)(2,1)S(1)}, bf16[5,128,128]{2,1,0:T(8,128)(2,1)S(1)}, u32[]{:S(2)}, u32[]{:S(2)}) collective-permute-start(bf16[5,128,128]{2,1,0:T(8,128)(2,1)S(1)} %pad_maximum_fusion.refs_0_.refs_1_), channel_id=1, source_target_pairs={{0,4},{4,0},{8,12},{12,8},{16,20},{20,16},{24,28},{28,24},{1,5},{5... | collective-permute-start | bytes 491528 | tf_op jit(solution)/shard_map/ppermute | solution.py:49
  237.2 7.3 %collective-permute-start.17 = (bf16[4,128,128]{2,1,0:T(8,128)(2,1)S(1)}, bf16[4,128,128]{2,1,0:T(8,128)(2,1)S(1)}, u32[]{:S(2)}, u32[]{:S(2)}) collective-permute-start(bf16[4,128,128]{2,1,0:T(8,128)(2,1)S(1)} %get-tuple-element.44.refs_0_.refs_1_), channel_id=1, source_target_pairs={{0,24},{4,28},{8,16},{12,20},{16,8},{20,12},{24,0},{28,4},{1,25},{... | collective-permute-start | bytes 393224 | tf_op jit(solution)/shard_map/ppermute | solution.py:49
  238.7 8.6 %collective-permute-start.16 = (bf16[4,128,128]{2,1,0:T(8,128)(2,1)S(1)}, bf16[4,128,128]{2,1,0:T(8,128)(2,1)S(1)}, u32[]{:S(2)}, u32[]{:S(2)}) collective-permute-start(bf16[4,128,128]{2,1,0:T(8,128)(2,1)S(1)} %get-tuple-element.44.refs_0_.refs_1_), channel_id=1, source_target_pairs={{0,16},{4,20},{8,24},{12,28},{16,0},{20,4},{24,8},{28,12},{1,17},{... | collective-permute-start | bytes 393224 | tf_op jit(solution)/shard_map/ppermute | solution.py:49
  240.3 7.1 %collective-permute-start.15 = (bf16[4,128,128]{2,1,0:T(8,128)(2,1)S(1)}, bf16[4,128,128]{2,1,0:T(8,128)(2,1)S(1)}, u32[]{:S(2)}, u32[]{:S(2)}) collective-permute-start(bf16[4,128,128]{2,1,0:T(8,128)(2,1)S(1)} %get-tuple-element.44.refs_0_.refs_1_), channel_id=1, source_target_pairs={{0,8},{4,12},{8,0},{12,4},{16,24},{20,28},{24,16},{28,20},{1,9},{5... | collective-permute-start | bytes 393224 | tf_op jit(solution)/shard_map/ppermute | solution.py:49
  240.7 7.0 %collective-permute-start.18 = (bf16[4,128,128]{2,1,0:T(8,128)(2,1)S(1)}, bf16[4,128,128]{2,1,0:T(8,128)(2,1)S(1)}, u32[]{:S(2)}, u32[]{:S(2)}) collective-permute-start(bf16[4,128,128]{2,1,0:T(8,128)(2,1)S(1)} %get-tuple-element.44.refs_0_.refs_1_), channel_id=1, source_target_pairs={{0,4},{4,0},{8,12},{12,8},{16,20},{20,16},{24,28},{28,24},{1,5},{5... | collective-permute-start | bytes 393224 | tf_op jit(solution)/shard_map/ppermute | solution.py:49
  256.6 5.9 %collective-permute-start.24 = (bf16[3,128,128]{2,1,0:T(8,128)(2,1)S(1)}, bf16[3,128,128]{2,1,0:T(8,128)(2,1)S(1)}, u32[]{:S(2)}, u32[]{:S(2)}) collective-permute-start(bf16[3,128,128]{2,1,0:T(8,128)(2,1)S(1)} %get-tuple-element.48.refs_0_), channel_id=1, source_target_pairs={{0,24},{4,28},{8,16},{12,20},{16,8},{20,12},{24,0},{28,4},{1,25},{... | collective-permute-start | bytes 294920 | tf_op jit(solution)/shard_map/ppermute | solution.py:49
  257.7 6.1 %collective-permute-start.23 = (bf16[3,128,128]{2,1,0:T(8,128)(2,1)S(1)}, bf16[3,128,128]{2,1,0:T(8,128)(2,1)S(1)}, u32[]{:S(2)}, u32[]{:S(2)}) collective-permute-start(bf16[3,128,128]{2,1,0:T(8,128)(2,1)S(1)} %get-tuple-element.48.refs_0_), channel_id=1, source_target_pairs={{0,16},{4,20},{8,24},{12,28},{16,0},{20,4},{24,8},{28,12},{1,17},{... | collective-permute-start | bytes 294920 | tf_op jit(solution)/shard_map/ppermute | solution.py:49
  259.2 4.9 %collective-permute-start.22 = (bf16[3,128,128]{2,1,0:T(8,128)(2,1)S(1)}, bf16[3,128,128]{2,1,0:T(8,128)(2,1)S(1)}, u32[]{:S(2)}, u32[]{:S(2)}) collective-permute-start(bf16[3,128,128]{2,1,0:T(8,128)(2,1)S(1)} %get-tuple-element.48.refs_0_), channel_id=1, source_target_pairs={{0,8},{4,12},{8,0},{12,4},{16,24},{20,28},{24,16},{28,20},{1,9},{5... | collective-permute-start | bytes 294920 | tf_op jit(solution)/shard_map/ppermute | solution.py:49
  260.1 4.2 %collective-permute-start.25 = (bf16[3,128,128]{2,1,0:T(8,128)(2,1)S(1)}, bf16[3,128,128]{2,1,0:T(8,128)(2,1)S(1)}, u32[]{:S(2)}, u32[]{:S(2)}) collective-permute-start(bf16[3,128,128]{2,1,0:T(8,128)(2,1)S(1)} %get-tuple-element.48.refs_0_), channel_id=1, source_target_pairs={{0,4},{4,0},{8,12},{12,8},{16,20},{20,16},{24,28},{28,24},{1,5},{5... | collective-permute-start | bytes 294920 | tf_op jit(solution)/shard_map/ppermute | solution.py:49
  (23 other events, 151.6 us)
Sparse Core Ops, SparseCore 0:
  56.8 88.5 all-gather.9
  189.6 34.5 all-gather.11

commit v3 on v2

--- a/solution.py
+++ b/solution.py
@@ -55,18 +55,53 @@
     return same + [swap(y, "col", col_count, 1) for y in same]
 
 
-def scatter_sum(other_half, own_half, col_count):
-    chips = col_count // 2
-    halves = own_half + swap(other_half, "col", col_count, 1)
+def halves_kernel(own, other, after, *outs):
+    del after
+    for m, out in enumerate(outs):
+        out[...] = own[m] + other[m]
+
+
+def scatter_sum(other_half, own_half, after, col_count):
+    chips, *shape = own_half.shape
+    swapped = swap(other_half, "col", col_count, 1)
+    halves = pl.pallas_call(
+        halves_kernel,
+        in_specs=[vmem(), vmem(), pl.BlockSpec(memory_space=pl.ANY)],
+        out_specs=[vmem()] * chips,
+        out_shape=[jax.ShapeDtypeStruct(shape, F32)] * chips,
+        compiler_params=params(12 * own_half.size // MIB + 4),
+        cost_estimate=cost(own_half.size, 12 * own_half.size),
+        name="halves",
+    )(own_half, swapped, after)
     whole = halves[0]
     for m in range(1, chips):
         whole = whole + swap(halves[m], "col", col_count, 2 * m)
-    return halves, whole
-
-
-def tables_kernel(col_count, place, diag, parent, chain, roots, picks, ahead, keep, into):
-    sections = diag.shape[0]
-    local_blocks = chain.shape[3]
+    return whole, halves[0]
+
+
+class Tables:
+    def __init__(self, sections, col_count, blocks):
+        self.sections, self.col_count, self.blocks = sections, col_count, blocks
+        grid, kids = sections * sections, sections * col_count
+        self.starts = {"mine": 0, "roots": grid}
+        self.starts["picks"] = self.starts["roots"] + grid
+        self.starts["ahead"] = self.starts["picks"] + grid
+        self.starts["keep"] = self.starts["ahead"] + kids * sections
+        self.starts["into"] = self.starts["keep"] + kids * blocks
+        self.size = self.starts["into"] + kids * blocks
+
+    def at(self, name, s, *rest):
+        place = s
+        widths = {"ahead": (self.col_count, self.sections)}.get(name, (self.col_count, self.blocks))
+        if name in ("mine", "roots", "picks"):
+            widths = (self.sections,)
+        for index, width in zip(rest, widths):
+            place = place * width + index
+        return self.starts[name] + place
+
+
+def tables_kernel(layout, place, diag, parent, chain, out):
+    sections, col_count, local_blocks = layout.sections, layout.col_count, layout.blocks
     chips = col_count // 2
     own = place[0]
     row = place[1]
@@ -91,30 +126,29 @@
 
     for s in range(sections):
         columns = path(s, own)
-        for j in range(sections):
-            if j < sections - s:
-                roots[s, j] = diag[s + j, columns[j]]
-                picks[s, j] = block_of(s, columns, j)
-            else:
-                roots[s, j] = 0
-                picks[s, j] = 0
+        for j in range(sections - s):
+            group = diag[s + j, columns[j]]
+            out[layout.at("mine", s, j)] = jnp.where(group == row, 1, 0)
+            out[layout.at("roots", s, j)] = group
+            out[layout.at("picks", s, j)] = block_of(s, columns, j)
     for s in range(1, sections):
         for slot in range(col_count):
             child = slot_column(slot, chips, own)
             hit = parent[s - 1, child] == own
             columns = path(s - 1, child)
-            for j in range(sections):
-                if j < sections - s:
-                    block = block_of(s - 1, columns, j + 1)
-                    group = diag[s + j, columns[j + 1]]
-                    left_out = (block == 0) & (group == diag[s - 1, child])
-                    ahead[s, slot, j] = jnp.where(hit & jnp.logical_not(left_out), 1, 0)
-                else:
-                    ahead[s, slot, j] = 0
+            for j in range(sections - s):
+                block = block_of(s - 1, columns, j + 1)
+                group = diag[s + j, columns[j + 1]]
+                left_out = (block == 0) & (group == diag[s - 1, child])
+                out[layout.at("ahead", s, slot, j)] = jnp.where(
+                    hit & jnp.logical_not(left_out), 1, 0
+                )
             for q in range(local_blocks):
                 left_out = (diag[s - 1, child] == row) & (q == 0)
-                keep[s, slot, q] = jnp.where(hit & jnp.logical_not(left_out), 1, 0)
-                into[s, slot, q] = chain[row, s - 1, child, q]
+                out[layout.at("keep", s, slot, q)] = jnp.where(
+                    hit & jnp.logical_not(left_out), 1, 0
+                )
+                out[layout.at("into", s, slot, q)] = chain[row, s - 1, child, q]
 
 
 def pick_kernel(index, source, out):
@@ -133,10 +167,30 @@
             out_specs=pl.BlockSpec((count, rows, width), lambda g, a: (0, 0, 0)),
         ),
         out_shape=jax.ShapeDtypeStruct((count, rows, width), source.dtype),
-        compiler_params=params(12),
+        compiler_params=params(48),
         cost_estimate=cost(0, 4 * count * rows * width),
         name="pick",
     )(index, source)
+
+
+def sum_kernel(after, x, out):
+    del after
+    total = x[0]
+    for r in range(1, x.shape[0]):
+        total = total + x[r]
+    out[...] = total
+
+
+def sum_rows(x, after):
+    return pl.pallas_call(
+        sum_kernel,
+        in_specs=[pl.BlockSpec(memory_space=pl.ANY), vmem()],
+        out_specs=vmem(),
+        out_shape=jax.ShapeDtypeStruct(x.shape[1:], x.dtype),
+        compiler_params=params(8),
+        cost_estimate=cost(x.size, 4 * x.size),
+        name="sum_rows",
+    )(after, x)
 
 
 def diagonal_kernel(table, heads, other, own, total):
@@ -181,8 +235,9 @@
     )(table, heads)
 
 
-def source_kernel(table, first, second, heads, after, other, own, total):
+def source_kernel(soon, table, first, second, heads, after, other, own, *refs):
     del after
+    rest, total = refs[:-1], refs[-1]
     g = pl.program_id(0)
     chunk, width, _ = first.shape
     chips = own.shape[0]
@@ -209,20 +264,24 @@
 
     @pl.when(g == pl.num_programs(0) - 1)
     def _():
-        other[...] = total[chips : 2 * chips]
-        own[...] = total[:chips]
-
-
-def source_sums(table, first, second, heads, after, chips):
+        other[...] = total[chips : 2 * chips, : soon * blocks]
+        own[...] = total[:chips, : soon * blocks]
+        if rest:
+            rest[0][...] = total[chips : 2 * chips, soon * blocks :]
+            rest[1][...] = total[:chips, soon * blocks :]
+
+
+def source_sums(soon, table, first, second, heads, after, chips):
     count, width, _ = first.shape
     blocks = 1 + second.shape[1]
     sections = table.shape[0]
     chunk = min(CHUNK, count)
-    half = (chips, sections * blocks, width, width)
-    out = jax.ShapeDtypeStruct(half, F32)
+    shapes = [(chips, soon * blocks, width, width)] * 2
+    if soon < sections:
+        shapes += [(chips, (sections - soon) * blocks, width, width)] * 2
     size = 4 * chips * sections * blocks * width * width
     return pl.pallas_call(
-        source_kernel,
+        functools.partial(source_kernel, soon),
         grid_spec=pltpu.PrefetchScalarGridSpec(
             num_scalar_prefetch=1,
             grid=(count // chunk,),
@@ -232,16 +291,70 @@
                 pl.BlockSpec((heads.shape[0], chunk, width, width), lambda g, a: (0, g, 0, 0)),
                 pl.BlockSpec(memory_space=pl.ANY),
             ],
-            out_specs=[pl.BlockSpec(half, lambda g, a: (0, 0, 0, 0))] * 2,
-            scratch_shapes=[pltpu.VMEM((2 * chips,) + half[1:], F32)],
+            out_specs=[pl.BlockSpec(shape, lambda g, a: (0, 0, 0, 0)) for shape in shapes],
+            scratch_shapes=[pltpu.VMEM((2 * chips, sections * blocks, width, width), F32)],
         ),
-        out_shape=[out, out],
-        compiler_params=params(6 * size // MIB + 12),
+        out_shape=[jax.ShapeDtypeStruct(shape, F32) for shape in shapes],
+        compiler_params=params(6 * size // MIB + 26),
         cost_estimate=cost(
             count * blocks * width * width * width * 2 * sections, count * width * width * 12
         ),
         name="source_sums",
     )(table, first, second, heads, after)
+
+
+def known_kernel(layout, begin, steps, pairs, tables, after, targets, sums, *refs):
+    del after
+    starts, out = refs[:-1], refs[-1]
+    zeros = jnp.zeros(out.shape[1:], F32)
+    n = 0
+    for s, j in pairs:
+        block = starts[0][s - begin, tables[layout.at("picks", s, j)]]
+        out[n] = jnp.where(tables[layout.at("mine", s, j)] > 0, block, zeros)
+        n += 1
+    for s in steps:
+        block = targets[s, 0] - sums[s]
+        out[n] = jnp.where(tables[layout.at("mine", s, 0)] > 0, block, zeros)
+        n += 1
+
+
+def known_blocks(
+    layout, steps, pairs, tables, after, targets, sums, starts=None, begin=0
+):
+    width = targets.shape[-1]
+    arrays = [targets, sums] + ([] if starts is None else [starts])
+    shape = (len(steps) + len(pairs), width, width)
+    return pl.pallas_call(
+        functools.partial(known_kernel, layout, begin, steps, pairs),
+        in_specs=[smem(), pl.BlockSpec(memory_space=pl.ANY)] + [vmem()] * len(arrays),
+        out_specs=vmem(),
+        out_shape=jax.ShapeDtypeStruct(shape, F32),
+        compiler_params=params(8),
+        cost_estimate=cost(targets.size, 4 * targets.size),
+        name="known_blocks",
+    )(tables, after, *arrays)
+
+
+def message_kernel(layout, tables, whole, own, out):
+    ahead = layout.sections - 1
+    for j in range(ahead):
+        group = tables[layout.at("roots", 0, j + 1)]
+        out[j] = whole[group, tables[layout.at("picks", 0, j + 1)]]
+    out[ahead:] = own[...]
+
+
+def first_message(layout, tables, whole, own):
+    blocks, width, _ = own.shape
+    shape = (layout.sections - 1 + blocks, width, width)
+    return pl.pallas_call(
+        functools.partial(message_kernel, layout),
+        in_specs=[smem(), vmem(), vmem()],
+        out_specs=vmem(),
+        out_shape=jax.ShapeDtypeStruct(shape, own.dtype),
+        compiler_params=params(4),
+        cost_estimate=cost(own.size, 8 * own.size),
+        name="first_message",
+    )(tables, whole, own)
 
 
 def split(x):
@@ -252,13 +365,13 @@
     return high, middle, low
 
 
-def factor_kernel(step, col_count, flags, start, *refs):
+def factor_kernel(step, layout, tables, start, *refs):
     children, (upper, inverse, work) = refs[:-3], refs[-3:]
     width = start.shape[0]
     work[:, :width] = start[...]
     for slot, child in enumerate(children):
 
-        @pl.when(flags[step, slot, 0] > 0)
+        @pl.when(tables[layout.at("ahead", step, slot, 0)] > 0)
         def _(child=child):
             work[:, :width] -= times_transposed(child[0], child[0])
 
@@ -292,11 +405,11 @@
     inverse[...] = work[:, width:]
 
 
-def factor(step, flags, start, children, col_count):
+def factor(step, layout, tables, start, children):
     width = start.shape[0]
     out = jax.ShapeDtypeStruct((width, width), F32)
     return pl.pallas_call(
-        functools.partial(factor_kernel, step, col_count),
+        functools.partial(factor_kernel, step, layout),
         in_specs=[smem(), vmem()] + [vmem()] * len(children),
         out_specs=[vmem(), vmem()],
         out_shape=[out, out],
@@ -304,12 +417,10 @@
         compiler_params=params(8),
         cost_estimate=cost(width * width * width * 200, 16 * width * width),
         name="factor",
-    )(flags, start, *children)
-
-
-def blocks_kernel(
-    step, ahead, send, place, roots, flags, keep, into, after, start, inverse, upper, *refs
-):
+    )(tables, start, *children)
+
+
+def blocks_kernel(step, layout, ahead, send, tables, after, start, inverse, upper, *refs):
     del after
     work, refs = refs[-1], refs[:-1]
     rounded, refs = (refs[-1], refs[:-1]) if send else (None, refs)
@@ -323,17 +434,16 @@
         skipped = child.shape[0] - blocks
         for j in range(ahead):
 
-            @pl.when(flags[step, slot, j + 1] > 0)
+            @pl.when(tables[layout.at("ahead", step, slot, j + 1)] > 0)
             def _(slot=slot, child=child, j=j):
                 work[j] -= times_transposed(child[j + 1], child[0])
 
         for q in range(blocks):
 
-            @pl.when(keep[step, slot, q] > 0)
+            @pl.when(tables[layout.at("keep", step, slot, q)] > 0)
             def _(slot=slot, child=child, q=q):
-                work[ahead + into[step, slot, q]] -= times_transposed(
-                    child[skipped + q], child[0]
-                )
+                into = tables[layout.at("into", step, slot, q)]
+                work[ahead + into] -= times_transposed(child[skipped + q], child[0])
 
     solved = times_transposed(
         work[...].reshape((ahead + blocks) * width, width), inverse[...], HIGHEST
@@ -342,12 +452,12 @@
     if send:
         rounded[...] = solved.astype(BF16).reshape(ahead + blocks, width, width)
 
-    @pl.when(place[1] == roots[step, 0])
+    @pl.when(tables[layout.at("mine", step, 0)] > 0)
     def _():
         out[:width, :] = upper[...].T
 
 
-def panel_blocks(step, tables, after, start, later, send, inverse, upper, children):
+def panel_blocks(step, layout, tables, after, start, later, send, inverse, upper, children):
     blocks, width, _ = start.shape
     ahead = 0 if later is None else later.shape[0]
     arrays = [start, inverse, upper] + ([later] if ahead else []) + list(children)
@@ -355,17 +465,15 @@
     if send:
         out.append(jax.ShapeDtypeStruct((ahead + blocks, width, width), BF16))
     return pl.pallas_call(
-        functools.partial(blocks_kernel, step, ahead, send),
-        in_specs=[smem()] * len(tables)
-        + [pl.BlockSpec(memory_space=pl.ANY)]
-        + [vmem()] * len(arrays),
+        functools.partial(blocks_kernel, step, layout, ahead, send),
+        in_specs=[smem(), pl.BlockSpec(memory_space=pl.ANY)] + [vmem()] * len(arrays),
         out_specs=[vmem()] * len(out),
         out_shape=out,
         scratch_shapes=[pltpu.VMEM((blocks + ahead, width, width), F32)],
         compiler_params=params(12),
         cost_estimate=cost(start.size * 2000, start.size * 16),
         name="panel_blocks",
-    )(*tables, after, *arrays)
+    )(tables, after, *arrays)
 
 
 def local(targets, src_panels, live_counts, dest_owner, relative_map, diag_row, parent, chain_map):
@@ -418,18 +526,12 @@
     second = jnp.stack([deal(q) for q in range(1, local_blocks)], axis=1)
 
     chain = lax.all_gather(chain_map[None], "row", axis=0, tiled=True)
-    tab = functools.partial(jax.ShapeDtypeStruct, dtype=jnp.int32)
-    roots, picks, ahead, keep, into = pl.pallas_call(
-        functools.partial(tables_kernel, col_count),
+    layout = Tables(sections, col_count, local_blocks)
+    tables = pl.pallas_call(
+        functools.partial(tables_kernel, layout),
         in_specs=[smem()] * 4,
-        out_specs=[smem()] * 5,
-        out_shape=[
-            tab((sections, sections)),
-            tab((sections, sections)),
-            tab((sections, col_count, sections)),
-            tab((sections, col_count, local_blocks)),
-            tab((sections, col_count, local_blocks)),
-        ],
+        out_specs=smem(),
+        out_shape=jax.ShapeDtypeStruct((layout.size,), jnp.int32),
         name="tables",
     )(place, diag_row, parent, chain)
 
@@ -446,50 +548,66 @@
     held = jnp.where(source_root == row_index, slots, 2 * chips)[:, None]
 
     other, mine = diagonal_sums(held, first, chips)
-    _, total = scatter_sum(other, mine, col_count)
-
-    def known(items):
-        return jnp.stack([jnp.where(root == row_index, x, 0.0) for root, x in items])
+    total, _ = scatter_sum(other, mine, place, col_count)
 
     def share(x):
         return jnp.sum(lax.all_gather(x, "row", axis=0), axis=0)
 
     last = sections - 1
     soon = min(2, sections)
-    items = [(roots[s, 0], targets[s, 0] - total[s]) for s in range(sections)]
-    diagonals = share(known(items[:soon]))
-    diagonals = [diagonals[s] for s in range(soon)]
-    factored = factor(0, ahead, diagonals[0], [], col_count)
-
-    sums = source_sums(table, first, second, heads, factored[0], chips)
-    _, whole = scatter_sum(*sums, col_count)
-    starts = targets - whole.reshape(targets.shape)
+    diagonals = share(known_blocks(layout, [0], [], tables, place, targets, total))
+    diagonals = [diagonals[0]]
+    factored = factor(0, layout, tables, diagonals[0], [])
+
+    sums = source_sums(soon, table, first, second, heads, factored[0], chips)
+    whole, _ = scatter_sum(sums[0], sums[1], place, col_count)
+    early = targets[:soon] - whole.reshape(targets[:soon].shape)
+    starts = [early[s] for s in range(soon)]
+    sent_rest = place
+    if soon < sections:
+        whole, sent_rest = scatter_sum(sums[2], sums[3], whole, col_count)
+        late = targets[soon:] - whole.reshape(targets[soon:].shape)
+        starts += [late[s - soon] for s in range(soon, sections)]
 
     later = [None] * sections
-    pairs = [(s, j) for s in range(1, last) for j in range(1, sections - s)]
-    group = known([(roots[s, j], starts[s][picks[s, j]]) for s, j in pairs] + items[soon:])
-    whole = share(group)
-    for s in range(1, last):
-        at = pairs.index((s, 1))
-        later[s] = whole[at : at + last - s]
-    diagonals += [whole[len(pairs) + n] for n in range(sections - soon)]
+    pairs = [(s, j) for s in range(1, min(soon, last)) for j in range(1, sections - s)]
+    middle = range(1, min(soon + 1, sections))
+    if last:
+        group = known_blocks(layout, middle, pairs, tables, place, targets, total, early)
+        whole = sum_rows(lax.all_gather(group, "row", axis=0), place)
+        if pairs:
+            later[1] = whole[: len(pairs)]
+        diagonals += [whole[len(pairs) + n] for n in range(len(middle))]
 
     results, children = [], []
-    tables = (place, roots, ahead, keep, into)
     for s in range(sections):
         upper, inverse = factored
         if s > 0:
-            upper, inverse = factor(s, ahead, diagonals[s], children, col_count)
+            upper, inverse = factor(s, layout, tables, diagonals[s], children)
+        if s == soon and s < last:
+            spread = sum_rows(gathered, upper)
+            diagonals += [spread[len(padded) + n] for n in range(len(final))]
+            for t in range(soon, last):
+                at = pairs.index((t, 1))
+                later[t] = spread[at : at + last - t]
         made = panel_blocks(
-            s, tables, group if s == 0 else place, starts[s], later[s], s < last, inverse, upper, children
+            s, layout, tables, sent_rest if s == 0 else place, starts[s],
+            later[s], s < last, inverse, upper, children
         )
         results.append(made[0])
         if s < last:
             message = made[1]
             if s == 0:
                 whole = lax.all_gather(message, "row", axis=0)
-                needed = [whole[roots[0, j], picks[0, j]] for j in range(1, sections)]
-                message = jnp.concatenate([jnp.stack(needed), message], axis=0)
+                message = first_message(layout, tables, whole, message)
+                pairs = [(t, j) for t in range(soon, last) for j in range(1, sections - t)]
+                final = range(len(diagonals), sections)
+                if pairs:
+                    padded = pairs + pairs[:1] * (4 - len(pairs) - len(final))
+                    known = known_blocks(
+                        layout, final, padded, tables, whole, targets, total, late, soon
+                    )
+                    gathered = lax.all_gather(known, "row", axis=0)
             children = gather_columns(message, col_count)
     return jnp.stack(results)[:, None]
 

time: 282 us -> 255 us (0.904)
  between operations: 35.2 us -> 14.2 us
  local copies, waits for them, and re-layouts: 15.5 us -> 8.09 us
  Pallas kernels: 49.5 us -> 55.7 us
  other arithmetic: 11 us -> 4.99 us
  blocking collectives: 63.1 us -> 57.2 us
  waiting for transfers between devices: 78.8 us -> 83.1 us
    all_gather x1, waiting for transfers between devices: 5.23 us -> 15.5 us  [local(): heads = lax.all_gather(first, 'row', axis=0)]
    ppermute x29 -> x33, waiting for transfers between devices: 47.3 us -> 39.1 us  [swap(): return lax.ppermute(x, axis, [(i, i ^ mask) for i in range(size)])]
    all_gather x1, blocking collectives: 23.1 us -> 17.2 us  [share(): return jnp.sum(lax.all_gather(x, 'row', axis=0), axis=0)]
    unnamed x28 -> x26, local copies, waits for them, and re-layouts: 9.31 us -> 5.66 us
    pallas_call x10 -> x19, Pallas kernels: 37.8 us -> 41.1 us  [the longest x4 19.6 us: factor(): pl.pallas_call(functools.partial(factor_kernel, step, layout), in_specs=[...]
    pallas_call x4, Pallas kernels: 6.51 us -> 9.46 us  [pick(): pl.pallas_call(pick_kernel, grid_spec=pltpu.PrefetchScalarGridSpec(num_sc...]
    ppermute x29 -> x33, starting transfers between devices: 19.7 us -> 22.4 us  [swap(): return lax.ppermute(x, axis, [(i, i ^ mask) for i in range(size)])]
  transfers between devices with their start and end apart: 33 -> 38, of which waited for: 23 -> 21; matrix products, arithmetic and copies ran while one was open for 3% -> 2% of each run, Pallas kernels for 8% -> 14%
where the time goes in v3:
time: 255 us; the launch traced here: 253 us
  waiting for transfers between devices  83.1 us (33%)
  blocking collectives  57.2 us (22%)
  Pallas kernels  55.7 us (22%)
  starting transfers between devices  29.9 us (12%)
  between operations  14.2 us (6%)
  local copies, waits for them, and re-layouts  8.09 us (3%)
  other arithmetic  4.99 us (2%)
    ppermute x33, waiting for transfers between devices, swap(): return lax.ppermute(x, axis, [(i, i ^ mask) for i in range(size)])  39.1 us
    all_to_all x2, waiting for transfers between devices, deal(): lax.all_to_all(pick(src_panels, sent, block, width), 'col', 0, 0, tiled=T...  26.3 us
    ppermute x33, starting transfers between devices, swap(): return lax.ppermute(x, axis, [(i, i ^ mask) for i in range(size)])  22.4 us
    pallas_call x4, Pallas kernels, factor(): pl.pallas_call(functools.partial(factor_kernel, step, layout), in_specs=[...  19.6 us
    all_gather x1, blocking collectives, share(): return jnp.sum(lax.all_gather(x, 'row', axis=0), axis=0)  17.2 us
    all_gather x1, blocking collectives, local(): whole = lax.all_gather(message, 'row', axis=0)  15.9 us
    all_gather x1, waiting for transfers between devices, local(): heads = lax.all_gather(first, 'row', axis=0)  15.5 us
    all_gather x1, blocking collectives, local(): chain = lax.all_gather(chain_map[None], 'row', axis=0, tiled=True)  13.4 us
  transfers between devices with their start and end apart: 38, of which 21 were waited for; matrix products, arithmetic and copies ran while one was open for 2% of the time, Pallas kernels for 14%

profile of v3, /device:TPU:0, one launch (start us, length us, event | category | flops | bytes accessed | tf_op | source)
XLA Modules:
  0.0 253.1 jit_solution(3837230450249180127)
XLA Ops:
  8.0 10.7 %all-gather.7 = s32[8,13,64]{2,1,0:T(8,128)S(1)} all-gather(s32[1,13,64]{2,1,0:T(8,128)S(1)} %add_bitcast_fusion), channel_id=3, replica_groups=mesh['col'=8,'row'=4] {'col'}, dimensions={0}, use_global_device_ids=true | all-gather | bytes 29952 | tf_op jit(solution)/shard_map/all_gather | solution.py:502
  20.5 3.6 %pick.4 = bf16[64,128,128]{2,1,0:T(8,128)(2,1)} custom-call(s32[64]{0:T(128)S(1)} %add.137.index, bf16[64,256,128]{2,1,0:T(8,128)(2,1)} %source.3), custom_call_target="tpu_custom_call" | custom-call | bytes 4194304 | tf_op jit(solution)/shard_map/pick/pallas_call | solution.py:161
  24.1 3.6 %all-to-all-start = ((bf16[64,128,128]{2,1,0:T(8,128)(2,1)}), bf16[64,128,128]{2,1,0:T(8,128)(2,1)S(1)}, u32[]{:S(2)}, u32[]{:S(2)}) async-start(bf16[64,128,128]{2,1,0:T(8,128)(2,1)} %pick.4), calls=%async_computation | async-start | bytes 4194304 | tf_op jit(solution)/shard_map/all_to_all | solution.py:521
  28.0 26.3 %all-to-all-done.source = bf16[64,128,128]{2,1,0:T(8,128)(2,1)S(1)} async-done(((bf16[64,128,128]{2,1,0:T(8,128)(2,1)}), bf16[64,128,128]{2,1,0:T(8,128)(2,1)S(1)}, u32[]{:S(2)}, u32[]{:S(2)}) %all-to-all-start) | async-done | bytes 2097184 | tf_op jit(solution)/shard_map/all_to_all | solution.py:521
  55.9 3.6 %pick.6 = bf16[64,128,128]{2,1,0:T(8,128)(2,1)} custom-call(s32[64]{0:T(128)S(1)} %add.137.index, bf16[64,256,128]{2,1,0:T(8,128)(2,1)} %source.3), custom_call_target="tpu_custom_call" | custom-call | bytes 4194304 | tf_op jit(solution)/shard_map/pick/pallas_call | solution.py:161
  59.6 3.8 %all-to-all-start.1 = ((bf16[64,128,128]{2,1,0:T(8,128)(2,1)}), bf16[64,128,128]{2,1,0:T(8,128)(2,1)S(1)}, u32[]{:S(2)}, u32[]{:S(2)}) async-start(bf16[64,128,128]{2,1,0:T(8,128)(2,1)} %pick.6), calls=%async_computation.1 | async-start | bytes 4194304 | tf_op jit(solution)/shard_map/all_to_all | solution.py:521
  64.5 5.1 %diagonal_sums.1 = (f32[4,4,128,128]{3,2,1,0:T(8,128)}, f32[4,4,128,128]{3,2,1,0:T(8,128)S(1)}) custom-call(s32[4,1,32]{2,1,0:T(1,128)S(1)} %copy.62.table, bf16[32,128,128]{2,1,0:T(8,128)(2,1)} %pick.5.heads.first), custom_call_target="tpu_custom_call" | custom-call | flops 268435456 | bytes 2097152 | tf_op jit(solution)/shard_map/diagonal_sums/pallas_call | solution.py:222
  70.0 13.4 %all-gather = s32[12,8,2]{1,2,0:T(2,128)S(1)} all-gather(s32[3,8,2]{1,2,0:T(2,128)S(1)} %copy-done.12), channel_id=2, replica_groups=mesh['col'=8,'row'=4] {'row'}, dimensions={0}, use_global_device_ids=true | all-gather | bytes 960 | tf_op jit(solution)/shard_map/all_gather | solution.py:528
  90.1 2.5 tables.1
  97.2 4.1 %collective-permute-done.3 = f32[4,128,128]{2,1,0:T(8,128)} collective-permute-done((f32[4,128,128]{2,1,0:T(8,128)}, f32[4,128,128]{2,1,0:T(8,128)}, u32[]{:S(2)}, u32[]{:S(2)}) %collective-permute-start.3) | collective-permute-done | bytes 262176 | tf_op jit(solution)/shard_map/ppermute | solution.py:49
  103.1 17.2 %all-gather.3 = f32[4,128,128]{2,1,0:T(8,128)S(1)} all-gather(f32[1,128,128]{2,1,0:T(8,128)S(1)} %known_blocks.3), channel_id=5, replica_groups=mesh['col'=8,'row'=4] {'row'}, dimensions={0}, use_global_device_ids=true | all-gather | bytes 327680 | tf_op jit(solution)/shard_map/all_gather | solution.py:554
  120.4 4.7 %factor.4 = (f32[128,128]{1,0:T(8,128)S(1)}, f32[128,128]{1,0:T(8,128)S(1)}) custom-call(s32[304]{0:T(512)S(1)} %copy-done.8, f32[128,128]{1,0:T(8,128)S(1)} %reduce.1.start), custom_call_target="tpu_custom_call" | custom-call | flops 419430400 | bytes 262144 | tf_op jit(solution)/shard_map/factor/pallas_call | solution.py:411
  125.1 15.5 %all-gather.12.cloned.1.call-done = bf16[128,128,128]{2,1,0:T(8,128)(2,1)} async-done(((bf16[32,128,128]{2,1,0:T(8,128)(2,1)}), bf16[128,128,128]{2,1,0:T(8,128)(2,1)}) %all-gather.12.cloned.1.call-update) | async-done | bytes 4194320 | tf_op jit(solution)/shard_map/all_gather | solution.py:525
  142.7 6.7 %source_sums.1 = (f32[4,4,128,128]{3,2,1,0:T(8,128)S(1)}, f32[4,4,128,128]{3,2,1,0:T(8,128)S(1)}, f32[4,4,128,128]{3,2,1,0:T(8,128)}, f32[4,4,128,128]{3,2,1,0:T(8,128)S(1)}) custom-call(s32[4,4,32]{2,1,0:T(4,128)S(1)} %pad_add_fusion.table, bf16[32,128,128]{2,1,0:T(8,128)(2,1)} %pick.5.heads.first, bf16[32,1,128,128]{3,2,1,0:T(8,128)(2,1)S(1)} %bitcast.75, ...), custom_call_target="tpu_custom_call" | custom-call | flops 1073741824 | bytes 6291456 | tf_op jit(solution)/shard_map/source_sums/pallas_call | solution.py:283
  149.4 2.7 %collective-permute-done.5.other = f32[4,4,128,128]{3,2,1,0:T(8,128)S(1)} collective-permute-done((f32[4,4,128,128]{3,2,1,0:T(8,128)S(1)}, f32[4,4,128,128]{3,2,1,0:T(8,128)S(1)}, u32[]{:S(2)}, u32[]{:S(2)}) %collective-permute-start.5) | collective-permute-done | bytes 1048608 | tf_op jit(solution)/shard_map/ppermute | solution.py:49
  155.9 5.5 %collective-permute-done.6 = f32[4,128,128]{2,1,0:T(8,128)S(1)} collective-permute-done((f32[4,128,128]{2,1,0:T(8,128)S(1)}, f32[4,128,128]{2,1,0:T(8,128)S(1)}, u32[]{:S(2)}, u32[]{:S(2)}) %collective-permute-start.6) | collective-permute-done | bytes 262176 | tf_op jit(solution)/shard_map/ppermute | solution.py:49
  161.4 5.9 %collective-permute-done.7 = f32[4,128,128]{2,1,0:T(8,128)S(1)} collective-permute-done((f32[4,128,128]{2,1,0:T(8,128)S(1)}, f32[4,128,128]{2,1,0:T(8,128)S(1)}, u32[]{:S(2)}, u32[]{:S(2)}) %collective-permute-start.7) | collective-permute-done | bytes 262176 | tf_op jit(solution)/shard_map/ppermute | solution.py:49
  174.7 15.9 %all-gather.5 = bf16[8,128,128]{2,1,0:T(8,128)(2,1)S(1)} all-gather(bf16[2,128,128]{2,1,0:T(8,128)(2,1)S(1)} %get-tuple-element.55.own), channel_id=7, replica_groups=mesh['col'=8,'row'=4] {'row'}, dimensions={0}, use_global_device_ids=true | all-gather | bytes 327680 | tf_op jit(solution)/shard_map/all_gather | solution.py:601
  202.1 5.0 %factor.5 = (f32[128,128]{1,0:T(8,128)S(1)}, f32[128,128]{1,0:T(8,128)S(1)}) custom-call(s32[304]{0:T(512)S(1)} %copy-done.8, f32[128,128]{1,0:T(8,128)S(1)} %get-tuple-element.77.start, bf16[5,128,128]{2,1,0:T(8,128)(2,1)S(1)} %first_message.1.refs_0_.refs_1_, bf16[5,128,128]{2,1,0:T(8,128)(2,1)S(1)} %collective-permute-done.9.refs_1_.refs_2_, ...), custom_call_target="tpu_custom_call" | custom-call | flops 419430400 | bytes 262144 | tf_op jit(solution)/shard_map/factor/pallas_call | solution.py:411
  212.0 2.8 %collective-permute-done.19.refs_1_.refs_2_ = bf16[4,128,128]{2,1,0:T(8,128)(2,1)S(1)} collective-permute-done((bf16[4,128,128]{2,1,0:T(8,128)(2,1)S(1)}, bf16[4,128,128]{2,1,0:T(8,128)(2,1)S(1)}, u32[]{:S(2)}, u32[]{:S(2)}) %collective-permute-start.19) | collective-permute-done | bytes 131104 | tf_op jit(solution)/shard_map/ppermute | solution.py:49
  214.9 3.8 %collective-permute-done.20.refs_2_.refs_3_ = bf16[4,128,128]{2,1,0:T(8,128)(2,1)S(1)} collective-permute-done((bf16[4,128,128]{2,1,0:T(8,128)(2,1)S(1)}, bf16[4,128,128]{2,1,0:T(8,128)(2,1)S(1)}, u32[]{:S(2)}, u32[]{:S(2)}) %collective-permute-start.20) | collective-permute-done | bytes 131104 | tf_op jit(solution)/shard_map/ppermute | solution.py:49
  220.2 4.9 %factor.6 = (f32[128,128]{1,0:T(8,128)S(1)}, f32[128,128]{1,0:T(8,128)S(1)}) custom-call(s32[304]{0:T(512)S(1)} %copy-done.8, f32[128,128]{1,0:T(8,128)S(1)} %get-tuple-element.78.start, bf16[4,128,128]{2,1,0:T(8,128)(2,1)S(1)} %get-tuple-element.62.refs_0_.refs_1_, bf16[4,128,128]{2,1,0:T(8,128)(2,1)S(1)} %collective-permute-done.19.refs_1_.refs_2_, ...), custom_call_target="tpu_custom_call" | custom-call | flops 419430400 | bytes 262144 | tf_op jit(solution)/shard_map/factor/pallas_call | solution.py:411
  234.8 2.2 collective-permute-done.27.refs_2_
  239.4 5.0 %factor.7 = (f32[128,128]{1,0:T(8,128)S(1)}, f32[128,128]{1,0:T(8,128)S(1)}) custom-call(s32[304]{0:T(512)S(1)} %copy-done.8, f32[128,128]{1,0:T(8,128)S(1)} %get-tuple-element.72.start, bf16[3,128,128]{2,1,0:T(8,128)(2,1)S(1)} %get-tuple-element.66.refs_0_, bf16[3,128,128]{2,1,0:T(8,128)(2,1)S(1)} %collective-permute-done.26.refs_1_, ...), custom_call_target="tpu_custom_call" | custom-call | flops 419430400 | bytes 262144 | tf_op jit(solution)/shard_map/factor/pallas_call | solution.py:411
  (151 shorter events, 64.4 us)
Async XLA Ops:
  24.1 30.2 %all-to-all-start = ((bf16[64,128,128]{2,1,0:T(8,128)(2,1)}), bf16[64,128,128]{2,1,0:T(8,128)(2,1)S(1)}, u32[]{:S(2)}, u32[]{:S(2)}) async-start(bf16[64,128,128]{2,1,0:T(8,128)(2,1)} %pick.4), calls=%async_computation | async-start | bytes 4194304 | tf_op jit(solution)/shard_map/all_to_all | solution.py:521
  27.8 112.8 %all-gather.12.cloned.1.call-start = ((), (), s32[]{:S(2)}) async-start(), calls=%async_computation.2 | async-start | bytes 5242880 | tf_op jit(solution)/shard_map/all_gather | solution.py:525
  59.6 33.0 %all-to-all-start.1 = ((bf16[64,128,128]{2,1,0:T(8,128)(2,1)}), bf16[64,128,128]{2,1,0:T(8,128)(2,1)S(1)}, u32[]{:S(2)}, u32[]{:S(2)}) async-start(bf16[64,128,128]{2,1,0:T(8,128)(2,1)} %pick.6), calls=%async_computation.1 | async-start | bytes 4194304 | tf_op jit(solution)/shard_map/all_to_all | solution.py:521
  63.3 137.4 %all-gather.14.cloned.1.call-start = ((), (), s32[]{:S(2)}) async-start(), calls=%async_computation.3 | async-start | bytes 1310720 | tf_op jit(solution)/shard_map/all_gather | solution.py:577
  69.6 14.7 %collective-permute-start = (f32[4,4,128,128]{3,2,1,0:T(8,128)}, f32[4,4,128,128]{3,2,1,0:T(8,128)}, u32[]{:S(2)}, u32[]{:S(2)}) collective-permute-start(f32[4,4,128,128]{3,2,1,0:T(8,128)} %get-tuple-element.38), channel_id=1, source_target_pairs={{0,4},{4,0},{8,12},{12,8},{16,20},{20,16},{24,28},{28,24},{1,5},{5... | collective-permute-start | bytes 3145736 | tf_op jit(solution)/shard_map/ppermute | solution.py:49
  86.4 9.6 %collective-permute-start.1 = (f32[4,128,128]{2,1,0:T(8,128)}, f32[4,128,128]{2,1,0:T(8,128)}, u32[]{:S(2)}, u32[]{:S(2)}) collective-permute-start(f32[4,128,128]{2,1,0:T(8,128)} %get-tuple-element.40), channel_id=1, source_target_pairs={{0,8},{4,12},{8,0},{12,4},{16,24},{20,28},{24,16},{28,20},{1,9},{5... | collective-permute-start | bytes 786440 | tf_op jit(solution)/shard_map/ppermute | solution.py:49
  88.2 9.0 %collective-permute-start.2 = (f32[4,128,128]{2,1,0:T(8,128)}, f32[4,128,128]{2,1,0:T(8,128)}, u32[]{:S(2)}, u32[]{:S(2)}) collective-permute-start(f32[4,128,128]{2,1,0:T(8,128)} %get-tuple-element.41), channel_id=1, source_target_pairs={{0,16},{4,20},{8,24},{12,28},{16,0},{20,4},{24,8},{28,12},{1,17},{... | collective-permute-start | bytes 786440 | tf_op jit(solution)/shard_map/ppermute | solution.py:49
  89.7 11.6 %collective-permute-start.3 = (f32[4,128,128]{2,1,0:T(8,128)}, f32[4,128,128]{2,1,0:T(8,128)}, u32[]{:S(2)}, u32[]{:S(2)}) collective-permute-start(f32[4,128,128]{2,1,0:T(8,128)} %get-tuple-element.42), channel_id=1, source_target_pairs={{0,24},{4,28},{8,16},{12,20},{16,8},{20,12},{24,0},{28,4},{1,25},{... | collective-permute-start | bytes 786440 | tf_op jit(solution)/shard_map/ppermute | solution.py:49
  152.2 9.2 %collective-permute-start.6 = (f32[4,128,128]{2,1,0:T(8,128)S(1)}, f32[4,128,128]{2,1,0:T(8,128)S(1)}, u32[]{:S(2)}, u32[]{:S(2)}) collective-permute-start(f32[4,128,128]{2,1,0:T(8,128)S(1)} %get-tuple-element.49), channel_id=1, source_target_pairs={{0,8},{4,12},{8,0},{12,4},{16,24},{20,28},{24,16},{28,20},{1,9},{5... | collective-permute-start | bytes 786440 | tf_op jit(solution)/shard_map/ppermute | solution.py:49
  153.7 13.7 %collective-permute-start.7 = (f32[4,128,128]{2,1,0:T(8,128)S(1)}, f32[4,128,128]{2,1,0:T(8,128)S(1)}, u32[]{:S(2)}, u32[]{:S(2)}) collective-permute-start(f32[4,128,128]{2,1,0:T(8,128)S(1)} %get-tuple-element.50), channel_id=1, source_target_pairs={{0,16},{4,20},{8,24},{12,28},{16,0},{20,4},{24,8},{28,12},{1,17},{... | collective-permute-start | bytes 786440 | tf_op jit(solution)/shard_map/ppermute | solution.py:49
  155.1 12.2 %collective-permute-start.8 = (f32[4,128,128]{2,1,0:T(8,128)S(1)}, f32[4,128,128]{2,1,0:T(8,128)S(1)}, u32[]{:S(2)}, u32[]{:S(2)}) collective-permute-start(f32[4,128,128]{2,1,0:T(8,128)S(1)} %get-tuple-element.51), channel_id=1, source_target_pairs={{0,24},{4,28},{8,16},{12,20},{16,8},{20,12},{24,0},{28,4},{1,25},{... | collective-permute-start | bytes 786440 | tf_op jit(solution)/shard_map/ppermute | solution.py:49
  155.8 13.0 %collective-permute-start.4 = (f32[4,4,128,128]{3,2,1,0:T(8,128)}, f32[4,4,128,128]{3,2,1,0:T(8,128)}, u32[]{:S(2)}, u32[]{:S(2)}) collective-permute-start(f32[4,4,128,128]{3,2,1,0:T(8,128)} %get-tuple-element.45), channel_id=1, source_target_pairs={{0,4},{4,0},{8,12},{12,8},{16,20},{20,16},{24,28},{28,24},{1,5},{5... | collective-permute-start | bytes 3145736 | tf_op jit(solution)/shard_map/ppermute | solution.py:49
  168.8 58.5 %all-gather.16.cloned.1.call-start = ((), (), s32[]{:S(2)}) async-start(), calls=%async_computation.4 | async-start | bytes 1310720 | tf_op jit(solution)/shard_map/all_gather | solution.py:610
  170.2 20.4 %collective-permute-start.16 = (f32[4,128,128]{2,1,0:T(8,128)S(1)}, f32[4,128,128]{2,1,0:T(8,128)S(1)}, u32[]{:S(2)}, u32[]{:S(2)}) collective-permute-start(f32[4,128,128]{2,1,0:T(8,128)S(1)} %get-tuple-element.59), channel_id=1, source_target_pairs={{0,8},{4,12},{8,0},{12,4},{16,24},{20,28},{24,16},{28,20},{1,9},{5... | collective-permute-start | bytes 786440 | tf_op jit(solution)/shard_map/ppermute | solution.py:49
  171.4 19.1 %collective-permute-start.17 = (f32[4,128,128]{2,1,0:T(8,128)S(1)}, f32[4,128,128]{2,1,0:T(8,128)S(1)}, u32[]{:S(2)}, u32[]{:S(2)}) collective-permute-start(f32[4,128,128]{2,1,0:T(8,128)S(1)} %get-tuple-element.60), channel_id=1, source_target_pairs={{0,16},{4,20},{8,24},{12,28},{16,0},{20,4},{24,8},{28,12},{1,17},{... | collective-permute-start | bytes 786440 | tf_op jit(solution)/shard_map/ppermute | solution.py:49
  172.3 18.2 %collective-permute-start.18 = (f32[4,128,128]{2,1,0:T(8,128)S(1)}, f32[4,128,128]{2,1,0:T(8,128)S(1)}, u32[]{:S(2)}, u32[]{:S(2)}) collective-permute-start(f32[4,128,128]{2,1,0:T(8,128)S(1)} %get-tuple-element.61), channel_id=1, source_target_pairs={{0,24},{4,28},{8,16},{12,20},{16,8},{20,12},{24,0},{28,4},{1,25},{... | collective-permute-start | bytes 786440 | tf_op jit(solution)/shard_map/ppermute | solution.py:49
  194.4 6.3 %collective-permute-start.11 = (bf16[5,128,128]{2,1,0:T(8,128)(2,1)S(1)}, bf16[5,128,128]{2,1,0:T(8,128)(2,1)S(1)}, u32[]{:S(2)}, u32[]{:S(2)}) collective-permute-start(bf16[5,128,128]{2,1,0:T(8,128)(2,1)S(1)} %first_message.1.refs_0_.refs_1_), channel_id=1, source_target_pairs={{0,24},{4,28},{8,16},{12,20},{16,8},{20,12},{24,0},{28,4},{1,25},{... | collective-permute-start | bytes 491528 | tf_op jit(solution)/shard_map/ppermute | solution.py:49
  196.1 5.9 %collective-permute-start.12 = (bf16[5,128,128]{2,1,0:T(8,128)(2,1)S(1)}, bf16[5,128,128]{2,1,0:T(8,128)(2,1)S(1)}, u32[]{:S(2)}, u32[]{:S(2)}) collective-permute-start(bf16[5,128,128]{2,1,0:T(8,128)(2,1)S(1)} %first_message.1.refs_0_.refs_1_), channel_id=1, source_target_pairs={{0,4},{4,0},{8,12},{12,8},{16,20},{20,16},{24,28},{28,24},{1,5},{5... | collective-permute-start | bytes 491528 | tf_op jit(solution)/shard_map/ppermute | solution.py:49
  208.4 6.4 %collective-permute-start.19 = (bf16[4,128,128]{2,1,0:T(8,128)(2,1)S(1)}, bf16[4,128,128]{2,1,0:T(8,128)(2,1)S(1)}, u32[]{:S(2)}, u32[]{:S(2)}) collective-permute-start(bf16[4,128,128]{2,1,0:T(8,128)(2,1)S(1)} %get-tuple-element.62.refs_0_.refs_1_), channel_id=1, source_target_pairs={{0,8},{4,12},{8,0},{12,4},{16,24},{20,28},{24,16},{28,20},{1,9},{5... | collective-permute-start | bytes 393224 | tf_op jit(solution)/shard_map/ppermute | solution.py:49
  210.2 8.5 %collective-permute-start.20 = (bf16[4,128,128]{2,1,0:T(8,128)(2,1)S(1)}, bf16[4,128,128]{2,1,0:T(8,128)(2,1)S(1)}, u32[]{:S(2)}, u32[]{:S(2)}) collective-permute-start(bf16[4,128,128]{2,1,0:T(8,128)(2,1)S(1)} %get-tuple-element.62.refs_0_.refs_1_), channel_id=1, source_target_pairs={{0,16},{4,20},{8,24},{12,28},{16,0},{20,4},{24,8},{28,12},{1,17},{... | collective-permute-start | bytes 393224 | tf_op jit(solution)/shard_map/ppermute | solution.py:49
  211.6 7.1 %collective-permute-start.21 = (bf16[4,128,128]{2,1,0:T(8,128)(2,1)S(1)}, bf16[4,128,128]{2,1,0:T(8,128)(2,1)S(1)}, u32[]{:S(2)}, u32[]{:S(2)}) collective-permute-start(bf16[4,128,128]{2,1,0:T(8,128)(2,1)S(1)} %get-tuple-element.62.refs_0_.refs_1_), channel_id=1, source_target_pairs={{0,24},{4,28},{8,16},{12,20},{16,8},{20,12},{24,0},{28,4},{1,25},{... | collective-permute-start | bytes 393224 | tf_op jit(solution)/shard_map/ppermute | solution.py:49
  211.9 7.3 %collective-permute-start.22 = (bf16[4,128,128]{2,1,0:T(8,128)(2,1)S(1)}, bf16[4,128,128]{2,1,0:T(8,128)(2,1)S(1)}, u32[]{:S(2)}, u32[]{:S(2)}) collective-permute-start(bf16[4,128,128]{2,1,0:T(8,128)(2,1)S(1)} %get-tuple-element.62.refs_0_.refs_1_), channel_id=1, source_target_pairs={{0,4},{4,0},{8,12},{12,8},{16,20},{20,16},{24,28},{28,24},{1,5},{5... | collective-permute-start | bytes 393224 | tf_op jit(solution)/shard_map/ppermute | solution.py:49
  231.2 5.8 %collective-permute-start.27 = (bf16[3,128,128]{2,1,0:T(8,128)(2,1)S(1)}, bf16[3,128,128]{2,1,0:T(8,128)(2,1)S(1)}, u32[]{:S(2)}, u32[]{:S(2)}) collective-permute-start(bf16[3,128,128]{2,1,0:T(8,128)(2,1)S(1)} %get-tuple-element.66.refs_0_), channel_id=1, source_target_pairs={{0,16},{4,20},{8,24},{12,28},{16,0},{20,4},{24,8},{28,12},{1,17},{... | collective-permute-start | bytes 294920 | tf_op jit(solution)/shard_map/ppermute | solution.py:49
  232.6 5.5 %collective-permute-start.28 = (bf16[3,128,128]{2,1,0:T(8,128)(2,1)S(1)}, bf16[3,128,128]{2,1,0:T(8,128)(2,1)S(1)}, u32[]{:S(2)}, u32[]{:S(2)}) collective-permute-start(bf16[3,128,128]{2,1,0:T(8,128)(2,1)S(1)} %get-tuple-element.66.refs_0_), channel_id=1, source_target_pairs={{0,24},{4,28},{8,16},{12,20},{16,8},{20,12},{24,0},{28,4},{1,25},{... | collective-permute-start | bytes 294920 | tf_op jit(solution)/shard_map/ppermute | solution.py:49
  (27 other events, 159.3 us)
Sparse Core Ops, SparseCore 0:
  56.1 84.4 all-gather.11
  168.9 30.0 all-gather.13
  200.6 26.6 all-gather.15

commit v4 on v3

--- a/solution.py
+++ b/solution.py
@@ -151,26 +151,55 @@
                 out[layout.at("into", s, slot, q)] = chain[row, s - 1, child, q]
 
 
-def pick_kernel(index, source, out):
-    for i in range(out.shape[0]):
-        out[i] = source[index[i]]
-
-
-def pick(source, index, block, rows):
-    count, width = index.shape[0], source.shape[2]
-    return pl.pallas_call(
-        pick_kernel,
+def split_kernel(index, source, *outs):
+    share = outs[0].shape[0]
+    for k, out in enumerate(outs):
+        for m in range(share):
+            out[m] = source[index[k * share + m]]
+
+
+def split_panels(source, index, block, width, parts):
+    share = index.shape[0] // parts
+    shape = (share, width, source.shape[2])
+    return pl.pallas_call(
+        split_kernel,
         grid_spec=pltpu.PrefetchScalarGridSpec(
             num_scalar_prefetch=1,
             grid=(1,),
-            in_specs=[pl.BlockSpec((source.shape[0], rows, width), lambda g, a: (0, block, 0))],
-            out_specs=pl.BlockSpec((count, rows, width), lambda g, a: (0, 0, 0)),
+            in_specs=[
+                pl.BlockSpec((source.shape[0], width, source.shape[2]), lambda g, a: (0, block, 0))
+            ],
+            out_specs=[pl.BlockSpec(shape, lambda g, a: (0, 0, 0))] * parts,
         ),
-        out_shape=jax.ShapeDtypeStruct((count, rows, width), source.dtype),
+        out_shape=[jax.ShapeDtypeStruct(shape, source.dtype)] * parts,
         compiler_params=params(48),
-        cost_estimate=cost(0, 4 * count * rows * width),
-        name="pick",
+        cost_estimate=cost(0, 4 * index.shape[0] * width * source.shape[2]),
+        name="split_panels",
     )(index, source)
+
+
+def merge_kernel(index, *refs):
+    parts, (out, work) = refs[:-2], refs[-2:]
+    share = parts[0].shape[0]
+    for k, part in enumerate(parts):
+        work[k * share : (k + 1) * share] = part[...]
+    for i in range(out.shape[0]):
+        out[i] = work[index[i]]
+
+
+def merge_panels(parts, index):
+    share, width, _ = parts[0].shape
+    count = index.shape[0]
+    return pl.pallas_call(
+        merge_kernel,
+        in_specs=[smem()] + [vmem()] * len(parts),
+        out_specs=vmem(),
+        out_shape=jax.ShapeDtypeStruct((count,) + parts[0].shape[1:], parts[0].dtype),
+        scratch_shapes=[pltpu.VMEM((len(parts) * share,) + parts[0].shape[1:], parts[0].dtype)],
+        compiler_params=params(16),
+        cost_estimate=cost(0, 8 * count * width * width),
+        name="merge_panels",
+    )(index, *parts)
 
 
 def sum_kernel(after, x, out):
@@ -378,23 +407,35 @@
     rows = lax.broadcasted_iota(jnp.int32, (width, width), 0)
     columns = lax.broadcasted_iota(jnp.int32, (width, width), 1)
     work[:, width:] = (rows == columns).astype(F32)
-    sub = lax.broadcasted_iota(jnp.int32, (PANEL, 1), 0)
+    groups = range(PANEL // 8)
+    sub = lax.broadcasted_iota(jnp.int32, (8, 1), 0)
     for first in range(0, width, PANEL):
         last = first + PANEL
-        slab = work[first:last, :]
+        slab = [work[first + 8 * g : first + 8 * g + 8, :] for g in groups]
         spans = [
-            jnp.broadcast_to(slab[:, first + k : first + k + 1], (PANEL, width))
+            {
+                g: jnp.broadcast_to(slab[g][:, first + k : first + k + 1], (8, width))
+                for g in groups
+                if g >= k // 8
+            }
             for k in range(PANEL)
         ]
-        scale = jnp.zeros((PANEL, 1), F32)
+        scale = [jnp.zeros((8, 1), F32) for _ in groups]
         for j in range(PANEL):
-            pivot = spans[j][j : j + 1, :]
-            ratio = jnp.where(sub > j, spans[j] * (1.0 / pivot), 0.0)
+            here, row = divmod(j, 8)
+            pivot = spans[j][here][row : row + 1, :]
+            inverted = 1.0 / pivot
+            ratio = {g: span * inverted for g, span in spans[j].items()}
+            ratio[here] = jnp.where(sub > row, ratio[here], 0.0)
             for k in range(j + 1, PANEL):
-                spans[k] = spans[k] - ratio * spans[k][j : j + 1, :]
-            slab = slab - jnp.concatenate([ratio, ratio], axis=1) * slab[j : j + 1, :]
-            scale = jnp.where(sub == j, lax.rsqrt(pivot[:, 0:1]), scale)
-        slab = slab * scale
+                crossing = spans[j][k // 8][k % 8 : k % 8 + 1, :]
+                for g in spans[k]:
+                    spans[k][g] = spans[k][g] - ratio[g] * crossing
+            line = slab[here][row : row + 1, :]
+            for g in ratio:
+                slab[g] = slab[g] - jnp.concatenate([ratio[g], ratio[g]], axis=1) * line
+            scale[here] = jnp.where(sub == row, lax.rsqrt(pivot[:, 0:1]), scale[here])
+        slab = jnp.concatenate([slab[g] * scale[g] for g in groups], axis=0)
         work[first:last, :] = slab
         if last < width:
             high, middle, low = split(slab)
@@ -504,9 +545,9 @@
     columns_of = jnp.arange(col_count)
     offsets = jnp.sum(jnp.where(columns_of[None, :] < columns_of[:, None], counts[None, :], 0), axis=1)
     own_offset = jnp.sum(jnp.where(columns_of == own, offsets, 0))
+    partner = jnp.bitwise_xor(columns_of, own)
     sent = (
-        jnp.mod(columns_of - own_offset, col_count)[:, None]
-        + col_count * jnp.arange(share)[None, :]
+        jnp.mod(partner - own_offset, col_count)[:, None] + col_count * jnp.arange(share)[None, :]
     ).reshape(-1)
     number = jnp.arange(dealt) * col_count + own
     source_column = jnp.sum(
@@ -515,11 +556,12 @@
     index = number - jnp.sum(
         jnp.where(columns_of[None, :] == source_column[:, None], offsets[None, :], 0), axis=1
     )
-    kept = source_column * share + index // col_count
+    kept = jnp.bitwise_xor(source_column, own) * share + index // col_count
 
     def deal(block):
-        mixed = lax.all_to_all(pick(src_panels, sent, block, width), "col", 0, 0, tiled=True)
-        return pick(mixed, kept, 0, width)
+        parts = split_panels(src_panels, sent, block, width, col_count)
+        parts = [swap(part, "col", col_count, k) if k else part for k, part in enumerate(parts)]
+        return merge_panels(parts, kept)
 
     first = deal(0)
     heads = lax.all_gather(first, "row", axis=0)

time: 255 us -> 251 us (0.984)
  Pallas kernels: 55.7 us -> 50 us
  starting transfers between devices: 29.9 us -> 35.5 us
  waiting for transfers between devices: 83.1 us -> 78.8 us
    ppermute x33 -> x47, waiting for transfers between devices: 39.1 us -> 69.4 us  [swap(): return lax.ppermute(x, axis, [(i, i ^ mask) for i in range(size)])]
    all_to_all x2 -> x0, waiting for transfers between devices: 26.3 us -> none  [deal(): lax.all_to_all(pick(src_panels, sent, block, width), 'col', 0, 0, tiled=T...]
    ppermute x33 -> x47, starting transfers between devices: 22.4 us -> 35.4 us  [swap(): return lax.ppermute(x, axis, [(i, i ^ mask) for i in range(size)])]
    all_gather x1, waiting for transfers between devices: 15.5 us -> 5.08 us  [local(): heads = lax.all_gather(first, 'row', axis=0)]
    all_to_all x2 -> x0, starting transfers between devices: 7.36 us -> none  [deal(): lax.all_to_all(pick(src_panels, sent, block, width), 'col', 0, 0, tiled=T...]
    pallas_call x4, Pallas kernels: 19.6 us -> 16 us  [factor(): pl.pallas_call(functools.partial(factor_kernel, step, layout), in_specs=[...]
    unnamed x26 -> x22, local copies, waits for them, and re-layouts: 5.66 us -> 6.07 us
  transfers between devices with their start and end apart: 38 -> 50, of which waited for: 21 -> 23; matrix products, arithmetic and copies ran while one was open for 2% -> 2% of each run, Pallas kernels for 14% -> 13%
where the time goes in v4:
time: 251 us; the launch traced here: 250 us
  waiting for transfers between devices  78.8 us (31%)
  blocking collectives  58.1 us (23%)
  Pallas kernels  50 us (20%)
  starting transfers between devices  35.5 us (14%)
  between operations  14.2 us (6%)
  local copies, waits for them, and re-layouts  8.49 us (3%)
  other arithmetic  4.85 us (2%)
    ppermute x47, waiting for transfers between devices, swap(): return lax.ppermute(x, axis, [(i, i ^ mask) for i in range(size)])  69.4 us
    ppermute x47, starting transfers between devices, swap(): return lax.ppermute(x, axis, [(i, i ^ mask) for i in range(size)])  35.4 us
    all_gather x1, blocking collectives, share(): return jnp.sum(lax.all_gather(x, 'row', axis=0), axis=0)  18.1 us
    pallas_call x4, Pallas kernels, factor(): pl.pallas_call(functools.partial(factor_kernel, step, layout), in_specs=[...  16 us
    all_gather x1, blocking collectives, local(): whole = lax.all_gather(message, 'row', axis=0)  15.9 us
    all_gather x1, blocking collectives, local(): chain = lax.all_gather(chain_map[None], 'row', axis=0, tiled=True)  13.5 us
    all_gather x1, blocking collectives, local(): facts = lax.all_gather(facts, 'col', axis=0)  10.7 us
    pallas_call x1, Pallas kernels, source_sums(): pl.pallas_call(functools.partial(source_kernel, soon), grid_spec=pltpu.Pr...  6.81 us
  transfers between devices with their start and end apart: 50, of which 23 were waited for; matrix products, arithmetic and copies ran while one was open for 2% of the time, Pallas kernels for 13%

profile of v4, /device:TPU:0, one launch (start us, length us, event | category | flops | bytes accessed | tf_op | source)
XLA Modules:
  0.0 250.0 jit_solution(15665708204892835407)
XLA Ops:
  8.0 10.7 %all-gather.7 = s32[8,13,64]{2,1,0:T(8,128)S(1)} all-gather(s32[1,13,64]{2,1,0:T(8,128)S(1)} %add_bitcast_fusion), channel_id=3, replica_groups=mesh['col'=8,'row'=4] {'col'}, dimensions={0}, use_global_device_ids=true | all-gather | bytes 29952 | tf_op jit(solution)/shard_map/all_gather | solution.py:543
  28.3 4.0 %collective-permute-done.1.refs_2_ = bf16[8,128,128]{2,1,0:T(8,128)(2,1)S(1)} collective-permute-done((bf16[8,128,128]{2,1,0:T(8,128)(2,1)S(1)}, bf16[8,128,128]{2,1,0:T(8,128)(2,1)S(1)}, u32[]{:S(2)}, u32[]{:S(2)}) %collective-permute-start.1) | collective-permute-done | bytes 262176 | tf_op jit(solution)/shard_map/ppermute | solution.py:49
  32.5 4.5 %collective-permute-done.2.refs_3_ = bf16[8,128,128]{2,1,0:T(8,128)(2,1)S(1)} collective-permute-done((bf16[8,128,128]{2,1,0:T(8,128)(2,1)S(1)}, bf16[8,128,128]{2,1,0:T(8,128)(2,1)S(1)}, u32[]{:S(2)}, u32[]{:S(2)}) %collective-permute-start.2) | collective-permute-done | bytes 262176 | tf_op jit(solution)/shard_map/ppermute | solution.py:49
  37.0 13.2 %collective-permute-done.4.refs_5_ = bf16[8,128,128]{2,1,0:T(8,128)(2,1)S(1)} collective-permute-done((bf16[8,128,128]{2,1,0:T(8,128)(2,1)S(1)}, bf16[8,128,128]{2,1,0:T(8,128)(2,1)S(1)}, u32[]{:S(2)}, u32[]{:S(2)}) %collective-permute-start.4) | collective-permute-done | bytes 262176 | tf_op jit(solution)/shard_map/ppermute | solution.py:49
  53.1 4.1 %diagonal_sums.1 = (f32[4,4,128,128]{3,2,1,0:T(8,128)S(1)}, f32[4,4,128,128]{3,2,1,0:T(8,128)S(1)}) custom-call(s32[4,1,32]{2,1,0:T(1,128)S(1)} %copy.62.table, bf16[32,128,128]{2,1,0:T(8,128)(2,1)} %merge_panels.2.heads.first), custom_call_target="tpu_custom_call" | custom-call | flops 268435456 | bytes 2097152 | tf_op jit(solution)/shard_map/diagonal_sums/pallas_call | solution.py:251
  57.4 3.5 %split_panels.3 = (bf16[8,128,128]{2,1,0:T(8,128)(2,1)S(1)}, bf16[8,128,128]{2,1,0:T(8,128)(2,1)}, bf16[8,128,128]{2,1,0:T(8,128)(2,1)S(1)}, bf16[8,128,128]{2,1...) custom-call(s32[64]{0:T(128)S(1)} %add.137.index, ...), custom_call_target="tpu_custom_call" | custom-call | bytes 4194304 | tf_op jit(solution)/shard_map/split_panels/pallas_call | solution.py:164
  67.1 13.5 %all-gather = s32[12,8,2]{1,2,0:T(2,128)S(1)} all-gather(s32[3,8,2]{1,2,0:T(2,128)S(1)} %copy-done.10), channel_id=2, replica_groups=mesh['col'=8,'row'=4] {'row'}, dimensions={0}, use_global_device_ids=true | all-gather | bytes 960 | tf_op jit(solution)/shard_map/all_gather | solution.py:570
  84.3 3.2 %collective-permute-done.11.refs_5_ = bf16[8,128,128]{2,1,0:T(8,128)(2,1)} collective-permute-done((bf16[8,128,128]{2,1,0:T(8,128)(2,1)}, bf16[8,128,128]{2,1,0:T(8,128)(2,1)}, u32[]{:S(2)}, u32[]{:S(2)}) %collective-permute-start.11) | collective-permute-done | bytes 262176 | tf_op jit(solution)/shard_map/ppermute | solution.py:49
  92.9 2.5 %tables.1 = s32[304]{0:T(512)} custom-call(s32[2]{0:T(128)} %copy-done.5, s32[4,8]{1,0:T(4,128)} %diag.1, s32[3,8]{1,0:T(4,128)} %parent.1, s32[4,3,8,2]{3,2,1,0:T(8,128)} %bitcast.91), custom_call_target="tpu_custom_call" | custom-call | tf_op jit(solution)/shard_map/tables/pallas_call | solution.py:572
  97.6 5.1 %collective-permute-done.15 = f32[4,128,128]{2,1,0:T(8,128)S(1)} collective-permute-done((f32[4,128,128]{2,1,0:T(8,128)}, f32[4,128,128]{2,1,0:T(8,128)S(1)}, u32[]{:S(2)}, u32[]{:S(2)}) %collective-permute-start.15) | collective-permute-done | bytes 262176 | tf_op jit(solution)/shard_map/ppermute | solution.py:49
  102.7 5.9 %collective-permute-done.17 = f32[4,128,128]{2,1,0:T(8,128)} collective-permute-done((f32[4,128,128]{2,1,0:T(8,128)}, f32[4,128,128]{2,1,0:T(8,128)}, u32[]{:S(2)}, u32[]{:S(2)}) %collective-permute-start.17) | collective-permute-done | bytes 262176 | tf_op jit(solution)/shard_map/ppermute | solution.py:49
  110.4 18.1 %all-gather.3 = f32[4,128,128]{2,1,0:T(8,128)S(1)} all-gather(f32[1,128,128]{2,1,0:T(8,128)S(1)} %known_blocks.3), channel_id=5, replica_groups=mesh['col'=8,'row'=4] {'row'}, dimensions={0}, use_global_device_ids=true | all-gather | bytes 327680 | tf_op jit(solution)/shard_map/all_gather | solution.py:596
  128.5 3.8 %factor.4 = (f32[128,128]{1,0:T(8,128)S(1)}, f32[128,128]{1,0:T(8,128)S(1)}) custom-call(s32[304]{0:T(512)S(1)} %copy-done.4, f32[128,128]{1,0:T(8,128)S(1)} %reduce.1.start), custom_call_target="tpu_custom_call" | custom-call | flops 419430400 | bytes 262144 | tf_op jit(solution)/shard_map/factor/pallas_call | solution.py:452
  132.3 5.1 %all-gather.12.cloned.1.call-done = bf16[128,128,128]{2,1,0:T(8,128)(2,1)} async-done(((bf16[32,128,128]{2,1,0:T(8,128)(2,1)}), bf16[128,128,128]{2,1,0:T(8,128)(2,1)}) %all-gather.12.cloned.1.call-update) | async-done | bytes 4194320 | tf_op jit(solution)/shard_map/all_gather | solution.py:567
  139.6 6.8 %source_sums.1 = (f32[4,4,128,128]{3,2,1,0:T(8,128)S(1)}, f32[4,4,128,128]{3,2,1,0:T(8,128)S(1)}, f32[4,4,128,128]{3,2,1,0:T(8,128)}, f32[4,4,128,128]{3,2,1,0:T(8,128)S(1)}) custom-call(s32[4,4,32]{2,1,0:T(4,128)S(1)} %pad_add_fusion.table, bf16[32,128,128]{2,1,0:T(8,128)(2,1)} %merge_panels.2.heads.first, bf16[32,1,128,128]{3,2,1,0:T(8,128)(2,1)S(1)} %bitcast.75, ...), custom_call_target="tpu_custom_call" | custom-call | flops 1073741824 | bytes 6291456 | tf_op jit(solution)/shard_map/source_sums/pallas_call | solution.py:312
  146.4 2.7 %collective-permute-done.19.other = f32[4,4,128,128]{3,2,1,0:T(8,128)S(1)} collective-permute-done((f32[4,4,128,128]{3,2,1,0:T(8,128)S(1)}, f32[4,4,128,128]{3,2,1,0:T(8,128)S(1)}, u32[]{:S(2)}, u32[]{:S(2)}) %collective-permute-start.19) | collective-permute-done | bytes 1048608 | tf_op jit(solution)/shard_map/ppermute | solution.py:49
  152.8 5.5 %collective-permute-done.20 = f32[4,128,128]{2,1,0:T(8,128)S(1)} collective-permute-done((f32[4,128,128]{2,1,0:T(8,128)S(1)}, f32[4,128,128]{2,1,0:T(8,128)S(1)}, u32[]{:S(2)}, u32[]{:S(2)}) %collective-permute-start.20) | collective-permute-done | bytes 262176 | tf_op jit(solution)/shard_map/ppermute | solution.py:49
  158.4 6.0 %collective-permute-done.21 = f32[4,128,128]{2,1,0:T(8,128)S(1)} collective-permute-done((f32[4,128,128]{2,1,0:T(8,128)S(1)}, f32[4,128,128]{2,1,0:T(8,128)S(1)}, u32[]{:S(2)}, u32[]{:S(2)}) %collective-permute-start.21) | collective-permute-done | bytes 262176 | tf_op jit(solution)/shard_map/ppermute | solution.py:49
  171.7 15.9 %all-gather.5 = bf16[8,128,128]{2,1,0:T(8,128)(2,1)S(1)} all-gather(bf16[2,128,128]{2,1,0:T(8,128)(2,1)S(1)} %get-tuple-element.87.own), channel_id=7, replica_groups=mesh['col'=8,'row'=4] {'row'}, dimensions={0}, use_global_device_ids=true | all-gather | bytes 327680 | tf_op jit(solution)/shard_map/all_gather | solution.py:643
  195.0 2.8 %collective-permute-done.24.refs_2_.refs_3_ = bf16[5,128,128]{2,1,0:T(8,128)(2,1)S(1)} collective-permute-done((bf16[5,128,128]{2,1,0:T(8,128)(2,1)S(1)}, bf16[5,128,128]{2,1,0:T(8,128)(2,1)S(1)}, u32[]{:S(2)}, u32[]{:S(2)}) %collective-permute-start.24) | collective-permute-done | bytes 163872 | tf_op jit(solution)/shard_map/ppermute | solution.py:49
  199.7 4.1 %factor.5 = (f32[128,128]{1,0:T(8,128)S(1)}, f32[128,128]{1,0:T(8,128)S(1)}) custom-call(s32[304]{0:T(512)S(1)} %copy-done.4, f32[128,128]{1,0:T(8,128)S(1)} %get-tuple-element.109.start, bf16[5,128,128]{2,1,0:T(8,128)(2,1)S(1)} %first_message.1.refs_0_.refs_1_, bf16[5,128,128]{2,1,0:T(8,128)(2,1)S(1)} %collective-permute-done.23.refs_1_.refs_2_, ...), custom_call_target="tpu_custom_call" | custom-call | flops 419430400 | bytes 262144 | tf_op jit(solution)/shard_map/factor/pallas_call | solution.py:452
  216.1 3.8 %factor.6 = (f32[128,128]{1,0:T(8,128)S(1)}, f32[128,128]{1,0:T(8,128)S(1)}) custom-call(s32[304]{0:T(512)S(1)} %copy-done.4, f32[128,128]{1,0:T(8,128)S(1)} %get-tuple-element.110.start, bf16[4,128,128]{2,1,0:T(8,128)(2,1)S(1)} %get-tuple-element.94.refs_0_.refs_1_, bf16[4,128,128]{2,1,0:T(8,128)(2,1)S(1)} %collective-permute-done.33.refs_1_.refs_2_, ...), custom_call_target="tpu_custom_call" | custom-call | flops 419430400 | bytes 262144 | tf_op jit(solution)/shard_map/factor/pallas_call | solution.py:452
  219.9 4.3 %all-gather.16.cloned.1.call-done = f32[16,128,128]{2,1,0:T(8,128)} async-done(((f32[4,128,128]{2,1,0:T(8,128)}), f32[16,128,128]{2,1,0:T(8,128)}) %all-gather.16.cloned.1.call-update) | async-done | bytes 1048592 | tf_op jit(solution)/shard_map/all_gather | solution.py:652
  236.7 4.3 %factor.7 = (f32[128,128]{1,0:T(8,128)S(1)}, f32[128,128]{1,0:T(8,128)S(1)}) custom-call(s32[304]{0:T(512)S(1)} %copy-done.4, f32[128,128]{1,0:T(8,128)S(1)} %get-tuple-element.104.start, bf16[3,128,128]{2,1,0:T(8,128)(2,1)S(1)} %get-tuple-element.98.refs_0_, bf16[3,128,128]{2,1,0:T(8,128)(2,1)S(1)} %collective-permute-done.40.refs_1_, ...), custom_call_target="tpu_custom_call" | custom-call | flops 419430400 | bytes 262144 | tf_op jit(solution)/shard_map/factor/pallas_call | solution.py:452
  (171 shorter events, 82.5 us)
Async XLA Ops:
  6.5 130.8 %all-gather.12.cloned.1.call-start = ((), (), s32[]{:S(2)}) async-start(), calls=%async_computation | async-start | bytes 5242880 | tf_op jit(solution)/shard_map/all_gather | solution.py:567
  24.7 12.3 %collective-permute-start.2 = (bf16[8,128,128]{2,1,0:T(8,128)(2,1)S(1)}, bf16[8,128,128]{2,1,0:T(8,128)(2,1)S(1)}, u32[]{:S(2)}, u32[]{:S(2)}) collective-permute-start(bf16[8,128,128]{2,1,0:T(8,128)(2,1)S(1)} %get-tuple-element.56), channel_id=1, source_target_pairs={{0,12},{4,8},{8,4},{12,0},{16,28},{20,24},{24,20},{28,16},{1,13},{... | collective-permute-start | bytes 786440 | tf_op jit(solution)/shard_map/ppermute | solution.py:49
  24.7 12.2 %collective-permute-start.3 = (bf16[8,128,128]{2,1,0:T(8,128)(2,1)S(1)}, bf16[8,128,128]{2,1,0:T(8,128)(2,1)S(1)}, u32[]{:S(2)}, u32[]{:S(2)}) collective-permute-start(bf16[8,128,128]{2,1,0:T(8,128)(2,1)S(1)} %get-tuple-element.57), channel_id=1, source_target_pairs={{0,16},{4,20},{8,24},{12,28},{16,0},{20,4},{24,8},{28,12},{1,17},{... | collective-permute-start | bytes 786440 | tf_op jit(solution)/shard_map/ppermute | solution.py:49
  26.2 23.9 %collective-permute-start.4 = (bf16[8,128,128]{2,1,0:T(8,128)(2,1)S(1)}, bf16[8,128,128]{2,1,0:T(8,128)(2,1)S(1)}, u32[]{:S(2)}, u32[]{:S(2)}) collective-permute-start(bf16[8,128,128]{2,1,0:T(8,128)(2,1)S(1)} %get-tuple-element.58), channel_id=1, source_target_pairs={{0,20},{4,16},{8,28},{12,24},{16,4},{20,0},{24,12},{28,8},{1,21},{... | collective-permute-start | bytes 786440 | tf_op jit(solution)/shard_map/ppermute | solution.py:49
  26.8 23.3 %collective-permute-start.5 = (bf16[8,128,128]{2,1,0:T(8,128)(2,1)S(1)}, bf16[8,128,128]{2,1,0:T(8,128)(2,1)S(1)}, u32[]{:S(2)}, u32[]{:S(2)}) collective-permute-start(bf16[8,128,128]{2,1,0:T(8,128)(2,1)S(1)} %get-tuple-element.59), channel_id=1, source_target_pairs={{0,24},{4,28},{8,16},{12,20},{16,8},{20,12},{24,0},{28,4},{1,25},{... | collective-permute-start | bytes 786440 | tf_op jit(solution)/shard_map/ppermute | solution.py:49
  32.3 17.8 %collective-permute-start.6 = (bf16[8,128,128]{2,1,0:T(8,128)(2,1)S(1)}, bf16[8,128,128]{2,1,0:T(8,128)(2,1)S(1)}, u32[]{:S(2)}, u32[]{:S(2)}) collective-permute-start(bf16[8,128,128]{2,1,0:T(8,128)(2,1)S(1)} %get-tuple-element.60), channel_id=1, source_target_pairs={{0,28},{4,24},{8,20},{12,16},{16,12},{20,8},{24,4},{28,0},{1,29},{... | collective-permute-start | bytes 786440 | tf_op jit(solution)/shard_map/ppermute | solution.py:49
  51.9 146.4 %all-gather.14.cloned.1.call-start = ((), (), s32[]{:S(2)}) async-start(), calls=%async_computation.1 | async-start | bytes 1310720 | tf_op jit(solution)/shard_map/all_gather | solution.py:619
  57.2 9.5 %collective-permute-start.14 = (f32[4,4,128,128]{3,2,1,0:T(8,128)S(1)}, f32[4,4,128,128]{3,2,1,0:T(8,128)S(1)}, u32[]{:S(2)}, u32[]{:S(2)}) collective-permute-start(f32[4,4,128,128]{3,2,1,0:T(8,128)S(1)} %get-tuple-element.70), channel_id=1, source_target_pairs={{0,4},{4,0},{8,12},{12,8},{16,20},{20,16},{24,28},{28,24},{1,5},{5... | collective-permute-start | bytes 3145736 | tf_op jit(solution)/shard_map/ppermute | solution.py:49
  62.3 20.6 %collective-permute-start.10 = (bf16[8,128,128]{2,1,0:T(8,128)(2,1)}, bf16[8,128,128]{2,1,0:T(8,128)(2,1)S(1)}, u32[]{:S(2)}, u32[]{:S(2)}) collective-permute-start(bf16[8,128,128]{2,1,0:T(8,128)(2,1)} %get-tuple-element.65), channel_id=1, source_target_pairs={{0,16},{4,20},{8,24},{12,28},{16,0},{20,4},{24,8},{28,12},{1,17},{... | collective-permute-start | bytes 786440 | tf_op jit(solution)/shard_map/ppermute | solution.py:49
  63.7 23.8 %collective-permute-start.11 = (bf16[8,128,128]{2,1,0:T(8,128)(2,1)}, bf16[8,128,128]{2,1,0:T(8,128)(2,1)}, u32[]{:S(2)}, u32[]{:S(2)}) collective-permute-start(bf16[8,128,128]{2,1,0:T(8,128)(2,1)} %get-tuple-element.66), channel_id=1, source_target_pairs={{0,20},{4,16},{8,28},{12,24},{16,4},{20,0},{24,12},{28,8},{1,21},{... | collective-permute-start | bytes 786440 | tf_op jit(solution)/shard_map/ppermute | solution.py:49
  64.0 25.2 %collective-permute-start.12 = (bf16[8,128,128]{2,1,0:T(8,128)(2,1)}, bf16[8,128,128]{2,1,0:T(8,128)(2,1)}, u32[]{:S(2)}, u32[]{:S(2)}) collective-permute-start(bf16[8,128,128]{2,1,0:T(8,128)(2,1)} %get-tuple-element.67), channel_id=1, source_target_pairs={{0,24},{4,28},{8,16},{12,20},{16,8},{20,12},{24,0},{28,4},{1,25},{... | collective-permute-start | bytes 786440 | tf_op jit(solution)/shard_map/ppermute | solution.py:49
  65.3 24.5 %collective-permute-start.13 = (bf16[8,128,128]{2,1,0:T(8,128)(2,1)}, bf16[8,128,128]{2,1,0:T(8,128)(2,1)}, u32[]{:S(2)}, u32[]{:S(2)}) collective-permute-start(bf16[8,128,128]{2,1,0:T(8,128)(2,1)} %get-tuple-element.68), channel_id=1, source_target_pairs={{0,28},{4,24},{8,20},{12,16},{16,12},{20,8},{24,4},{28,0},{1,29},{... | collective-permute-start | bytes 786440 | tf_op jit(solution)/shard_map/ppermute | solution.py:49
  66.7 24.6 %collective-permute-start.7 = (bf16[8,128,128]{2,1,0:T(8,128)(2,1)}, bf16[8,128,128]{2,1,0:T(8,128)(2,1)}, u32[]{:S(2)}, u32[]{:S(2)}) collective-permute-start(bf16[8,128,128]{2,1,0:T(8,128)(2,1)} %get-tuple-element.62), channel_id=1, source_target_pairs={{0,4},{4,0},{8,12},{12,8},{16,20},{20,16},{24,28},{28,24},{1,5},{5... | collective-permute-start | bytes 786440 | tf_op jit(solution)/shard_map/ppermute | solution.py:49
  82.9 12.6 %collective-permute-start.8 = (bf16[8,128,128]{2,1,0:T(8,128)(2,1)}, bf16[8,128,128]{2,1,0:T(8,128)(2,1)S(1)}, u32[]{:S(2)}, u32[]{:S(2)}) collective-permute-start(bf16[8,128,128]{2,1,0:T(8,128)(2,1)} %copy-done.8), channel_id=1, source_target_pairs={{0,8},{4,12},{8,0},{12,4},{16,24},{20,28},{24,16},{28,20},{1,9},{5... | collective-permute-start | bytes 786440 | tf_op jit(solution)/shard_map/ppermute | solution.py:49
  89.3 13.5 %collective-permute-start.15 = (f32[4,128,128]{2,1,0:T(8,128)}, f32[4,128,128]{2,1,0:T(8,128)S(1)}, u32[]{:S(2)}, u32[]{:S(2)}) collective-permute-start(f32[4,128,128]{2,1,0:T(8,128)} %get-tuple-element.72), channel_id=1, source_target_pairs={{0,8},{4,12},{8,0},{12,4},{16,24},{20,28},{24,16},{28,20},{1,9},{5... | collective-permute-start | bytes 786440 | tf_op jit(solution)/shard_map/ppermute | solution.py:49
  89.8 12.9 %collective-permute-start.16 = (f32[4,128,128]{2,1,0:T(8,128)}, f32[4,128,128]{2,1,0:T(8,128)}, u32[]{:S(2)}, u32[]{:S(2)}) collective-permute-start(f32[4,128,128]{2,1,0:T(8,128)} %get-tuple-element.73), channel_id=1, source_target_pairs={{0,16},{4,20},{8,24},{12,28},{16,0},{20,4},{24,8},{28,12},{1,17},{... | collective-permute-start | bytes 786440 | tf_op jit(solution)/shard_map/ppermute | solution.py:49
  91.3 17.4 %collective-permute-start.17 = (f32[4,128,128]{2,1,0:T(8,128)}, f32[4,128,128]{2,1,0:T(8,128)}, u32[]{:S(2)}, u32[]{:S(2)}) collective-permute-start(f32[4,128,128]{2,1,0:T(8,128)} %get-tuple-element.74), channel_id=1, source_target_pairs={{0,24},{4,28},{8,16},{12,20},{16,8},{20,12},{24,0},{28,4},{1,25},{... | collective-permute-start | bytes 786440 | tf_op jit(solution)/shard_map/ppermute | solution.py:49
  150.7 13.7 %collective-permute-start.21 = (f32[4,128,128]{2,1,0:T(8,128)S(1)}, f32[4,128,128]{2,1,0:T(8,128)S(1)}, u32[]{:S(2)}, u32[]{:S(2)}) collective-permute-start(f32[4,128,128]{2,1,0:T(8,128)S(1)} %get-tuple-element.82), channel_id=1, source_target_pairs={{0,16},{4,20},{8,24},{12,28},{16,0},{20,4},{24,8},{28,12},{1,17},{... | collective-permute-start | bytes 786440 | tf_op jit(solution)/shard_map/ppermute | solution.py:49
  152.1 12.2 %collective-permute-start.22 = (f32[4,128,128]{2,1,0:T(8,128)S(1)}, f32[4,128,128]{2,1,0:T(8,128)S(1)}, u32[]{:S(2)}, u32[]{:S(2)}) collective-permute-start(f32[4,128,128]{2,1,0:T(8,128)S(1)} %get-tuple-element.83), channel_id=1, source_target_pairs={{0,24},{4,28},{8,16},{12,20},{16,8},{20,12},{24,0},{28,4},{1,25},{... | collective-permute-start | bytes 786440 | tf_op jit(solution)/shard_map/ppermute | solution.py:49
  152.7 13.1 %collective-permute-start.18 = (f32[4,4,128,128]{3,2,1,0:T(8,128)}, f32[4,4,128,128]{3,2,1,0:T(8,128)}, u32[]{:S(2)}, u32[]{:S(2)}) collective-permute-start(f32[4,4,128,128]{3,2,1,0:T(8,128)} %get-tuple-element.77), channel_id=1, source_target_pairs={{0,4},{4,0},{8,12},{12,8},{16,20},{20,16},{24,28},{28,24},{1,5},{5... | collective-permute-start | bytes 3145736 | tf_op jit(solution)/shard_map/ppermute | solution.py:49
  165.8 58.4 %all-gather.16.cloned.1.call-start = ((), (), s32[]{:S(2)}) async-start(), calls=%async_computation.2 | async-start | bytes 1310720 | tf_op jit(solution)/shard_map/all_gather | solution.py:652
  167.3 20.3 %collective-permute-start.30 = (f32[4,128,128]{2,1,0:T(8,128)S(1)}, f32[4,128,128]{2,1,0:T(8,128)S(1)}, u32[]{:S(2)}, u32[]{:S(2)}) collective-permute-start(f32[4,128,128]{2,1,0:T(8,128)S(1)} %get-tuple-element.91), channel_id=1, source_target_pairs={{0,8},{4,12},{8,0},{12,4},{16,24},{20,28},{24,16},{28,20},{1,9},{5... | collective-permute-start | bytes 786440 | tf_op jit(solution)/shard_map/ppermute | solution.py:49
  168.5 19.1 %collective-permute-start.31 = (f32[4,128,128]{2,1,0:T(8,128)S(1)}, f32[4,128,128]{2,1,0:T(8,128)S(1)}, u32[]{:S(2)}, u32[]{:S(2)}) collective-permute-start(f32[4,128,128]{2,1,0:T(8,128)S(1)} %get-tuple-element.92), channel_id=1, source_target_pairs={{0,16},{4,20},{8,24},{12,28},{16,0},{20,4},{24,8},{28,12},{1,17},{... | collective-permute-start | bytes 786440 | tf_op jit(solution)/shard_map/ppermute | solution.py:49
  169.4 18.2 %collective-permute-start.32 = (f32[4,128,128]{2,1,0:T(8,128)S(1)}, f32[4,128,128]{2,1,0:T(8,128)S(1)}, u32[]{:S(2)}, u32[]{:S(2)}) collective-permute-start(f32[4,128,128]{2,1,0:T(8,128)S(1)} %get-tuple-element.93), channel_id=1, source_target_pairs={{0,24},{4,28},{8,16},{12,20},{16,8},{20,12},{24,0},{28,4},{1,25},{... | collective-permute-start | bytes 786440 | tf_op jit(solution)/shard_map/ppermute | solution.py:49
  (37 other events, 268.1 us)
Sparse Core Ops, SparseCore 0:
  52.0 85.3 all-gather.11
  165.9 30.0 all-gather.13
  197.6 26.5 all-gather.15

commit v5 on v4

--- a/solution.py
+++ b/solution.py
@@ -324,7 +324,7 @@
             scratch_shapes=[pltpu.VMEM((2 * chips, sections * blocks, width, width), F32)],
         ),
         out_shape=[jax.ShapeDtypeStruct(shape, F32) for shape in shapes],
-        compiler_params=params(6 * size // MIB + 26),
+        compiler_params=params(6 * size // MIB + 38),
         cost_estimate=cost(
             count * blocks * width * width * width * 2 * sections, count * width * width * 12
         ),

time: 251 us -> 249 us (level)
    unnamed x22 -> x26, local copies, waits for them, and re-layouts: 6.07 us -> 3.48 us
    all_gather x1, waiting for transfers between devices: 5.08 us -> 7.61 us  [local(): heads = lax.all_gather(first, 'row', axis=0)]
  transfers between devices with their start and end apart: 50 -> 50, of which waited for: 23 -> 24; matrix products, arithmetic and copies ran while one was open for 2% -> 1% of each run, Pallas kernels for 13% -> 12%
where the time goes in v5:
time: 249 us; the launch traced here: 248 us
  waiting for transfers between devices  80.2 us (32%)
  blocking collectives  58 us (23%)
  Pallas kernels  49.7 us (20%)
  starting transfers between devices  35.5 us (14%)
  between operations  14.2 us (6%)
  local copies, waits for them, and re-layouts  6.61 us (3%)
  other arithmetic  3.8 us (2%)
    ppermute x47, waiting for transfers between devices, swap(): return lax.ppermute(x, axis, [(i, i ^ mask) for i in range(size)])  67.7 us
    ppermute x47, starting transfers between devices, swap(): return lax.ppermute(x, axis, [(i, i ^ mask) for i in range(size)])  35.4 us
    all_gather x1, blocking collectives, share(): return jnp.sum(lax.all_gather(x, 'row', axis=0), axis=0)  18.1 us
    pallas_call x4, Pallas kernels, factor(): pl.pallas_call(functools.partial(factor_kernel, step, layout), in_specs=[...  15.9 us
    all_gather x1, blocking collectives, local(): whole = lax.all_gather(message, 'row', axis=0)  15.7 us
    all_gather x1, blocking collectives, local(): chain = lax.all_gather(chain_map[None], 'row', axis=0, tiled=True)  13.5 us
    all_gather x1, blocking collectives, local(): facts = lax.all_gather(facts, 'col', axis=0)  10.7 us
    pallas_call x1, Pallas kernels, source_sums(): pl.pallas_call(functools.partial(source_kernel, soon), grid_spec=pltpu.Pr...  7.98 us
  transfers between devices with their start and end apart: 50, of which 24 were waited for; matrix products, arithmetic and copies ran while one was open for 1% of the time, Pallas kernels for 12%

profile of v5, /device:TPU:0, one launch (start us, length us, event | category | flops | bytes accessed | tf_op | source)
XLA Modules:
  0.0 248.0 jit_solution(14725575213866118754)
XLA Ops:
  8.0 10.7 %all-gather.7 = s32[8,13,64]{2,1,0:T(8,128)S(1)} all-gather(s32[1,13,64]{2,1,0:T(8,128)S(1)} %add_bitcast_fusion), channel_id=3, replica_groups=mesh['col'=8,'row'=4] {'col'}, dimensions={0}, use_global_device_ids=true | all-gather | bytes 29952 | tf_op jit(solution)/shard_map/all_gather | solution.py:543
  28.3 4.0 %collective-permute-done.1.refs_2_ = bf16[8,128,128]{2,1,0:T(8,128)(2,1)S(1)} collective-permute-done((bf16[8,128,128]{2,1,0:T(8,128)(2,1)S(1)}, bf16[8,128,128]{2,1,0:T(8,128)(2,1)S(1)}, u32[]{:S(2)}, u32[]{:S(2)}) %collective-permute-start.1) | collective-permute-done | bytes 262176 | tf_op jit(solution)/shard_map/ppermute | solution.py:49
  32.5 4.5 %collective-permute-done.2.refs_3_ = bf16[8,128,128]{2,1,0:T(8,128)(2,1)S(1)} collective-permute-done((bf16[8,128,128]{2,1,0:T(8,128)(2,1)S(1)}, bf16[8,128,128]{2,1,0:T(8,128)(2,1)S(1)}, u32[]{:S(2)}, u32[]{:S(2)}) %collective-permute-start.2) | collective-permute-done | bytes 262176 | tf_op jit(solution)/shard_map/ppermute | solution.py:49
  37.0 13.2 %collective-permute-done.4.refs_5_ = bf16[8,128,128]{2,1,0:T(8,128)(2,1)S(1)} collective-permute-done((bf16[8,128,128]{2,1,0:T(8,128)(2,1)S(1)}, bf16[8,128,128]{2,1,0:T(8,128)(2,1)S(1)}, u32[]{:S(2)}, u32[]{:S(2)}) %collective-permute-start.4) | collective-permute-done | bytes 262176 | tf_op jit(solution)/shard_map/ppermute | solution.py:49
  53.1 4.1 %diagonal_sums.1 = (f32[4,4,128,128]{3,2,1,0:T(8,128)S(1)}, f32[4,4,128,128]{3,2,1,0:T(8,128)S(1)}) custom-call(s32[4,1,32]{2,1,0:T(1,128)S(1)} %copy.62.table, bf16[32,128,128]{2,1,0:T(8,128)(2,1)} %merge_panels.2.heads.first), custom_call_target="tpu_custom_call" | custom-call | flops 268435456 | bytes 2097152 | tf_op jit(solution)/shard_map/diagonal_sums/pallas_call | solution.py:251
  57.4 3.5 %split_panels.3 = (bf16[8,128,128]{2,1,0:T(8,128)(2,1)S(1)}, bf16[8,128,128]{2,1,0:T(8,128)(2,1)}, bf16[8,128,128]{2,1,0:T(8,128)(2,1)S(1)}, bf16[8,128,128]{2,1...) custom-call(s32[64]{0:T(128)S(1)} %add.137.index, ...), custom_call_target="tpu_custom_call" | custom-call | bytes 4194304 | tf_op jit(solution)/shard_map/split_panels/pallas_call | solution.py:164
  65.9 13.5 %all-gather = s32[12,8,2]{1,2,0:T(2,128)S(1)} all-gather(s32[3,8,2]{1,2,0:T(2,128)S(1)} %copy-done.12), channel_id=2, replica_groups=mesh['col'=8,'row'=4] {'row'}, dimensions={0}, use_global_device_ids=true | all-gather | bytes 960 | tf_op jit(solution)/shard_map/all_gather | solution.py:570
  83.0 3.3 %collective-permute-done.11.refs_5_ = bf16[8,128,128]{2,1,0:T(8,128)(2,1)} collective-permute-done((bf16[8,128,128]{2,1,0:T(8,128)(2,1)}, bf16[8,128,128]{2,1,0:T(8,128)(2,1)}, u32[]{:S(2)}, u32[]{:S(2)}) %collective-permute-start.11) | collective-permute-done | bytes 262176 | tf_op jit(solution)/shard_map/ppermute | solution.py:49
  97.3 4.1 %collective-permute-done.15 = f32[4,128,128]{2,1,0:T(8,128)S(1)} collective-permute-done((f32[4,128,128]{2,1,0:T(8,128)}, f32[4,128,128]{2,1,0:T(8,128)S(1)}, u32[]{:S(2)}, u32[]{:S(2)}) %collective-permute-start.15) | collective-permute-done | bytes 262176 | tf_op jit(solution)/shard_map/ppermute | solution.py:49
  101.5 5.8 %collective-permute-done.17 = f32[4,128,128]{2,1,0:T(8,128)S(1)} collective-permute-done((f32[4,128,128]{2,1,0:T(8,128)}, f32[4,128,128]{2,1,0:T(8,128)S(1)}, u32[]{:S(2)}, u32[]{:S(2)}) %collective-permute-start.17) | collective-permute-done | bytes 262176 | tf_op jit(solution)/shard_map/ppermute | solution.py:49
  107.9 18.1 %all-gather.3 = f32[4,128,128]{2,1,0:T(8,128)S(1)} all-gather(f32[1,128,128]{2,1,0:T(8,128)S(1)} %known_blocks.3), channel_id=5, replica_groups=mesh['col'=8,'row'=4] {'row'}, dimensions={0}, use_global_device_ids=true | all-gather | bytes 327680 | tf_op jit(solution)/shard_map/all_gather | solution.py:596
  126.0 3.8 %factor.4 = (f32[128,128]{1,0:T(8,128)S(1)}, f32[128,128]{1,0:T(8,128)S(1)}) custom-call(s32[304]{0:T(512)S(1)} %copy-done.5, f32[128,128]{1,0:T(8,128)S(1)} %reduce.1.start), custom_call_target="tpu_custom_call" | custom-call | flops 419430400 | bytes 262144 | tf_op jit(solution)/shard_map/factor/pallas_call | solution.py:452
  129.8 7.6 %all-gather.12.cloned.1.call-done = bf16[128,128,128]{2,1,0:T(8,128)(2,1)} async-done(((bf16[32,128,128]{2,1,0:T(8,128)(2,1)}), bf16[128,128,128]{2,1,0:T(8,128)(2,1)}) %all-gather.12.cloned.1.call-update) | async-done | bytes 4194320 | tf_op jit(solution)/shard_map/all_gather | solution.py:567
  137.4 8.0 %source_sums.1 = (f32[4,4,128,128]{3,2,1,0:T(8,128)S(1)}, f32[4,4,128,128]{3,2,1,0:T(8,128)S(1)}, f32[4,4,128,128]{3,2,1,0:T(8,128)}, f32[4,4,128,128]{3,2,1,0:T(8,128)}) custom-call(s32[4,4,32]{2,1,0:T(4,128)S(1)} %pad_add_fusion.table, bf16[32,128,128]{2,1,0:T(8,128)(2,1)} %merge_panels.2.heads.first, bf16[32,1,128,128]{3,2,1,0:T(8,128)(2,1)} %bitcast.75, ...), custom_call_target="tpu_custom_call" | custom-call | flops 1073741824 | bytes 6291456 | tf_op jit(solution)/shard_map/source_sums/pallas_call | solution.py:312
  145.4 2.7 %collective-permute-done.19.other = f32[4,4,128,128]{3,2,1,0:T(8,128)S(1)} collective-permute-done((f32[4,4,128,128]{3,2,1,0:T(8,128)S(1)}, f32[4,4,128,128]{3,2,1,0:T(8,128)S(1)}, u32[]{:S(2)}, u32[]{:S(2)}) %collective-permute-start.19) | collective-permute-done | bytes 1048608 | tf_op jit(solution)/shard_map/ppermute | solution.py:49
  152.4 4.9 %collective-permute-done.20 = f32[4,128,128]{2,1,0:T(8,128)S(1)} collective-permute-done((f32[4,128,128]{2,1,0:T(8,128)S(1)}, f32[4,128,128]{2,1,0:T(8,128)S(1)}, u32[]{:S(2)}, u32[]{:S(2)}) %collective-permute-start.20) | collective-permute-done | bytes 262176 | tf_op jit(solution)/shard_map/ppermute | solution.py:49
  157.4 6.0 %collective-permute-done.21 = f32[4,128,128]{2,1,0:T(8,128)S(1)} collective-permute-done((f32[4,128,128]{2,1,0:T(8,128)S(1)}, f32[4,128,128]{2,1,0:T(8,128)S(1)}, u32[]{:S(2)}, u32[]{:S(2)}) %collective-permute-start.21) | collective-permute-done | bytes 262176 | tf_op jit(solution)/shard_map/ppermute | solution.py:49
  169.4 15.7 %all-gather.5 = bf16[8,128,128]{2,1,0:T(8,128)(2,1)S(1)} all-gather(bf16[2,128,128]{2,1,0:T(8,128)(2,1)S(1)} %get-tuple-element.87.own), channel_id=7, replica_groups=mesh['col'=8,'row'=4] {'row'}, dimensions={0}, use_global_device_ids=true | all-gather | bytes 327680 | tf_op jit(solution)/shard_map/all_gather | solution.py:643
  196.9 4.1 %factor.5 = (f32[128,128]{1,0:T(8,128)S(1)}, f32[128,128]{1,0:T(8,128)S(1)}) custom-call(s32[304]{0:T(512)S(1)} %copy-done.5, f32[128,128]{1,0:T(8,128)S(1)} %get-tuple-element.109.start, bf16[5,128,128]{2,1,0:T(8,128)(2,1)S(1)} %first_message.1.refs_0_.refs_1_, bf16[5,128,128]{2,1,0:T(8,128)(2,1)S(1)} %collective-permute-done.23.refs_1_.refs_2_, ...), custom_call_target="tpu_custom_call" | custom-call | flops 419430400 | bytes 262144 | tf_op jit(solution)/shard_map/factor/pallas_call | solution.py:452
  206.2 2.8 %collective-permute-done.33.refs_1_.refs_2_ = bf16[4,128,128]{2,1,0:T(8,128)(2,1)S(1)} collective-permute-done((bf16[4,128,128]{2,1,0:T(8,128)(2,1)S(1)}, bf16[4,128,128]{2,1,0:T(8,128)(2,1)S(1)}, u32[]{:S(2)}, u32[]{:S(2)}) %collective-permute-start.33) | collective-permute-done | bytes 131104 | tf_op jit(solution)/shard_map/ppermute | solution.py:49
  209.0 3.1 %collective-permute-done.34.refs_2_.refs_3_ = bf16[4,128,128]{2,1,0:T(8,128)(2,1)S(1)} collective-permute-done((bf16[4,128,128]{2,1,0:T(8,128)(2,1)S(1)}, bf16[4,128,128]{2,1,0:T(8,128)(2,1)S(1)}, u32[]{:S(2)}, u32[]{:S(2)}) %collective-permute-start.34) | collective-permute-done | bytes 131104 | tf_op jit(solution)/shard_map/ppermute | solution.py:49
  213.7 4.1 %factor.6 = (f32[128,128]{1,0:T(8,128)S(1)}, f32[128,128]{1,0:T(8,128)S(1)}) custom-call(s32[304]{0:T(512)S(1)} %copy-done.5, f32[128,128]{1,0:T(8,128)S(1)} %get-tuple-element.110.start, bf16[4,128,128]{2,1,0:T(8,128)(2,1)S(1)} %get-tuple-element.94.refs_0_.refs_1_, bf16[4,128,128]{2,1,0:T(8,128)(2,1)S(1)} %collective-permute-done.33.refs_1_.refs_2_, ...), custom_call_target="tpu_custom_call" | custom-call | flops 419430400 | bytes 262144 | tf_op jit(solution)/shard_map/factor/pallas_call | solution.py:452
  217.8 4.8 %all-gather.16.cloned.1.call-done = f32[16,128,128]{2,1,0:T(8,128)} async-done(((f32[4,128,128]{2,1,0:T(8,128)}), f32[16,128,128]{2,1,0:T(8,128)}) %all-gather.16.cloned.1.call-update) | async-done | bytes 1048592 | tf_op jit(solution)/shard_map/all_gather | solution.py:652
  235.5 4.0 %factor.7 = (f32[128,128]{1,0:T(8,128)S(1)}, f32[128,128]{1,0:T(8,128)S(1)}) custom-call(s32[304]{0:T(512)S(1)} %copy-done.5, f32[128,128]{1,0:T(8,128)S(1)} %get-tuple-element.104.start, bf16[3,128,128]{2,1,0:T(8,128)(2,1)S(1)} %get-tuple-element.98.refs_0_, bf16[3,128,128]{2,1,0:T(8,128)(2,1)S(1)} %collective-permute-done.40.refs_1_, ...), custom_call_target="tpu_custom_call" | custom-call | flops 419430400 | bytes 262144 | tf_op jit(solution)/shard_map/factor/pallas_call | solution.py:452
  (175 shorter events, 77.4 us)
Async XLA Ops:
  6.5 130.9 %all-gather.12.cloned.1.call-start = ((), (), s32[]{:S(2)}) async-start(), calls=%async_computation | async-start | bytes 5242880 | tf_op jit(solution)/shard_map/all_gather | solution.py:567
  24.7 12.3 %collective-permute-start.2 = (bf16[8,128,128]{2,1,0:T(8,128)(2,1)S(1)}, bf16[8,128,128]{2,1,0:T(8,128)(2,1)S(1)}, u32[]{:S(2)}, u32[]{:S(2)}) collective-permute-start(bf16[8,128,128]{2,1,0:T(8,128)(2,1)S(1)} %get-tuple-element.56), channel_id=1, source_target_pairs={{0,12},{4,8},{8,4},{12,0},{16,28},{20,24},{24,20},{28,16},{1,13},{... | collective-permute-start | bytes 786440 | tf_op jit(solution)/shard_map/ppermute | solution.py:49
  24.7 12.2 %collective-permute-start.3 = (bf16[8,128,128]{2,1,0:T(8,128)(2,1)S(1)}, bf16[8,128,128]{2,1,0:T(8,128)(2,1)S(1)}, u32[]{:S(2)}, u32[]{:S(2)}) collective-permute-start(bf16[8,128,128]{2,1,0:T(8,128)(2,1)S(1)} %get-tuple-element.57), channel_id=1, source_target_pairs={{0,16},{4,20},{8,24},{12,28},{16,0},{20,4},{24,8},{28,12},{1,17},{... | collective-permute-start | bytes 786440 | tf_op jit(solution)/shard_map/ppermute | solution.py:49
  26.2 23.9 %collective-permute-start.4 = (bf16[8,128,128]{2,1,0:T(8,128)(2,1)S(1)}, bf16[8,128,128]{2,1,0:T(8,128)(2,1)S(1)}, u32[]{:S(2)}, u32[]{:S(2)}) collective-permute-start(bf16[8,128,128]{2,1,0:T(8,128)(2,1)S(1)} %get-tuple-element.58), channel_id=1, source_target_pairs={{0,20},{4,16},{8,28},{12,24},{16,4},{20,0},{24,12},{28,8},{1,21},{... | collective-permute-start | bytes 786440 | tf_op jit(solution)/shard_map/ppermute | solution.py:49
  26.8 23.3 %collective-permute-start.5 = (bf16[8,128,128]{2,1,0:T(8,128)(2,1)S(1)}, bf16[8,128,128]{2,1,0:T(8,128)(2,1)S(1)}, u32[]{:S(2)}, u32[]{:S(2)}) collective-permute-start(bf16[8,128,128]{2,1,0:T(8,128)(2,1)S(1)} %get-tuple-element.59), channel_id=1, source_target_pairs={{0,24},{4,28},{8,16},{12,20},{16,8},{20,12},{24,0},{28,4},{1,25},{... | collective-permute-start | bytes 786440 | tf_op jit(solution)/shard_map/ppermute | solution.py:49
  32.3 17.8 %collective-permute-start.6 = (bf16[8,128,128]{2,1,0:T(8,128)(2,1)S(1)}, bf16[8,128,128]{2,1,0:T(8,128)(2,1)S(1)}, u32[]{:S(2)}, u32[]{:S(2)}) collective-permute-start(bf16[8,128,128]{2,1,0:T(8,128)(2,1)S(1)} %get-tuple-element.60), channel_id=1, source_target_pairs={{0,28},{4,24},{8,20},{12,16},{16,12},{20,8},{24,4},{28,0},{1,29},{... | collective-permute-start | bytes 786440 | tf_op jit(solution)/shard_map/ppermute | solution.py:49
  51.9 143.6 %all-gather.14.cloned.1.call-start = ((), (), s32[]{:S(2)}) async-start(), calls=%async_computation.1 | async-start | bytes 1310720 | tf_op jit(solution)/shard_map/all_gather | solution.py:619
  60.9 20.6 %collective-permute-start.10 = (bf16[8,128,128]{2,1,0:T(8,128)(2,1)}, bf16[8,128,128]{2,1,0:T(8,128)(2,1)S(1)}, u32[]{:S(2)}, u32[]{:S(2)}) collective-permute-start(bf16[8,128,128]{2,1,0:T(8,128)(2,1)} %get-tuple-element.65), channel_id=1, source_target_pairs={{0,16},{4,20},{8,24},{12,28},{16,0},{20,4},{24,8},{28,12},{1,17},{... | collective-permute-start | bytes 786440 | tf_op jit(solution)/shard_map/ppermute | solution.py:49
  62.4 23.9 %collective-permute-start.11 = (bf16[8,128,128]{2,1,0:T(8,128)(2,1)}, bf16[8,128,128]{2,1,0:T(8,128)(2,1)}, u32[]{:S(2)}, u32[]{:S(2)}) collective-permute-start(bf16[8,128,128]{2,1,0:T(8,128)(2,1)} %get-tuple-element.66), channel_id=1, source_target_pairs={{0,20},{4,16},{8,28},{12,24},{16,4},{20,0},{24,12},{28,8},{1,21},{... | collective-permute-start | bytes 786440 | tf_op jit(solution)/shard_map/ppermute | solution.py:49
  62.7 25.2 %collective-permute-start.12 = (bf16[8,128,128]{2,1,0:T(8,128)(2,1)}, bf16[8,128,128]{2,1,0:T(8,128)(2,1)}, u32[]{:S(2)}, u32[]{:S(2)}) collective-permute-start(bf16[8,128,128]{2,1,0:T(8,128)(2,1)} %get-tuple-element.67), channel_id=1, source_target_pairs={{0,24},{4,28},{8,16},{12,20},{16,8},{20,12},{24,0},{28,4},{1,25},{... | collective-permute-start | bytes 786440 | tf_op jit(solution)/shard_map/ppermute | solution.py:49
  64.0 24.5 %collective-permute-start.13 = (bf16[8,128,128]{2,1,0:T(8,128)(2,1)}, bf16[8,128,128]{2,1,0:T(8,128)(2,1)}, u32[]{:S(2)}, u32[]{:S(2)}) collective-permute-start(bf16[8,128,128]{2,1,0:T(8,128)(2,1)} %get-tuple-element.68), channel_id=1, source_target_pairs={{0,28},{4,24},{8,20},{12,16},{16,12},{20,8},{24,4},{28,0},{1,29},{... | collective-permute-start | bytes 786440 | tf_op jit(solution)/shard_map/ppermute | solution.py:49
  65.4 24.6 %collective-permute-start.7 = (bf16[8,128,128]{2,1,0:T(8,128)(2,1)}, bf16[8,128,128]{2,1,0:T(8,128)(2,1)}, u32[]{:S(2)}, u32[]{:S(2)}) collective-permute-start(bf16[8,128,128]{2,1,0:T(8,128)(2,1)} %get-tuple-element.62), channel_id=1, source_target_pairs={{0,4},{4,0},{8,12},{12,8},{16,20},{20,16},{24,28},{28,24},{1,5},{5... | collective-permute-start | bytes 786440 | tf_op jit(solution)/shard_map/ppermute | solution.py:49
  81.5 12.6 %collective-permute-start.8 = (bf16[8,128,128]{2,1,0:T(8,128)(2,1)}, bf16[8,128,128]{2,1,0:T(8,128)(2,1)S(1)}, u32[]{:S(2)}, u32[]{:S(2)}) collective-permute-start(bf16[8,128,128]{2,1,0:T(8,128)(2,1)} %copy-done.9), channel_id=1, source_target_pairs={{0,8},{4,12},{8,0},{12,4},{16,24},{20,28},{24,16},{28,20},{1,9},{5... | collective-permute-start | bytes 786440 | tf_op jit(solution)/shard_map/ppermute | solution.py:49
  87.9 13.5 %collective-permute-start.15 = (f32[4,128,128]{2,1,0:T(8,128)}, f32[4,128,128]{2,1,0:T(8,128)S(1)}, u32[]{:S(2)}, u32[]{:S(2)}) collective-permute-start(f32[4,128,128]{2,1,0:T(8,128)} %get-tuple-element.72), channel_id=1, source_target_pairs={{0,8},{4,12},{8,0},{12,4},{16,24},{20,28},{24,16},{28,20},{1,9},{5... | collective-permute-start | bytes 786440 | tf_op jit(solution)/shard_map/ppermute | solution.py:49
  88.5 12.9 %collective-permute-start.16 = (f32[4,128,128]{2,1,0:T(8,128)}, f32[4,128,128]{2,1,0:T(8,128)S(1)}, u32[]{:S(2)}, u32[]{:S(2)}) collective-permute-start(f32[4,128,128]{2,1,0:T(8,128)} %get-tuple-element.73), channel_id=1, source_target_pairs={{0,16},{4,20},{8,24},{12,28},{16,0},{20,4},{24,8},{28,12},{1,17},{... | collective-permute-start | bytes 786440 | tf_op jit(solution)/shard_map/ppermute | solution.py:49
  90.0 17.3 %collective-permute-start.17 = (f32[4,128,128]{2,1,0:T(8,128)}, f32[4,128,128]{2,1,0:T(8,128)S(1)}, u32[]{:S(2)}, u32[]{:S(2)}) collective-permute-start(f32[4,128,128]{2,1,0:T(8,128)} %get-tuple-element.74), channel_id=1, source_target_pairs={{0,24},{4,28},{8,16},{12,20},{16,8},{20,12},{24,0},{28,4},{1,25},{... | collective-permute-start | bytes 786440 | tf_op jit(solution)/shard_map/ppermute | solution.py:49
  148.1 9.2 %collective-permute-start.20 = (f32[4,128,128]{2,1,0:T(8,128)S(1)}, f32[4,128,128]{2,1,0:T(8,128)S(1)}, u32[]{:S(2)}, u32[]{:S(2)}) collective-permute-start(f32[4,128,128]{2,1,0:T(8,128)S(1)} %get-tuple-element.81), channel_id=1, source_target_pairs={{0,8},{4,12},{8,0},{12,4},{16,24},{20,28},{24,16},{28,20},{1,9},{5... | collective-permute-start | bytes 786440 | tf_op jit(solution)/shard_map/ppermute | solution.py:49
  149.7 13.7 %collective-permute-start.21 = (f32[4,128,128]{2,1,0:T(8,128)S(1)}, f32[4,128,128]{2,1,0:T(8,128)S(1)}, u32[]{:S(2)}, u32[]{:S(2)}) collective-permute-start(f32[4,128,128]{2,1,0:T(8,128)S(1)} %get-tuple-element.82), channel_id=1, source_target_pairs={{0,16},{4,20},{8,24},{12,28},{16,0},{20,4},{24,8},{28,12},{1,17},{... | collective-permute-start | bytes 786440 | tf_op jit(solution)/shard_map/ppermute | solution.py:49
  151.2 12.2 %collective-permute-start.22 = (f32[4,128,128]{2,1,0:T(8,128)S(1)}, f32[4,128,128]{2,1,0:T(8,128)S(1)}, u32[]{:S(2)}, u32[]{:S(2)}) collective-permute-start(f32[4,128,128]{2,1,0:T(8,128)S(1)} %get-tuple-element.83), channel_id=1, source_target_pairs={{0,24},{4,28},{8,16},{12,20},{16,8},{20,12},{24,0},{28,4},{1,25},{... | collective-permute-start | bytes 786440 | tf_op jit(solution)/shard_map/ppermute | solution.py:49
  152.4 12.5 %collective-permute-start.18 = (f32[4,4,128,128]{3,2,1,0:T(8,128)}, f32[4,4,128,128]{3,2,1,0:T(8,128)S(1)}, u32[]{:S(2)}, u32[]{:S(2)}) collective-permute-start(f32[4,4,128,128]{3,2,1,0:T(8,128)} %get-tuple-element.77), channel_id=1, source_target_pairs={{0,4},{4,0},{8,12},{12,8},{16,20},{20,16},{24,28},{28,24},{1,5},{5... | collective-permute-start | bytes 3145736 | tf_op jit(solution)/shard_map/ppermute | solution.py:49
  164.8 57.8 %all-gather.16.cloned.1.call-start = ((), (), s32[]{:S(2)}) async-start(), calls=%async_computation.2 | async-start | bytes 1310720 | tf_op jit(solution)/shard_map/all_gather | solution.py:652
  165.0 20.1 %collective-permute-start.30 = (f32[4,128,128]{2,1,0:T(8,128)S(1)}, f32[4,128,128]{2,1,0:T(8,128)S(1)}, u32[]{:S(2)}, u32[]{:S(2)}) collective-permute-start(f32[4,128,128]{2,1,0:T(8,128)S(1)} %get-tuple-element.91), channel_id=1, source_target_pairs={{0,8},{4,12},{8,0},{12,4},{16,24},{20,28},{24,16},{28,20},{1,9},{5... | collective-permute-start | bytes 786440 | tf_op jit(solution)/shard_map/ppermute | solution.py:49
  166.3 18.8 %collective-permute-start.31 = (f32[4,128,128]{2,1,0:T(8,128)S(1)}, f32[4,128,128]{2,1,0:T(8,128)S(1)}, u32[]{:S(2)}, u32[]{:S(2)}) collective-permute-start(f32[4,128,128]{2,1,0:T(8,128)S(1)} %get-tuple-element.92), channel_id=1, source_target_pairs={{0,16},{4,20},{8,24},{12,28},{16,0},{20,4},{24,8},{28,12},{1,17},{... | collective-permute-start | bytes 786440 | tf_op jit(solution)/shard_map/ppermute | solution.py:49
  167.1 18.0 %collective-permute-start.32 = (f32[4,128,128]{2,1,0:T(8,128)S(1)}, f32[4,128,128]{2,1,0:T(8,128)S(1)}, u32[]{:S(2)}, u32[]{:S(2)}) collective-permute-start(f32[4,128,128]{2,1,0:T(8,128)S(1)} %get-tuple-element.93), channel_id=1, source_target_pairs={{0,24},{4,28},{8,16},{12,20},{16,8},{20,12},{24,0},{28,4},{1,25},{... | collective-permute-start | bytes 786440 | tf_op jit(solution)/shard_map/ppermute | solution.py:49
  (39 other events, 309.0 us)
Sparse Core Ops, SparseCore 0:
  52.0 85.3 all-gather.11
  164.9 28.9 all-gather.13
  195.5 27.0 all-gather.15
